TPU v7x, 256 devices: a whole 4x4x8 slice. The times are simulated.
256 devices in a mesh: ctx: 64 (over z, x_hi, y), head: 4 (over x_lo, core).
Axes of the slice: x: 4 (x_hi: 2, x_lo: 2; x = x_hi * 2 + x_lo), y: 4, z: 8, core: 2. Of those that a mesh axis runs over, the one named last changes fastest.
Arguments:
- query: bfloat16 [32768, 4096], P(('ctx', 'head')), may hold values from -16 to 16
- key: bfloat16 [32768, 4096], P(('ctx', 'head')), may hold values from -4.5 to 4.5
- value: bfloat16 [32768, 4096], P(('ctx', 'head')), may hold values from -12 to 12
- out_grad: bfloat16 [32768, 4096], P(('ctx', 'head')), may hold values from -6 to 6
- offsets: int32 [2, 32], P(None, 'head'), may hold values from 0 to 63, as said below
Outputs:
- attended: bfloat16 [32768, 4096], P(('ctx', 'head'))
- query_grad: bfloat16 [32768, 4096], P(('ctx', 'head'))
- key_grad: bfloat16 [32768, 4096], P(('ctx', 'head'))
- value_grad: bfloat16 [32768, 4096], P(('ctx', 'head'))
Inputs may be any that keep to these rules, and one draw needn't show every extreme that they name: `offsets`: row 0 holds values 0 to 15 with 15 among them; row 1 holds values 0 to 63 with 63 among them.
All inputs are finite; a program needn't handle non-finite values.
Results may differ from a plain program's by a relative error of at most 0.04.
Values may be sent and summed in bfloat16 or wider, within the bound.
No kernel may reach another device: no remote copies, remote signals or barrier semaphores. Data moves between devices by JAX's collectives and lax.ppermute only.
A program may use at most 128 MiB of HBM per device.

v0:
```python
import jax
import jax.numpy as jnp
from jax import lax
from jax.sharding import PartitionSpec as P

MIDDLE_DILATION = 16
UPPER_DILATION = 64


def partner(block, axis, bit):
    count = lax.axis_size(axis)
    route = []
    for low in range(count):
        high = low | 1 << bit
        if high != low and high < count:
            route += [(low, high), (high, low)]
    return lax.ppermute(block, axis, route)


def head_mask(dilation_rate, start_offset, ndim):
    heads = start_offset.shape[0]
    mask = lax.broadcasted_iota(jnp.int32, (dilation_rate, heads), 0) == start_offset[None, :]
    return mask.reshape((1, dilation_rate, heads) + (1,) * (ndim - 2))


def selector(values, dilation_rate, start_offset):
    if dilation_rate == 1:
        return values
    shaped = values.reshape((values.shape[0] // dilation_rate, dilation_rate) + values.shape[1:])
    mask = head_mask(dilation_rate, start_offset, values.ndim)
    return jnp.sum(jnp.where(mask, shaped, jnp.zeros((), values.dtype)), axis=1)


def spread_factor(rows, dilation_rate, start_offset):
    if dilation_rate == 1:
        return rows
    mask = head_mask(dilation_rate, start_offset, rows.ndim)
    full = jnp.where(mask, rows[:, None], jnp.zeros((), rows.dtype))
    return full.reshape((rows.shape[0] * dilation_rate,) + rows.shape[1:])


def merge_top(current, rows, dilation_rate, start_offset):
    shaped = current.reshape((current.shape[0] // dilation_rate, dilation_rate) + current.shape[1:])
    mask = head_mask(dilation_rate, start_offset, current.ndim)
    shaped = jnp.where(mask, jnp.maximum(shaped, rows[:, None]), shaped)
    return shaped.reshape(current.shape)


def doubled(piece, bits, trade, place_index):
    for bit in range(bits):
        other = trade(piece, bit)
        upper = place_index // (1 << bit) % 2 == 1
        piece = jnp.where(
            upper, jnp.concatenate([other, piece], 1), jnp.concatenate([piece, other], 1)
        )
    return piece


def halved(total, bits, trade, place_index):
    for bit in reversed(range(bits)):
        half = total.shape[0] // 2
        lower, higher = (total[:half], total[half:])
        upper = place_index // (1 << bit) % 2 == 1
        keep = jnp.where(upper, higher, lower)
        sent = jnp.where(upper, lower, higher)
        total = keep + trade(sent, bit)
    return total


def local(query, key, value, out_grad, offsets):
    heads_dev = offsets.shape[1]
    query, key, value, out_grad = (
        lax.all_to_all(query, "head", split_axis=1, concat_axis=0, tiled=True),
        lax.all_to_all(key, "head", split_axis=1, concat_axis=0, tiled=True),
        lax.all_to_all(value, "head", split_axis=1, concat_axis=0, tiled=True),
        lax.all_to_all(out_grad, "head", split_axis=1, concat_axis=0, tiled=True),
    )
    tok = query.shape[0]
    head_dim = query.shape[1] // heads_dev
    softmax_scale = head_dim ** (-0.5)
    query_full = query.reshape(tok, heads_dev, head_dim)
    key_full = key.reshape(tok, heads_dev, head_dim)
    value_full = value.reshape(tok, heads_dev, head_dim)
    gradient_full = out_grad.reshape(tok, heads_dev, head_dim)
    ctx_count = lax.axis_size("ctx")
    place_index = lax.axis_index("ctx")
    mid_bits = (ctx_count // 4).bit_length() - 1
    middle_offset = offsets[0]
    upper_offset = offsets[1]
    middle_query = selector(query_full, MIDDLE_DILATION, middle_offset)
    middle_gradient = selector(gradient_full, MIDDLE_DILATION, middle_offset)
    middle_owned_rows = jnp.stack(
        [
            selector(key_full, MIDDLE_DILATION, middle_offset),
            selector(value_full, MIDDLE_DILATION, middle_offset),
        ]
    )
    middle_key_rows = doubled(
        middle_owned_rows, mid_bits, lambda piece, bit: partner(piece, "ctx", bit), place_index
    )
    upper_query = selector(query_full, UPPER_DILATION, upper_offset)
    upper_gradient = selector(gradient_full, UPPER_DILATION, upper_offset)
    upper_owned_rows = jnp.stack(
        [
            selector(key_full, UPPER_DILATION, upper_offset),
            selector(value_full, UPPER_DILATION, upper_offset),
        ]
    )
    upper_key_rows = lax.all_gather(upper_owned_rows, "ctx", axis=1, tiled=True)
    levels = [
        (query_full, gradient_full, key_full, value_full, 1, middle_offset),
        (
            middle_query,
            middle_gradient,
            middle_key_rows[0],
            middle_key_rows[1],
            MIDDLE_DILATION,
            middle_offset,
        ),
        (
            upper_query,
            upper_gradient,
            upper_key_rows[0],
            upper_key_rows[1],
            UPPER_DILATION,
            upper_offset,
        ),
    ]
    scores = [
        jnp.einsum("qhd,khd->hqk", lq, lk, preferred_element_type=jnp.float32) * softmax_scale
        for lq, lg, lk, lv, dilation_rate, off in levels
    ]
    top_stat = scores[0].max(-1).T
    for index in (1, 2):
        dilation_rate, off = (levels[index][4], levels[index][5])
        top_stat = merge_top(top_stat, scores[index].max(-1).T, dilation_rate, off)
    total = jnp.zeros((tok, heads_dev), jnp.float32)
    numer = jnp.zeros((tok, heads_dev, head_dim), jnp.float32)
    for index in range(3):
        lq, lg, lk, lv, dilation_rate, off = levels[index]
        shift = selector(top_stat, dilation_rate, off)
        level_weight = jnp.exp(scores[index] - shift.T[:, :, None])
        total = total + spread_factor(level_weight.sum(-1).T, dilation_rate, off)
        part = jnp.einsum(
            "hqk,khd->qhd",
            level_weight.astype(jnp.bfloat16),
            lv,
            preferred_element_type=jnp.float32,
        )
        numer = numer + spread_factor(part, dilation_rate, off)
    attended = (numer / total[:, :, None]).astype(jnp.bfloat16)
    lse = top_stat + jnp.log(total)
    delta = jnp.sum(gradient_full.astype(jnp.float32) * attended.astype(jnp.float32), -1)
    query_grad = jnp.zeros((tok, heads_dev, head_dim), jnp.float32)
    grads_back = []
    for index in range(3):
        lq, lg, lk, lv, dilation_rate, off = levels[index]
        lse_rows = selector(lse, dilation_rate, off)
        delta_rows = selector(delta, dilation_rate, off)
        probability = jnp.exp(scores[index] - lse_rows.T[:, :, None])
        probability_gradient = jnp.einsum(
            "qhd,khd->hqk", lg, lv, preferred_element_type=jnp.float32
        )
        score_gradient = (probability * (probability_gradient - delta_rows.T[:, :, None])).astype(
            jnp.bfloat16
        )
        prob_b = probability.astype(jnp.bfloat16)
        query_grad = query_grad + spread_factor(
            softmax_scale
            * jnp.einsum("hqk,khd->qhd", score_gradient, lk, preferred_element_type=jnp.float32),
            dilation_rate,
            off,
        )
        grads_back.append((score_gradient, prob_b, lse_rows, delta_rows))
    dscore0, prob0, lse0, delta0 = grads_back[0]
    key_grad = softmax_scale * jnp.einsum(
        "hqk,qhd->khd", dscore0, query_full, preferred_element_type=jnp.float32
    )
    value_grad = jnp.einsum(
        "hqk,qhd->khd", prob0, gradient_full, preferred_element_type=jnp.float32
    )
    dscore1, prob1, lse1, delta1 = grads_back[1]
    mid_term = jnp.stack(
        [
            softmax_scale
            * jnp.einsum("hqk,qhd->khd", dscore1, middle_query, preferred_element_type=jnp.float32),
            jnp.einsum("hqk,qhd->khd", prob1, middle_gradient, preferred_element_type=jnp.float32),
        ],
        1,
    )
    middle_local_part = halved(
        mid_term,
        mid_bits,
        lambda piece, bit: partner(piece.astype(jnp.bfloat16), "ctx", bit).astype(piece.dtype),
        place_index,
    )
    dscore2, prob2, lse2, delta2 = grads_back[2]
    upper_local_part = lax.psum_scatter(
        jnp.stack(
            [
                softmax_scale
                * jnp.einsum(
                    "hqk,qhd->khd", dscore2, upper_query, preferred_element_type=jnp.float32
                ),
                jnp.einsum(
                    "hqk,qhd->khd", prob2, upper_gradient, preferred_element_type=jnp.float32
                ),
            ],
            1,
        ),
        "ctx",
        scatter_dimension=0,
        tiled=True,
    )
    key_grad = (
        key_grad
        + spread_factor(middle_local_part[:, 0], MIDDLE_DILATION, middle_offset)
        + spread_factor(upper_local_part[:, 0], UPPER_DILATION, upper_offset)
    )
    value_grad = (
        value_grad
        + spread_factor(middle_local_part[:, 1], MIDDLE_DILATION, middle_offset)
        + spread_factor(upper_local_part[:, 1], UPPER_DILATION, upper_offset)
    )
    flat = heads_dev * head_dim
    outputs = (
        attended.reshape(tok, flat),
        query_grad.astype(jnp.bfloat16).reshape(tok, flat),
        key_grad.astype(jnp.bfloat16).reshape(tok, flat),
        value_grad.astype(jnp.bfloat16).reshape(tok, flat),
    )
    attended_out, query_out, key_out, value_out = (
        lax.all_to_all(outputs[0], "head", split_axis=0, concat_axis=1, tiled=True),
        lax.all_to_all(outputs[1], "head", split_axis=0, concat_axis=1, tiled=True),
        lax.all_to_all(outputs[2], "head", split_axis=0, concat_axis=1, tiled=True),
        lax.all_to_all(outputs[3], "head", split_axis=0, concat_axis=1, tiled=True),
    )
    return (attended_out, query_out, key_out, value_out)


def solution(mesh):
    in_specs = (
        P(("ctx", "head"), None),
        P(("ctx", "head"), None),
        P(("ctx", "head"), None),
        P(("ctx", "head"), None),
        P(None, "head"),
    )
    out_specs = (
        P(("ctx", "head"), None),
        P(("ctx", "head"), None),
        P(("ctx", "head"), None),
        P(("ctx", "head"), None),
    )
    return jax.shard_map(local, mesh=mesh, in_specs=in_specs, out_specs=out_specs, check_vma=False)
```

profile of v0, /device:TPU:1, one launch (start us, length us, event | category | flops | bytes accessed | tf_op | source)
XLA Modules:
  0.0 666.1 jit_solution(5002200563853450316)
XLA Ops:
  9.5 6.7 %all-to-all-start.4 = ((bf16[128,4,1024]{2,0,1:T(8,128)(2,1)}), bf16[128,4,1024]{2,0,1:T(8,128)(2,1)S(1)}, u32[]{:S(2)}, u32[]{:S(2)}) async-start(bf16[128,4,1024]{2,0,1:T(8,128)(2,1)} %bitcast.258), calls=%async_computation.4 | async-start | bytes 2097152 | tf_op jit(solution)/shard_map/all_to_all | solution.py:76
  17.3 12.5 %all-to-all-done.4 = bf16[128,4,1024]{2,0,1:T(8,128)(2,1)S(1)} async-done(((bf16[128,4,1024]{2,0,1:T(8,128)(2,1)}), bf16[128,4,1024]{2,0,1:T(8,128)(2,1)S(1)}, u32[]{:S(2)}, u32[]{:S(2)}) %all-to-all-start.4) | async-done | bytes 1048608 | tf_op jit(solution)/shard_map/all_to_all | solution.py:76
  29.9 4.4 all-to-all-start.1
  35.3 12.5 %all-to-all-done.1 = bf16[128,4,1024]{2,0,1:T(8,128)(2,1)S(1)} async-done(((bf16[128,4,1024]{2,0,1:T(8,128)(2,1)}), bf16[128,4,1024]{2,0,1:T(8,128)(2,1)S(1)}, u32[]{:S(2)}, u32[]{:S(2)}) %all-to-all-start.1) | async-done | bytes 1048608 | tf_op jit(solution)/shard_map/all_to_all | solution.py:74
  47.8 4.4 all-to-all-start.2
  54.5 11.3 %all-to-all-done.2 = bf16[128,4,1024]{2,0,1:T(8,128)(2,1)S(1)} async-done(((bf16[128,4,1024]{2,0,1:T(8,128)(2,1)}), bf16[128,4,1024]{2,0,1:T(8,128)(2,1)S(1)}, u32[]{:S(2)}, u32[]{:S(2)}) %all-to-all-start.2) | async-done | bytes 1048608 | tf_op jit(solution)/shard_map/all_to_all | solution.py:75
  65.8 5.1 all-to-all-start
  73.7 10.9 %all-to-all-done = bf16[128,4,1024]{2,0,1:T(8,128)(2,1)} async-done(((bf16[128,4,1024]{2,0,1:T(8,128)(2,1)}), bf16[128,4,1024]{2,0,1:T(8,128)(2,1)}, u32[]{:S(2)}, u32[]{:S(2)}) %all-to-all-start) | async-done | bytes 1048608 | tf_op jit(solution)/shard_map/all_to_all | solution.py:73
  89.5 3.3 fusion.32
  93.5 3.7 collective-permute-done
  99.6 6.5 collective-permute-done.1
  109.1 11.5 %collective-permute-done.2 = bf16[2,128,8,128]{3,1,2,0:T(8,128)(2,1)} collective-permute-done((bf16[2,128,8,128]{3,1,2,0:T(8,128)(2,1)}, bf16[2,128,8,128]{3,1,2,0:T(8,128)(2,1)}, u32[]{:S(2)}, u32[]{:S(2)}) %collective-permute-start.2) | collective-permute-done | bytes 524320 | tf_op jit(solution)/shard_map/ppermute | solution.py:17
  128.1 4.5 multiply_reduce_fusion
  134.1 13.8 %collective-permute-done.3 = bf16[2,256,8,128]{3,1,2,0:T(8,128)(2,1)} collective-permute-done((bf16[2,256,8,128]{3,1,2,0:T(8,128)(2,1)}, bf16[2,256,8,128]{3,1,2,0:T(8,128)(2,1)}, u32[]{:S(2)}, u32[]{:S(2)}) %collective-permute-start.3) | collective-permute-done | bytes 1048608 | tf_op jit(solution)/shard_map/ppermute | solution.py:17
  152.8 46.3 %all-gather.2.cloned.1.call-done = bf16[2,512,8,128]{3,1,2,0:T(8,128)(2,1)} async-done(((bf16[2,8,8,128]{3,1,2,0:T(8,128)(2,1)}), bf16[2,512,8,128]{3,1,2,0:T(8,128)(2,1)}) %all-gather.2.cloned.1.call-update) | async-done | bytes 2097168 | tf_op jit(solution)/shard_map/all_gather | solution.py:109
  214.3 4.8 fusion
  219.2 8.3 %multiply_reduce_fusion.1 = (f32[512,8]{0,1:T(8,128)S(1)}, bf16[512,8,128]{0,2,1:T(8,128)(2,1)}) fusion(bf16[512,8,128]{0,2,1:T(8,128)(2,1)} %copy.249, f32[512,8]{0,1:T(8,128)S(1)} %get-tuple-element.31, f32[512,8,128]{0,2,1:T(8,128)} %copy.210, pred[512,8]{0,1:T(8,128)(4,1)S(1)} %broadcast_in_dim.279, f32[512,8,128]{0,2,1:T(8,128)} %copy.206, ...), kind=kOutput, calls=%fused_computation.36 | convolution fusion | flops 548401152 | bytes 15785984 | tf_op jit(solution)/shard_map/hqk,khd->qhd/dot_general | solution.py:144
  232.7 5.5 copy.235
  245.5 9.0 %all-to-all-start.3 = ((bf16[4,128,1024]{1,2,0:T(8,128)(2,1)}), bf16[4,128,1024]{1,2,0:T(8,128)(2,1)}, u32[]{:S(2)}, u32[]{:S(2)}) async-start(bf16[4,128,1024]{1,2,0:T(8,128)(2,1)} %copy.211), calls=%async_computation.3 | async-start | bytes 2097152 | tf_op jit(solution)/shard_map/all_to_all | solution.py:233
  254.6 11.4 %collective-permute-done.4 = bf16[256,2,8,128]{0,3,2,1:T(8,128)(2,1)} collective-permute-done((bf16[256,2,8,128]{0,3,2,1:T(8,128)(2,1)}, bf16[256,2,8,128]{0,3,2,1:T(8,128)(2,1)}, u32[]{:S(2)}, u32[]{:S(2)}) %collective-permute-start.4) | collective-permute-done | bytes 1048608 | tf_op jit(solution)/shard_map/ppermute | solution.py:17
  266.0 3.0 convert_add_fusion
  270.3 6.1 multiply_convert_fusion
  276.3 3.7 collective-permute-done.5
  296.7 3.4 fusion.17
  316.2 12.4 %all-to-all-start.5 = ((bf16[4,128,1024]{1,2,0:T(8,128)(2,1)}), bf16[4,128,1024]{1,2,0:T(8,128)(2,1)S(1)}, u32[]{:S(2)}, u32[]{:S(2)}) async-start(bf16[4,128,1024]{1,2,0:T(8,128)(2,1)} %copy.226), calls=%async_computation.5 | async-start | bytes 2097152 | tf_op jit(solution)/shard_map/all_to_all | solution.py:234
  328.7 230.5 %reduce-scatter.2.cloned.1.call-done = f32[8,2,8,128]{3,2,1,0:T(8,128)} async-done(((f32[512,2,8,128]{3,2,1,0:T(8,128)}), f32[8,2,8,128]{3,2,1,0:T(8,128)}) %reduce-scatter.2.cloned.1.call-update) | async-done | bytes 65552 | tf_op jit(solution)/shard_map/reduce_scatter | solution.py:198
  564.4 5.1 fusion.15
  572.9 53.5 %all-to-all-start.6 = ((bf16[4,128,1024]{1,2,0:T(8,128)(2,1)}), bf16[4,128,1024]{1,2,0:T(8,128)(2,1)S(1)}, u32[]{:S(2)}, u32[]{:S(2)}) async-start(bf16[4,128,1024]{1,2,0:T(8,128)(2,1)} %copy.237), calls=%async_computation.7 | async-start | bytes 2097152 | tf_op jit(solution)/shard_map/all_to_all | solution.py:235
  626.4 7.6 %fusion.13 = bf16[512,8,128]{0,2,1:T(8,128)(2,1)} fusion(f32[512,8,128]{0,2,1:T(8,128)} %copy.242, f32[512,8,128]{0,2,1:T(8,128)} %copy.241, bf16[512,8,128]{0,2,1:T(8,128)(2,1)S(1)} %copy-done.8, f32[8,512,512]{1,2,0:T(8,128)} %get-tuple-element.39, f32[8,512]{1,0:T(8,128)S(1)} %bitcast.299, pred[512,8]{0,1:T(8,128)(4,1)S(1)} %copy-done.24, ...), kind=kOutput, calls=%fused_computation.21 | convolution fusion | flops 545783808 | bytes 14704640 | tf_op jit(solution)/shard_map/hqk,qhd->khd/dot_general | solution.py:179
  636.4 3.6 all-to-all-done.6
  640.0 4.4 all-to-all-start.7
  649.2 8.7 %all-to-all-done.7 = bf16[4,128,1024]{1,2,0:T(8,128)(2,1)S(1)} async-done(((bf16[4,128,1024]{1,2,0:T(8,128)(2,1)}), bf16[4,128,1024]{1,2,0:T(8,128)(2,1)S(1)}, u32[]{:S(2)}, u32[]{:S(2)}) %all-to-all-start.7) | async-done | bytes 1048608 | tf_op jit(solution)/shard_map/all_to_all | solution.py:236
  (195 shorter events, 113.0 us)
Async XLA Ops:
  7.2 9.1 %copy-start.14 = (bf16[128,4096]{1,0:T(8,128)(2,1)S(1)}, bf16[128,4096]{1,0:T(8,128)(2,1)}, u32[]{:S(2)}) copy-start(bf16[128,4096]{1,0:T(8,128)(2,1)} %param.6) | copy-start | bytes 3145732
  9.5 20.3 %all-to-all-start.4 = ((bf16[128,4,1024]{2,0,1:T(8,128)(2,1)}), bf16[128,4,1024]{2,0,1:T(8,128)(2,1)S(1)}, u32[]{:S(2)}, u32[]{:S(2)}) async-start(bf16[128,4,1024]{2,0,1:T(8,128)(2,1)} %bitcast.258), calls=%async_computation.4 | async-start | bytes 2097152 | tf_op jit(solution)/shard_map/all_to_all | solution.py:76
  17.3 16.9 %copy-start.15 = (bf16[128,4096]{1,0:T(8,128)(2,1)S(1)}, bf16[128,4096]{1,0:T(8,128)(2,1)}, u32[]{:S(2)}) copy-start(bf16[128,4096]{1,0:T(8,128)(2,1)} %param.7) | copy-start | bytes 3145732
  29.9 18.0 %all-to-all-start.1 = ((bf16[128,4,1024]{2,0,1:T(8,128)(2,1)}), bf16[128,4,1024]{2,0,1:T(8,128)(2,1)S(1)}, u32[]{:S(2)}, u32[]{:S(2)}) async-start(bf16[128,4,1024]{2,0,1:T(8,128)(2,1)} %bitcast.259), calls=%async_computation.1 | async-start | bytes 2097152 | tf_op jit(solution)/shard_map/all_to_all | solution.py:74
  47.8 18.0 %all-to-all-start.2 = ((bf16[128,4,1024]{2,0,1:T(8,128)(2,1)}), bf16[128,4,1024]{2,0,1:T(8,128)(2,1)S(1)}, u32[]{:S(2)}, u32[]{:S(2)}) async-start(bf16[128,4,1024]{2,0,1:T(8,128)(2,1)} %bitcast.293), calls=%async_computation.2 | async-start | bytes 2097152 | tf_op jit(solution)/shard_map/all_to_all | solution.py:75
  52.2 18.7 %copy-start.33 = (s32[2,8]{1,0:T(2,128)S(1)}, s32[2,8]{1,0:T(2,128)}, u32[]{:S(2)}) copy-start(s32[2,8]{1,0:T(2,128)} %param.9) | copy-start | bytes 196
  65.8 6.4 copy-start.10
  65.8 18.8 %all-to-all-start = ((bf16[128,4,1024]{2,0,1:T(8,128)(2,1)}), bf16[128,4,1024]{2,0,1:T(8,128)(2,1)}, u32[]{:S(2)}, u32[]{:S(2)}) async-start(bf16[128,4,1024]{2,0,1:T(8,128)(2,1)} %bitcast.291), calls=%async_computation | async-start | bytes 2097152 | tf_op jit(solution)/shard_map/all_to_all | solution.py:73
  70.9 128.3 %all-gather.2.cloned.1.call-start = ((), (), s32[]{:S(2)}) async-start(), calls=%async_computation.9 | async-start | bytes 2129920 | tf_op jit(solution)/shard_map/all_gather | solution.py:109
  70.9 15.2 %copy-start.27 = (pred[64,8]{1,0:T(8,128)(4,1)}, pred[64,8]{1,0:T(8,128)(4,1)S(1)}, u32[]{:S(2)}) copy-start(pred[64,8]{1,0:T(8,128)(4,1)S(1)} %iota_compare_fusion) | copy-start | bytes 1540
  88.8 110.4 %copy-start.18 = (bf16[8,8,128]{2,1,0:T(8,128)(2,1)}, bf16[8,8,128]{2,1,0:T(8,128)(2,1)S(1)}, u32[]{:S(2)}) copy-start(bf16[8,8,128]{2,1,0:T(8,128)(2,1)S(1)} %get-tuple-element.21) | copy-start | bytes 49156
  89.5 469.7 %reduce-scatter.2.cloned.1.call-start = ((), (), s32[]{:S(2)}) async-start(), calls=%async_computation.10 | async-start | bytes 4259840 | tf_op jit(solution)/shard_map/reduce_scatter | solution.py:198
  92.9 4.3 collective-permute-start
  98.4 7.7 %collective-permute-start.1 = (bf16[2,64,8,128]{3,1,2,0:T(8,128)(2,1)S(1)}, bf16[2,64,8,128]{3,1,2,0:T(8,128)(2,1)}, u32[]{:S(2)}, u32[]{:S(2)}) collective-permute-start(bf16[2,64,8,128]{3,1,2,0:T(8,128)(2,1)S(1)} %maximum_select_fusion.3), channel_id=1, source_target_pairs={{0,8},{8,0},{4,12},{12,4},{16,24},{24,16},{20,28},{28,20},{32,40},... | collective-permute-start | bytes 786440 | tf_op jit(solution)/shard_map/ppermute | solution.py:17
  108.0 12.5 %collective-permute-start.2 = (bf16[2,128,8,128]{3,1,2,0:T(8,128)(2,1)}, bf16[2,128,8,128]{3,1,2,0:T(8,128)(2,1)}, u32[]{:S(2)}, u32[]{:S(2)}) collective-permute-start(bf16[2,128,8,128]{3,1,2,0:T(8,128)(2,1)} %maximum_select_fusion.2), channel_id=1, source_target_pairs={{0,16},{16,0},{4,20},{20,4},{8,24},{24,8},{12,28},{28,12},{32,48},... | collective-permute-start | bytes 1572872 | tf_op jit(solution)/shard_map/ppermute | solution.py:17
  123.4 24.5 %collective-permute-start.3 = (bf16[2,256,8,128]{3,1,2,0:T(8,128)(2,1)}, bf16[2,256,8,128]{3,1,2,0:T(8,128)(2,1)}, u32[]{:S(2)}, u32[]{:S(2)}) collective-permute-start(bf16[2,256,8,128]{3,1,2,0:T(8,128)(2,1)} %maximum_select_fusion.1), channel_id=1, source_target_pairs={{0,32},{32,0},{4,36},{36,4},{8,40},{40,8},{12,44},{44,12},{16,48},... | collective-permute-start | bytes 3145736 | tf_op jit(solution)/shard_map/ppermute | solution.py:17
  125.0 94.2 %copy-start.23 = (pred[512,8]{0,1:T(8,128)(4,1)}, pred[512,8]{0,1:T(8,128)(4,1)S(1)}, u32[]{:S(2)}) copy-start(pred[512,8]{0,1:T(8,128)(4,1)S(1)} %broadcast_in_dim.279) | copy-start | bytes 12292
  125.6 93.6 %copy-start.25 = (pred[512,8]{0,1:T(8,128)(4,1)}, pred[512,8]{0,1:T(8,128)(4,1)S(1)}, u32[]{:S(2)}) copy-start(pred[512,8]{0,1:T(8,128)(4,1)S(1)} %broadcast_in_dim.281) | copy-start | bytes 12292
  150.8 50.2 %copy-start.30 = (pred[16,8]{0,1:T(8,128)(4,1)S(1)}, pred[16,8]{0,1:T(8,128)(4,1)}, u32[]{:S(2)}) copy-start(pred[16,8]{0,1:T(8,128)(4,1)} %copy-done.29) | copy-start | bytes 388
  219.2 8.4 %copy-start.32 = (pred[64,8]{0,1:T(8,128)(4,1)S(1)}, pred[64,8]{0,1:T(8,128)(4,1)}, u32[]{:S(2)}) copy-start(pred[64,8]{0,1:T(8,128)(4,1)} %copy-done.31) | copy-start | bytes 1540
  219.2 8.5 %copy-start.20 = (bf16[8,8,128]{2,1,0:T(8,128)(2,1)S(1)}, bf16[8,8,128]{2,1,0:T(8,128)(2,1)}, u32[]{:S(2)}) copy-start(bf16[8,8,128]{2,1,0:T(8,128)(2,1)} %get-tuple-element.18) | copy-start | bytes 49156
  227.5 10.8 %copy-start.21 = (f32[512,8]{0,1:T(8,128)}, f32[512,8]{0,1:T(8,128)S(1)}, u32[]{:S(2)}) copy-start(f32[512,8]{0,1:T(8,128)S(1)} %get-tuple-element.44) | copy-start | bytes 49156
  242.6 23.4 %collective-permute-start.4 = (bf16[256,2,8,128]{0,3,2,1:T(8,128)(2,1)}, bf16[256,2,8,128]{0,3,2,1:T(8,128)(2,1)}, u32[]{:S(2)}, u32[]{:S(2)}) collective-permute-start(bf16[256,2,8,128]{0,3,2,1:T(8,128)(2,1)} %select_convert_fusion), channel_id=1, source_target_pairs={{0,32},{32,0},{4,36},{36,4},{8,40},{40,8},{12,44},{44,12},{16,48},... | collective-permute-start | bytes 3145736 | tf_op jit(solution)/shard_map/ppermute | solution.py:17
  245.5 70.7 %all-to-all-start.3 = ((bf16[4,128,1024]{1,2,0:T(8,128)(2,1)}), bf16[4,128,1024]{1,2,0:T(8,128)(2,1)}, u32[]{:S(2)}, u32[]{:S(2)}) async-start(bf16[4,128,1024]{1,2,0:T(8,128)(2,1)} %copy.211), calls=%async_computation.3 | async-start | bytes 2097152 | tf_op jit(solution)/shard_map/all_to_all | solution.py:233
  254.6 14.7 %copy-start.22 = (f32[512,8]{0,1:T(8,128)S(1)}, f32[512,8]{0,1:T(8,128)}, u32[]{:S(2)}) copy-start(f32[512,8]{0,1:T(8,128)} %copy-done.21) | copy-start | bytes 49156
  269.1 10.9 %collective-permute-start.5 = (bf16[128,2,8,128]{0,3,2,1:T(8,128)(2,1)S(1)}, bf16[128,2,8,128]{0,3,2,1:T(8,128)(2,1)S(1)}, u32[]{:S(2)}, u32[]{:S(2)}) collective-permute-start(bf16[128,2,8,128]{0,3,2,1:T(8,128)(2,1)S(1)} %select_convert_fusion.3), channel_id=1, source_target_pairs={{0,16},{16,0},{4,20},{20,4},{8,24},{24,8},{12,28},{28,12},{32,48},... | collective-permute-start | bytes 1572872 | tf_op jit(solution)/shard_map/ppermute | solution.py:17
  281.2 10.9 %collective-permute-start.6 = (bf16[64,2,8,128]{0,3,2,1:T(8,128)(2,1)}, bf16[64,2,8,128]{0,3,2,1:T(8,128)(2,1)}, u32[]{:S(2)}, u32[]{:S(2)}) collective-permute-start(bf16[64,2,8,128]{0,3,2,1:T(8,128)(2,1)} %select_convert_fusion.2), channel_id=1, source_target_pairs={{0,8},{8,0},{4,12},{12,4},{16,24},{24,16},{20,28},{28,20},{32,40},... | collective-permute-start | bytes 786440 | tf_op jit(solution)/shard_map/ppermute | solution.py:17
  295.6 9.9 %collective-permute-start.7 = (bf16[32,2,8,128]{0,3,2,1:T(8,128)(2,1)}, bf16[32,2,8,128]{0,3,2,1:T(8,128)(2,1)}, u32[]{:S(2)}, u32[]{:S(2)}) collective-permute-start(bf16[32,2,8,128]{0,3,2,1:T(8,128)(2,1)} %select_convert_fusion.1), channel_id=1, source_target_pairs={{0,4},{4,0},{8,12},{12,8},{16,20},{20,16},{24,28},{28,24},{32,36},... | collective-permute-start | bytes 393224 | tf_op jit(solution)/shard_map/ppermute | solution.py:17
  316.2 256.6 %all-to-all-start.5 = ((bf16[4,128,1024]{1,2,0:T(8,128)(2,1)}), bf16[4,128,1024]{1,2,0:T(8,128)(2,1)S(1)}, u32[]{:S(2)}, u32[]{:S(2)}) async-start(bf16[4,128,1024]{1,2,0:T(8,128)(2,1)} %copy.226), calls=%async_computation.5 | async-start | bytes 2097152 | tf_op jit(solution)/shard_map/all_to_all | solution.py:234
  572.9 53.5 %copy-start.8 = (bf16[512,8,128]{0,2,1:T(8,128)(2,1)S(1)}, bf16[512,8,128]{0,2,1:T(8,128)(2,1)}, u32[]{:S(2)}) copy-start(bf16[512,8,128]{0,2,1:T(8,128)(2,1)} %copy.249) | copy-start | bytes 3145732
  572.9 67.1 %all-to-all-start.6 = ((bf16[4,128,1024]{1,2,0:T(8,128)(2,1)}), bf16[4,128,1024]{1,2,0:T(8,128)(2,1)S(1)}, u32[]{:S(2)}, u32[]{:S(2)}) async-start(bf16[4,128,1024]{1,2,0:T(8,128)(2,1)} %copy.237), calls=%async_computation.7 | async-start | bytes 2097152 | tf_op jit(solution)/shard_map/all_to_all | solution.py:235
  640.0 18.0 %all-to-all-start.7 = ((bf16[4,128,1024]{1,2,0:T(8,128)(2,1)}), bf16[4,128,1024]{1,2,0:T(8,128)(2,1)S(1)}, u32[]{:S(2)}, u32[]{:S(2)}) async-start(bf16[4,128,1024]{1,2,0:T(8,128)(2,1)} %copy.243), calls=%async_computation.8 | async-start | bytes 2097152 | tf_op jit(solution)/shard_map/all_to_all | solution.py:236
  (20 other events, 50.0 us)
Sparse Core Ops, SparseCore 0:
  89.6 109.5 all-gather.1
  238.3 320.8 reduce-scatter.1
where the time goes:
time: 668 us; the launch traced here: 666 us
  waiting for transfers between devices  389 us (58%)
  starting transfers between devices  104 us (16%)
  local copies, waits for them, and re-layouts  80.2 us (12%)
  matrix products  44.7 us (7%)
  other arithmetic  33.3 us (5%)
  between operations  14.7 us (2%)
    reduce_scatter x1, waiting for transfers between devices, local(): lax.psum_scatter(jnp.stack([softmax_scale * jnp.einsum('hqk,qhd->khd', ds...  231 us
    all_to_all x1, starting transfers between devices, local(): lax.all_to_all(outputs[2], 'head', split_axis=0, concat_axis=1, tiled=True)  53.5 us
    ppermute x8, waiting for transfers between devices, partner(): return lax.ppermute(block, axis, route)  52.6 us
    all_gather x1, waiting for transfers between devices, local(): upper_key_rows = lax.all_gather(upper_owned_rows, 'ctx', axis=1, tiled=True)  46.3 us
    broadcast_in_dim x24, local copies, waits for them, and re-layouts, spread_factor(): full = jnp.where(mask, rows[:, None], jnp.zeros((), rows.dtype))  34.5 us
    unnamed x76, local copies, waits for them, and re-layouts  16.7 us
  transfers between devices with their start and end apart: 18, of which 16 were waited for; matrix products, arithmetic and copies ran while one was open for 15% of the time, Pallas kernels for 0%

commit v1 on v0

v1 whole, which is shorter than its diff:
```python
import functools

import jax
import jax.numpy as jnp
from jax import lax
from jax.experimental import pallas as pl
from jax.experimental.pallas import tpu as pltpu
from jax.sharding import PartitionSpec as P

AXES = ("ctx", "head")
SCALE = 128.0 ** -0.5
F32 = jnp.float32
BF16 = jnp.bfloat16
VMEM_LIMIT = 48 * 1024 * 1024


def decode(i):
    return i // 64, i // 32 % 2, i // 16 % 2, i // 4 % 4, i // 2 % 2, i % 2


def encode(s, zl, xh, y, xl, c):
    return ((((s * 2 + zl) * 2 + xh) * 4 + y) * 2 + xl) * 2 + c


def route(move):
    return [(i, encode(*move(*decode(i)))) for i in range(256)]


def rel_route(r):
    return route(lambda s, zl, xh, y, xl, c: (s, zl, xh, y, xl ^ (r >> 1), c ^ (r & 1)))


ZL_ROUTE = route(lambda s, zl, xh, y, xl, c: (s, zl ^ 1, xh, y, xl, c))


def s_route(k):
    return route(lambda s, zl, xh, y, xl, c: ((s + k) % 4, zl, xh, y, xl, c))


def unit_groups():
    groups = {}
    for i in range(256):
        s, zl, xh, y, xl, c = decode(i)
        groups.setdefault((s, zl, xl ^ xh, c), []).append(i)
    return list(groups.values())


def send(value, where):
    return lax.ppermute(value, AXES, where)


def unit_exchange(value):
    return lax.all_to_all(value, AXES, 0, 0, tiled=True, axis_index_groups=unit_groups())


def dot_nt(a, b):
    return lax.dot_general(a, b, (((1,), (1,)), ((), ())), preferred_element_type=F32)


def dot_nn(a, b):
    return lax.dot_general(a, b, (((1,), (0,)), ((), ())), preferred_element_type=F32)


def dot_tn(a, b):
    return lax.dot_general(a, b, (((0,), (0,)), ((), ())), preferred_element_type=F32)


def params():
    return pltpu.CompilerParams(vmem_limit_bytes=VMEM_LIMIT)


def cost(flops, bytes_accessed, exps=0):
    return pl.CostEstimate(flops=flops, bytes_accessed=bytes_accessed, transcendentals=exps)


SMEM = pl.BlockSpec(memory_space=pltpu.SMEM)
VMEM = pl.BlockSpec(memory_space=pltpu.VMEM)
ANY = pl.BlockSpec(memory_space=pl.ANY)


def columns(group, index):
    return pl.ds(pl.multiple_of(group * 1024 + index * 128, 128), 128)


def pack_kernel(meta, first, second, *refs):
    outs, sem = refs[:-1], refs[-1]
    group = meta[64]
    parts = len(outs) // 4
    wide = 1024 // parts
    copies = []
    for part in range(parts):
        for r in range(4):
            at = pl.ds(pl.multiple_of((group ^ r) * 1024 + part * wide, 128), wide)
            out = outs[part * 4 + r]
            for half, source in enumerate((first, second)):
                copies.append(
                    pltpu.make_async_copy(
                        source.at[:, at],
                        out.at[pl.ds(half * 128, 128), :],
                        sem.at[len(copies)],
                    )
                )
    for copy in copies:
        copy.start()
    for copy in copies:
        copy.wait()


def pack(meta, first, second, parts):
    shape = jax.ShapeDtypeStruct((256, 1024 // parts), BF16)
    return pl.pallas_call(
        pack_kernel,
        out_shape=[shape] * (4 * parts),
        in_specs=[SMEM, ANY, ANY],
        out_specs=[ANY] * (4 * parts),
        scratch_shapes=[pltpu.SemaphoreType.DMA((8 * parts,))],
        compiler_params=params(),
        cost_estimate=cost(0, 4 << 20),
        name="pack",
    )(meta, first, second)


def select_kernel(meta, key, value, query, grad, *refs):
    outs, full, tops = refs[:4], refs[4], refs[5]
    group = meta[64]
    for r in range(4):
        for h in range(8):
            head = (group ^ r) * 8 + h
            at = columns(group ^ r, h)
            rows = []
            for a, ref in enumerate((key, value, query, grad)):
                full[a] = ref[:, at].astype(F32)
                rows.append(full[a, pl.ds(meta[head], 8, stride=16), :])
                tops[pl.ds(2 * a, 2), :] = full[a, pl.ds(meta[32 + head], 2, stride=64), :]
            rows.append(tops[...])
            outs[r][:, h * 128 : h * 128 + 128] = jnp.concatenate(rows, 0).astype(BF16)


def select(meta, key, value, query, grad):
    return pl.pallas_call(
        select_kernel,
        out_shape=[jax.ShapeDtypeStruct((40, 1024), BF16)] * 4,
        in_specs=[SMEM] + [VMEM] * 4,
        out_specs=[VMEM] * 4,
        scratch_shapes=[pltpu.VMEM((4, 128, 128), F32), pltpu.VMEM((8, 128), F32)],
        compiler_params=params(),
        cost_estimate=cost(0, 5 << 20),
        name="select",
    )(meta, key, value, query, grad)


def lane(shape):
    return lax.broadcasted_iota(jnp.int32, shape, 1)


def row(shape):
    return lax.broadcasted_iota(jnp.int32, shape, 0)


def softmax_stats(score, dprob):
    top = jnp.max(score, -1, keepdims=True)
    weight = jnp.exp(score - top)
    total = jnp.sum(weight, -1, keepdims=True)
    delta = jnp.sum(weight * dprob, -1, keepdims=True) / total
    return top + jnp.log(total), delta


def stats_kernel(act, kv0, kv1, kv2, kv3, out):
    kvs = (kv0, kv1, kv2, kv3)
    key = jnp.concatenate([kv[:128] for kv in kvs], 0)
    value = jnp.concatenate([kv[128:] for kv in kvs], 0)
    score = dot_nt(act[2], key) * SCALE
    lse, delta = softmax_stats(score, dot_nt(act[3], value))
    at = lane((40, 128))
    out[0] = jnp.where(at == 0, lse, jnp.where(at == 1, delta, 0.0))


def stats(act, kvs):
    return pl.pallas_call(
        stats_kernel,
        grid=(8,),
        out_shape=jax.ShapeDtypeStruct((8, 40, 128), F32),
        in_specs=[pl.BlockSpec((4, 40, 128), lambda h: (0, 0, h))]
        + [pl.BlockSpec((256, 128), lambda h: (0, h))] * 4,
        out_specs=pl.BlockSpec((1, 40, 128), lambda h: (h, 0, 0)),
        compiler_params=params(),
        cost_estimate=cost(8 * 40 * 512 * 512, 3 << 20, 8 * 40 * 512),
        name="stats",
    )(act, *kvs)


def split_three(x):
    high = x.astype(BF16)
    rest = x - high.astype(F32)
    middle = rest.astype(BF16)
    low = (rest - middle.astype(F32)).astype(BF16)
    return high.astype(F32), middle.astype(F32), low.astype(F32)


def encode_stats(lse, delta, rows):
    at = lane((rows, 128))
    out = jnp.zeros((rows, 128), F32)
    for index, part in enumerate(split_three(lse) + split_three(delta)):
        out = jnp.where(at == index, part, out)
    return out.astype(BF16)


def decode_stats(x):
    at = lane(x.shape)
    lse = jnp.sum(jnp.where(at < 3, x, 0.0), -1, keepdims=True)
    delta = jnp.sum(jnp.where((at >= 3) & (at < 6), x, 0.0), -1, keepdims=True)
    return lse, delta


def merge_stats(entries):
    top = functools.reduce(jnp.maximum, [lse for lse, _ in entries])
    weights = [jnp.exp(lse - top) for lse, _ in entries]
    total = sum(weights)
    delta = sum(w * d for w, (_, d) in zip(weights, entries)) / total
    return top + jnp.log(total), delta


NONE = -1e30


def unit_kernel(meta, mid, top, oth, t1, t2, t3, st_mid, st_top, out_mid, out_top, mid_oth, top_far):
    head = meta[65]
    o1, o2 = meta[head], meta[32 + head]
    lap = lax.rem(o2, 16) == o1
    shift = lax.div(o2, 16)
    far = (t1, t2, t3)

    def keys(a):
        low = jnp.concatenate([mid[a], oth[a, :256]], 0)
        high = jnp.concatenate([top[a], oth[a, 256:]] + [t[a] for t in far], 0)
        return low, high

    (k1, k2), (v1, v2) = keys(0), keys(1)
    q1, g1, q2, g2 = mid[2], mid[3], top[2], top[3]
    s1, s2 = dot_nt(q1, k1) * SCALE, dot_nt(q2, k2) * SCALE
    p1, p2 = dot_nt(g1, v1), dot_nt(g2, v2)
    lse1, d1 = softmax_stats(s1, p1)
    lse2, d2 = softmax_stats(s2, p2)
    up = (lane((64, 256)) == 4 * row((64, 256)) + shift) & lap
    down = (row((256, 64)) == 4 * lane((256, 64)) + shift) & lap
    one = jnp.ones((), F32)
    none = jnp.zeros((), F32)
    at_top = dot_nn(jnp.where(up, one, none).astype(BF16), encode_stats(lse1, d1, 256))
    at_mid = dot_nn(jnp.where(down, one, none).astype(BF16), encode_stats(lse2, d2, 64))
    lse1_top, d1_top = decode_stats(at_top)
    lse2_mid, d2_mid = decode_stats(at_mid)
    lse1_top = jnp.where(lap, lse1_top, NONE)
    has = (lax.rem(row((256, 1)), 4) == shift) & lap
    lse2_mid = jnp.where(has, lse2_mid, NONE)

    def pick(st):
        at = lane(st.shape)
        return (
            jnp.sum(jnp.where(at == 0, st, 0.0), -1, keepdims=True),
            jnp.sum(jnp.where(at == 1, st, 0.0), -1, keepdims=True),
        )

    lse_m, delta_m = merge_stats([pick(st_mid[...]), (lse1, d1), (lse2_mid, d2_mid)])
    lse_t, delta_t = merge_stats([pick(st_top[...]), (lse2, d2), (lse1_top, d1_top)])

    def back(score, dprob, lse, delta, q, k, v, g):
        prob = jnp.exp(score - lse)
        dscore = (prob * (dprob - delta)).astype(BF16)
        prob = prob.astype(BF16)
        return (
            dot_nn(prob, v).astype(BF16),
            (dot_nn(dscore, k) * SCALE).astype(BF16),
            dot_tn(dscore, q) * SCALE,
            dot_tn(prob, g),
        )

    oo, qq, kk, vv = back(s1, p1, lse_m, delta_m, q1, k1, v1, g1)
    out_mid[0] = oo
    out_mid[1] = qq
    out_mid[2] = kk[:256].astype(BF16)
    out_mid[3] = vv[:256].astype(BF16)
    out_mid[4] = encode_stats(lse_m, delta_m, 256)
    mid_oth[0] = kk[256:].astype(BF16)
    mid_oth[1] = vv[256:].astype(BF16)
    oo, qq, kk, vv = back(s2, p2, lse_t, delta_t, q2, k2, v2, g2)
    out_top[0] = oo
    out_top[1] = qq
    out_top[2] = encode_stats(lse_t, delta_t, 64)
    for k in range(4):
        top_far[k, 0] = kk[128 * k : 128 * k + 128].astype(BF16)
        top_far[k, 1] = vv[128 * k : 128 * k + 128].astype(BF16)


def unit(meta, *arrays):
    return pl.pallas_call(
        unit_kernel,
        out_shape=[
            jax.ShapeDtypeStruct((5, 256, 128), BF16),
            jax.ShapeDtypeStruct((3, 64, 128), BF16),
            jax.ShapeDtypeStruct((2, 256, 128), BF16),
            jax.ShapeDtypeStruct((4, 2, 128, 128), BF16),
        ],
        in_specs=[SMEM] + [VMEM] * 8,
        out_specs=[VMEM] * 4,
        compiler_params=params(),
        cost_estimate=cost(6 * 320 * 512 * 256, 2 << 20, 2 * 320 * 512),
        name="unit",
    )(meta, *arrays)


def main_kernel(first, meta, *refs):
    kvs, qgs, oqs = refs[:4], refs[4:8], refs[8:12]
    dk, dv = refs[12:14]
    ds_all, p_all = refs[14:]
    head = meta[64] * 8 + first + pl.program_id(0)
    o1, o2 = meta[head], meta[32 + head]
    key = jnp.concatenate([kv[:128] for kv in kvs], 0)
    value = jnp.concatenate([kv[128:] for kv in kvs], 0)
    for r in range(4):
        query, grad = qgs[r][:128], qgs[r][128:]
        score = dot_nt(query, key) * SCALE
        weight = jnp.exp(score - jnp.max(score, -1, keepdims=True))
        inverse = 1.0 / jnp.sum(weight, -1, keepdims=True)
        attended = (dot_nn(weight.astype(BF16), value) * inverse).astype(BF16)
        delta = jnp.sum(attended.astype(F32) * grad.astype(F32), -1, keepdims=True)
        prob = weight * inverse
        dscore = (prob * (dot_nt(grad, value) - delta)).astype(BF16)
        oqs[r][:128] = attended
        oqs[r][128:] = (dot_nn(dscore, key) * SCALE).astype(BF16)
        ds_all[128 * r : 128 * r + 128] = dscore
        p_all[128 * r : 128 * r + 128] = prob.astype(BF16)
    at = row((128, 128))
    active = (lax.rem(at, 16) == o1) | (lax.rem(at, 64) == o2)

    def rest(half):
        blocks = []
        for r in range(4):
            block = qgs[r][half * 128 : half * 128 + 128].astype(F32)
            blocks.append(jnp.where(active, 0.0, block).astype(BF16))
        return jnp.concatenate(blocks, 0)

    dk[0] = dot_tn(ds_all[...], rest(0)) * SCALE
    dv[0] = dot_tn(p_all[...], rest(1))


def main(meta, kvs, qgs, first, count):
    return pl.pallas_call(
        functools.partial(main_kernel, first),
        grid=(count,),
        out_shape=[jax.ShapeDtypeStruct((256, 128 * count), BF16)] * 4
        + [jax.ShapeDtypeStruct((count, 512, 128), F32)] * 2,
        in_specs=[SMEM]
        + [pl.BlockSpec((256, 128), lambda h: (0, first + h))] * 4
        + [pl.BlockSpec((256, 128), lambda h: (0, h))] * 4,
        out_specs=[pl.BlockSpec((256, 128), lambda h: (0, h))] * 4
        + [pl.BlockSpec((1, 512, 128), lambda h: (h, 0, 0))] * 2,
        scratch_shapes=[pltpu.VMEM((512, 512), BF16)] * 2,
        compiler_params=params(),
        cost_estimate=cost(count * 12 * 512 * 512 * 128 * 2, count << 20, count * 512 * 512),
        name="main",
    )(meta, *kvs, *qgs)


def late_kernel(first, meta, *refs):
    act, back, dk0, dv0 = refs[:4]
    kvs = refs[4:8]
    dkvs, oas = refs[8:12], refs[12:16]
    full = refs[16]
    head = meta[64] * 8 + first + pl.program_id(0)
    o1, o2 = meta[head], meta[32 + head]
    lap = lax.rem(o2, 16) == o1
    shift = lax.div(o2, 16)
    key = jnp.concatenate([kv[:128] for kv in kvs], 0)
    value = jnp.concatenate([kv[128:] for kv in kvs], 0)
    query, grad = act[2], act[3]
    ret = back[0].astype(F32)
    lse, delta = decode_stats(ret[160:200])
    prob = jnp.exp(dot_nt(query, key) * SCALE - lse)
    dscore = (prob * (dot_nt(grad, value) - delta)).astype(BF16)
    prob = prob.astype(BF16)
    o_act, q_act = dot_nn(prob, value), dot_nn(dscore, key) * SCALE
    up = (lane((8, 32)) == 4 * row((8, 32)) + shift) & lap
    up = jnp.where(up, 1.0, 0.0).astype(BF16)
    o_mid = o_act[:32] + ret[0:32]
    q_mid = q_act[:32] + ret[32:64]
    o_top = o_act[32:] + ret[128:136] + dot_nn(up, ret[0:32].astype(BF16))
    q_top = q_act[32:] + ret[136:144] + dot_nn(up, ret[32:64].astype(BF16))
    for r in range(4):
        oas[r][...] = jnp.concatenate(
            [o_mid[8 * r : 8 * r + 8], q_mid[8 * r : 8 * r + 8], o_top, q_top], 0
        ).astype(BF16)
    twice = (row((40, 128)) >= 32) & lap
    for half, (start, weights, rows, mid_at, top_at, scale) in enumerate(
        ((dk0, dscore, query, 64, 144, SCALE), (dv0, prob, grad, 96, 152, 1.0))
    ):
        rows = jnp.where(twice, 0.0, rows.astype(F32)).astype(BF16)
        full[...] = start[0] + dot_tn(weights, rows) * scale
        at_mid = pl.ds(o1, 32, stride=16)
        full[at_mid, :] = full[at_mid, :] + ret[mid_at : mid_at + 32]
        at_top = pl.ds(o2, 8, stride=64)
        full[at_top, :] = full[at_top, :] + ret[top_at : top_at + 8]
        for r in range(4):
            dkvs[r][half * 128 : half * 128 + 128] = full[128 * r : 128 * r + 128].astype(BF16)


def late(meta, act, back, dk0, dv0, kvs, first, count):
    return pl.pallas_call(
        functools.partial(late_kernel, first),
        grid=(count,),
        out_shape=[jax.ShapeDtypeStruct((256, 128 * count), BF16)] * 4
        + [jax.ShapeDtypeStruct((32, 128 * count), BF16)] * 4,
        in_specs=[
            SMEM,
            pl.BlockSpec((4, 40, 128), lambda h: (0, 0, first + h)),
            pl.BlockSpec((1, 200, 128), lambda h: (first + h, 0, 0)),
            pl.BlockSpec((1, 512, 128), lambda h: (h, 0, 0)),
            pl.BlockSpec((1, 512, 128), lambda h: (h, 0, 0)),
        ]
        + [pl.BlockSpec((256, 128), lambda h: (0, first + h))] * 4,
        out_specs=[pl.BlockSpec((256, 128), lambda h: (0, h))] * 4
        + [pl.BlockSpec((32, 128), lambda h: (0, h))] * 4,
        scratch_shapes=[pltpu.VMEM((512, 128), F32)],
        compiler_params=params(),
        cost_estimate=cost(count * 12 * 40 * 512 * 128, count << 20, count * 40 * 512),
        name="late",
    )(meta, act, back, dk0, dv0, *kvs)


def finish_oq_kernel(meta, *refs):
    oqs, oas = refs[:8], refs[8:16]
    attended, query_grad, full = refs[16:]
    group = meta[64]
    for r in range(4):
        for h in range(8):
            head = (group ^ r) * 8 + h
            at = columns(group ^ r, h)
            part, near = h // 4, h % 4 * 128
            rows = oas[part * 4 + r][:, near : near + 128].astype(F32)
            for half, out in enumerate((attended, query_grad)):
                block = oqs[part * 4 + r][half * 128 : half * 128 + 128, near : near + 128]
                full[half] = block.astype(F32)
                full[half, pl.ds(meta[head], 8, stride=16), :] = rows[8 * half : 8 * half + 8]
                from_row = 16 + 8 * half + 2 * r
                full[half, pl.ds(meta[32 + head], 2, stride=64), :] = rows[from_row : from_row + 2]
                out[:, at] = full[half].astype(BF16)


def finish_oq(meta, oqs, oas):
    return pl.pallas_call(
        finish_oq_kernel,
        out_shape=[jax.ShapeDtypeStruct((128, 4096), BF16)] * 2,
        in_specs=[SMEM] + [VMEM] * 16,
        out_specs=[VMEM] * 2,
        scratch_shapes=[pltpu.VMEM((2, 128, 128), F32)],
        compiler_params=params(),
        cost_estimate=cost(0, 5 << 20),
        name="finish_oq",
    )(meta, *oqs, *oas)


def finish_kv_kernel(meta, *refs):
    dkvs, key_grad, value_grad, sem = refs[:8], refs[8], refs[9], refs[10]
    group = meta[64]
    copies = []
    for part in range(2):
        for r in range(4):
            at = pl.ds(pl.multiple_of((group ^ r) * 1024 + part * 512, 128), 512)
            for half, out in enumerate((key_grad, value_grad)):
                copies.append(
                    pltpu.make_async_copy(
                        dkvs[part * 4 + r].at[pl.ds(half * 128, 128), :],
                        out.at[:, at],
                        sem.at[len(copies)],
                    )
                )
    for copy in copies:
        copy.start()
    for copy in copies:
        copy.wait()


def finish_kv(meta, dkvs):
    return pl.pallas_call(
        finish_kv_kernel,
        out_shape=[jax.ShapeDtypeStruct((128, 4096), BF16)] * 2,
        in_specs=[SMEM] + [ANY] * 8,
        out_specs=[ANY] * 2,
        scratch_shapes=[pltpu.SemaphoreType.DMA((16,))],
        compiler_params=params(),
        cost_estimate=cost(0, 4 << 20),
        name="finish_kv",
    )(meta, *dkvs)


def local(query, key, value, out_grad, offsets):
    place = lax.axis_index("ctx")
    slot = lax.axis_index("head")
    xh, y = place // 4 % 2, place % 4
    group = slot ^ (2 * xh)
    routes = [None] + [rel_route(r) for r in (1, 2, 3)]

    def spread(blocks):
        return [blocks[0]] + [send(blocks[r], routes[r]) for r in (1, 2, 3)]

    rel = jnp.stack(spread([offsets] * 4))
    rel = jnp.where(slot % 2 == 1, rel[jnp.array([1, 0, 3, 2])], rel)
    rel = jnp.where(slot // 2 == 1, rel[jnp.array([2, 3, 0, 1])], rel)
    table = rel.transpose(1, 0, 2).reshape(64)
    meta = jnp.concatenate([table, jnp.stack([group, group * 8 + xh * 4 + y])])
    place_meta = jnp.concatenate([jnp.zeros((64,), jnp.int32), jnp.stack([group, group])])

    kvs = pack(place_meta, key, value, 1)
    acts = spread(select(meta, key, value, query, out_grad))
    kvs = spread(kvs)
    qgs = pack(place_meta, query, out_grad, 2)
    qgs = [spread(qgs[:4]), spread(qgs[4:])]

    stack = jnp.stack(acts)
    act_mid = stack[:, :32].reshape(4, 4, 8, 1024).transpose(1, 0, 2, 3).reshape(4, 32, 1024)
    act_top = stack[:, 32:].reshape(4, 4, 2, 1024).transpose(1, 0, 2, 3).reshape(4, 8, 1024)
    act = jnp.concatenate([act_mid, act_top], 1)
    sent = act.reshape(160, 8, 128).transpose(1, 0, 2).reshape(8 * 160, 128)
    got = unit_exchange(sent).reshape(8, 4, 40, 128)
    mid = got[:, :, :32].transpose(1, 0, 2, 3).reshape(4, 256, 128)
    top = got[:, :, 32:].transpose(1, 0, 2, 3).reshape(4, 64, 128)
    oth = send(jnp.concatenate([mid[:2], top[:2]], 1), ZL_ROUTE)
    top_pair = jnp.concatenate([top[:2], oth[:, 256:]], 1)
    far = [send(top_pair, s_route(k)) for k in (1, 2, 3)]

    st = unit_exchange(stats(act, kvs).reshape(320, 128)).reshape(8, 40, 128)
    out_mid, out_top, mid_oth, top_far = unit(
        meta,
        mid,
        top,
        oth,
        *far,
        st[:, :32].reshape(256, 128),
        st[:, 32:].reshape(64, 128),
    )
    near = send(mid_oth, ZL_ROUTE)
    tops = [send(top_far[k], s_route(4 - k)) for k in (1, 2, 3)]
    total = sum(t.astype(F32) for t in tops) + top_far[0].astype(F32)
    total_near = send(total[:, 64:].astype(BF16), ZL_ROUTE)
    top_kv = (total[:, :64] + total_near.astype(F32)).astype(BF16)
    mid_kv = (out_mid[2:4].astype(F32) + near.astype(F32)).astype(BF16)

    def by_source(x):
        return x.reshape(x.shape[0], 8, -1, 128).transpose(1, 0, 2, 3).reshape(8, -1, 128)

    back = jnp.concatenate(
        [
            by_source(out_mid[:2]),
            by_source(mid_kv),
            by_source(out_top[:2]),
            by_source(top_kv),
            by_source(out_mid[4:]),
            by_source(out_top[2:]),
        ],
        1,
    )
    back = unit_exchange(back.reshape(1600, 128)).reshape(8, 200, 128)

    oqs, oas, dkvs = [], [], []
    for part in range(2):
        outs = main(meta, kvs, qgs[part], 4 * part, 4)
        oqs += spread(outs[:4])
        ends = late(meta, act, back, outs[4], outs[5], kvs, 4 * part, 4)
        oas += spread(ends[4:])
        dkvs += spread(ends[:4])
    attended, query_grad = finish_oq(meta, oqs, oas)
    key_grad, value_grad = finish_kv(place_meta, dkvs)
    return attended, query_grad, key_grad, value_grad


def solution(mesh):
    rows = P(AXES, None)
    return jax.shard_map(
        local,
        mesh=mesh,
        in_specs=(rows, rows, rows, rows, P(None, "head")),
        out_specs=(rows, rows, rows, rows),
        check_vma=False,
    )
```

time: 668 us -> 198 us (0.30)
  waiting for transfers between devices: 389 us -> 49 us
  local copies, waits for them, and re-layouts: 80.2 us -> 26 us
  Pallas kernels: 0 us -> 47.8 us
  matrix products: 44.7 us -> 0 us
  starting transfers between devices: 104 us -> 71.8 us
  other arithmetic: 33.3 us -> 1.64 us
  between operations: 14.7 us -> 1.22 us
    reduce_scatter x1 -> x0, waiting for transfers between devices: 231 us -> none  [local(): lax.psum_scatter(jnp.stack([softmax_scale * jnp.einsum('hqk,qhd->khd', ds...]
    all_to_all x8 -> x3, starting transfers between devices: 99.9 us -> 18.4 us  [unit_exchange(): lax.all_to_all(value, AXES, 0, 0, tiled=True, axis_index_groups=unit_grou...]
    all_to_all x8 -> x3, waiting for transfers between devices: 59.6 us -> 3.71 us  [unit_exchange(): lax.all_to_all(value, AXES, 0, 0, tiled=True, axis_index_groups=unit_grou...]
    ppermute x8 -> x42, starting transfers between devices: 4.15 us -> 53.3 us  [send(): return lax.ppermute(value, AXES, where)]
    pallas_call x0 -> x11, Pallas kernels: none -> 47.8 us  [the longest x2 24 us: main(): pl.pallas_call(functools.partial(main_kernel, first), grid=(count,), out_...]
    all_gather x1 -> x0, waiting for transfers between devices: 46.3 us -> none  [local(): upper_key_rows = lax.all_gather(upper_owned_rows, 'ctx', axis=1, tiled=True)]
    dot_general x18 -> x0, matrix products: 44.7 us -> none  [the longest x3 11.4 us: local(): jnp.einsum('hqk,khd->qhd', level_weight.astype(jnp.bfloat16), lv, preferr...]
    broadcast_in_dim x29 -> x1, local copies, waits for them, and re-layouts: 34.8 us -> 0.01 us  [local(): jnp.zeros((64,), jnp.int32)]
  transfers between devices with their start and end apart: 18 -> 45, of which waited for: 16 -> 16; matrix products, arithmetic and copies ran while one was open for 15% -> 5% of each run, Pallas kernels for 0% -> 22%
where the time goes in v1:
time: 198 us; the launch traced here: 197 us
  starting transfers between devices  71.8 us (36%)
  waiting for transfers between devices  49 us (25%)
  Pallas kernels  47.8 us (24%)
  local copies, waits for them, and re-layouts  26 us (13%)
    ppermute x42, starting transfers between devices, send(): return lax.ppermute(value, AXES, where)  53.3 us
    ppermute x42, waiting for transfers between devices, send(): return lax.ppermute(value, AXES, where)  45.3 us
    pallas_call x2, Pallas kernels, main(): pl.pallas_call(functools.partial(main_kernel, first), grid=(count,), out_...  24 us
    all_to_all x3, starting transfers between devices, unit_exchange(): lax.all_to_all(value, AXES, 0, 0, tiled=True, axis_index_groups=unit_grou...  18.4 us
    unnamed x63, local copies, waits for them, and re-layouts  18.1 us
    pallas_call x2, Pallas kernels, late(): pl.pallas_call(functools.partial(late_kernel, first), grid=(count,), out_...  6.88 us
  transfers between devices with their start and end apart: 45, of which 16 were waited for; matrix products, arithmetic and copies ran while one was open for 5% of the time, Pallas kernels for 22%

profile of v1, /device:TPU:1, one launch (start us, length us, event | category | flops | bytes accessed | tf_op | source)
XLA Modules:
  0.0 197.4 jit_solution(3409674093676535794)
XLA Ops:
  0.6 3.3 %collective-permute-start = (s32[2,8]{1,0:T(2,128)}, s32[2,8]{1,0:T(2,128)S(1)}, u32[]{:S(2)}, u32[]{:S(2)}) collective-permute-start(s32[2,8]{1,0:T(2,128)} %param.11), channel_id=1, source_target_pairs={{0,1},{1,0},{2,3},{3,2},{4,5},{5,4},{6,7},{7,6},{8,9},{9,8},{10,11... | collective-permute-start | bytes 200 | tf_op jit(solution)/shard_map/ppermute | solution.py:49
  14.1 2.1 %select.15 = (bf16[40,1024]{1,0:T(8,128)(2,1)S(1)}, bf16[40,1024]{1,0:T(8,128)(2,1)S(1)}, bf16[40,1024]{1,0:T(8,128)(2,1)S(1)}, bf16[40,1024]{1,0:T(8,128)(2,1)S(1)}) custom-call(s32[66]{0:T(128)S(1)} %pad_add_fusion.1.meta, bf16[128,4096]{1,0:T(8,128)(2,1)S(1)} %copy-done, bf16[128,4096]{1,0:T(8,128)(2,1)S(1)} %copy-done.2, ...), custom_call_target="tpu_custom_call" | custom-call | bytes 5242880 | tf_op jit(solution)/shard_map/select/pallas_call | solution.py:140
  18.8 2.7 %collective-permute-done.19 = bf16[40,1024]{1,0:T(8,128)(2,1)S(1)} collective-permute-done((bf16[40,1024]{1,0:T(8,128)(2,1)S(1)}, bf16[40,1024]{1,0:T(8,128)(2,1)S(1)}, u32[]{:S(2)}, u32[]{:S(2)}) %collective-permute-start.19) | collective-permute-done | bytes 81952 | tf_op jit(solution)/shard_map/ppermute | solution.py:49
  21.5 1.7 collective-permute-done.20
  24.3 5.2 %all-to-all-start = ((bf16[8,160,128]{2,1,0:T(8,128)(2,1)}), bf16[8,160,128]{2,1,0:T(8,128)(2,1)}, u32[]{:S(2)}, u32[]{:S(2)}) async-start(bf16[8,160,128]{2,1,0:T(8,128)(2,1)} %bitcast.76), calls=%async_computation | async-start | bytes 655360 | tf_op jit(solution)/shard_map/all_to_all | solution.py:53
  33.5 3.7 %all-to-all-done = bf16[8,160,128]{2,1,0:T(8,128)(2,1)} async-done(((bf16[8,160,128]{2,1,0:T(8,128)(2,1)}), bf16[8,160,128]{2,1,0:T(8,128)(2,1)}, u32[]{:S(2)}, u32[]{:S(2)}) %all-to-all-start) | async-done | bytes 327712 | tf_op jit(solution)/shard_map/all_to_all | solution.py:53
  37.2 1.7 copy_bitcast_fusion.5
  42.2 3.3 %collective-permute-done.4.refs_2_.kv2.refs_6_ = bf16[256,1024]{1,0:T(8,128)(2,1)S(1)} collective-permute-done((bf16[256,1024]{1,0:T(8,128)(2,1)}, bf16[256,1024]{1,0:T(8,128)(2,1)S(1)}, u32[]{:S(2)}, u32[]{:S(2)}) %collective-permute-start.4) | collective-permute-done | bytes 524320 | tf_op jit(solution)/shard_map/ppermute | solution.py:49
  45.5 11.4 %collective-permute-done.5.refs_3_.kv3.refs_7_ = bf16[256,1024]{1,0:T(8,128)(2,1)S(1)} collective-permute-done((bf16[256,1024]{1,0:T(8,128)(2,1)S(1)}, bf16[256,1024]{1,0:T(8,128)(2,1)S(1)}, u32[]{:S(2)}, u32[]{:S(2)}) %collective-permute-start.5) | collective-permute-done | bytes 524320 | tf_op jit(solution)/shard_map/ppermute | solution.py:49
  56.9 3.4 %stats.1 = f32[8,40,128]{2,1,0:T(8,128)S(1)} custom-call(bf16[4,40,1024]{2,1,0:T(8,128)(2,1)S(1)} %pad_maximum_fusion.1.act.refs_0_, bf16[256,1024]{1,0:T(8,128)(2,1)S(1)} %get-tuple-element.56.refs_0_.kv0.refs_4_, bf16[256,1024]{1,0:T(8,128)(2,1)S(1)} %collective-permute-done.3.refs_1_.kv1.refs_5_, ...), custom_call_target="tpu_custom_call" | custom-call | flops 83886080 | bytes 3145728 | tf_op jit(solution)/shard_map/stats/pallas_call | solution.py:179
  61.0 6.6 %all-to-all-start.1 = ((f32[8,40,128]{2,1,0:T(8,128)}), f32[8,40,128]{2,1,0:T(8,128)}, u32[]{:S(2)}, u32[]{:S(2)}) async-start(f32[8,40,128]{2,1,0:T(8,128)} %copy-done.14), calls=%async_computation.1 | async-start | bytes 327680 | tf_op jit(solution)/shard_map/all_to_all | solution.py:53
  68.9 1.8 pack.3
  74.1 6.1 %collective-permute-start.24 = (bf16[2,128,128]{2,1,0:T(8,128)(2,1)S(1)}, bf16[2,128,128]{2,1,0:T(8,128)(2,1)S(1)}, u32[]{:S(2)}, u32[]{:S(2)}) collective-permute-start(bf16[2,128,128]{2,1,0:T(8,128)(2,1)S(1)} %pad_maximum_fusion.4), channel_id=1, source_target_pairs={{0,192},{1,193},{2,194},{3,195},{4,196},{5,197},{6,198},{7,199},{8... | collective-permute-start | bytes 196616 | tf_op jit(solution)/shard_map/ppermute | solution.py:49
  81.2 2.3 %collective-permute-start.22 = (bf16[2,128,128]{2,1,0:T(8,128)(2,1)S(1)}, bf16[2,128,128]{2,1,0:T(8,128)(2,1)S(1)}, u32[]{:S(2)}, u32[]{:S(2)}) collective-permute-start(bf16[2,128,128]{2,1,0:T(8,128)(2,1)S(1)} %pad_maximum_fusion.4), channel_id=1, source_target_pairs={{0,64},{1,65},{2,66},{3,67},{4,68},{5,69},{6,70},{7,71},{8,72},{9,... | collective-permute-start | bytes 196616 | tf_op jit(solution)/shard_map/ppermute | solution.py:49
  85.2 2.3 %collective-permute-done.23.t2 = bf16[2,128,128]{2,1,0:T(8,128)(2,1)S(1)} collective-permute-done((bf16[2,128,128]{2,1,0:T(8,128)(2,1)S(1)}, bf16[2,128,128]{2,1,0:T(8,128)(2,1)S(1)}, u32[]{:S(2)}, u32[]{:S(2)}) %collective-permute-start.23) | collective-permute-done | bytes 65568 | tf_op jit(solution)/shard_map/ppermute | solution.py:49
  88.4 2.6 %unit.1 = (bf16[5,256,128]{2,1,0:T(8,128)(2,1)S(1)}, bf16[3,64,128]{2,1,0:T(8,128)(2,1)S(1)}, bf16[2,256,128]{2,1,0:T(8,128)(2,1)S(1)}, bf16[4,2,128,128]{3,2,1,0:T(8,128)(2,1)S(1)}) custom-call(s32[66]{0:T(128)S(1)} %pad_add_fusion.1.meta, bf16[4,256,128]{2,1,0:T(8,128)(2,1)S(1)} %bitcast.81, bf16[4,64,128]{2,1,0:T(8,128)(2,1)S(1)} %get-tuple-element.114.top, ...), custom_call_target="tpu_custom_call" | custom-call | flops 251658240 | bytes 2097152 | tf_op jit(solution)/shard_map/unit/pallas_call | solution.py:295
  91.0 2.2 %collective-permute-start.26 = (bf16[2,128,128]{2,1,0:T(8,128)(2,1)S(1)}, bf16[2,128,128]{2,1,0:T(8,128)(2,1)S(1)}, u32[]{:S(2)}, u32[]{:S(2)}) collective-permute-start(bf16[2,128,128]{2,1,0:T(8,128)(2,1)S(1)} %get-tuple-element.108), channel_id=1, source_target_pairs={{0,192},{1,193},{2,194},{3,195},{4,196},{5,197},{6,198},{7,199},{8... | collective-permute-start | bytes 196616 | tf_op jit(solution)/shard_map/ppermute | solution.py:49
  93.5 4.3 %collective-permute-start.27 = (bf16[2,128,128]{2,1,0:T(8,128)(2,1)S(1)}, bf16[2,128,128]{2,1,0:T(8,128)(2,1)S(1)}, u32[]{:S(2)}, u32[]{:S(2)}) collective-permute-start(bf16[2,128,128]{2,1,0:T(8,128)(2,1)S(1)} %get-tuple-element.110), channel_id=1, source_target_pairs={{0,128},{1,129},{2,130},{3,131},{4,132},{5,133},{6,134},{7,135},{8... | collective-permute-start | bytes 196616 | tf_op jit(solution)/shard_map/ppermute | solution.py:49
  98.5 2.2 %collective-permute-start.12 = (bf16[256,512]{1,0:T(8,128)(2,1)}, bf16[256,512]{1,0:T(8,128)(2,1)}, u32[]{:S(2)}, u32[]{:S(2)}) collective-permute-start(bf16[256,512]{1,0:T(8,128)(2,1)} %get-tuple-element.69), channel_id=1, source_target_pairs={{0,1},{1,0},{2,3},{3,2},{4,5},{5,4},{6,7},{7,6},{8,9},{9,8},{10,11... | collective-permute-start | bytes 786440 | tf_op jit(solution)/shard_map/ppermute | solution.py:49
  103.5 2.8 %collective-permute-done.25 = bf16[2,256,128]{2,1,0:T(8,128)(2,1)S(1)} collective-permute-done((bf16[2,256,128]{2,1,0:T(8,128)(2,1)S(1)}, bf16[2,256,128]{2,1,0:T(8,128)(2,1)S(1)}, u32[]{:S(2)}, u32[]{:S(2)}) %collective-permute-start.25) | collective-permute-done | bytes 131104 | tf_op jit(solution)/shard_map/ppermute | solution.py:49
  109.8 6.0 %collective-permute-start.14 = (bf16[256,512]{1,0:T(8,128)(2,1)S(1)}, bf16[256,512]{1,0:T(8,128)(2,1)}, u32[]{:S(2)}, u32[]{:S(2)}) collective-permute-start(bf16[256,512]{1,0:T(8,128)(2,1)S(1)} %copy-done.23), channel_id=1, source_target_pairs={{0,3},{1,2},{2,1},{3,0},{4,7},{5,6},{6,5},{7,4},{8,11},{9,10},{10,... | collective-permute-start | bytes 786440 | tf_op jit(solution)/shard_map/ppermute | solution.py:49
  117.7 6.6 %all-to-all-start.2 = ((bf16[8,200,128]{2,1,0:T(8,128)(2,1)}), bf16[8,200,128]{2,1,0:T(8,128)(2,1)S(1)}, u32[]{:S(2)}, u32[]{:S(2)}) async-start(bf16[8,200,128]{2,1,0:T(8,128)(2,1)} %bitcast_dynamic-update-slice_fusion.2), calls=%async_computation.2 | async-start | bytes 819200 | tf_op jit(solution)/shard_map/all_to_all | solution.py:53
  124.4 12.0 %main.3 = (bf16[256,512]{1,0:T(8,128)(2,1)S(1)}, bf16[256,512]{1,0:T(8,128)(2,1)S(1)}, bf16[256,512]{1,0:T(8,128)(2,1)}, bf16[256,512]{1,0:T(8,128)(2,1)}, f32[4...) custom-call(s32[66]{0:T(128)S(1)} %pad_add_fusion.1.meta, bf16[256,1024]{1,0:T(8,128)(2,1)S(1)} %get-tuple-element.56.refs_0_.kv0.refs_4_, ...), custom_call_target="tpu_custom_call" | custom-call | flops 3221225472 | bytes 4194304 | tf_op jit(solution)/shard_map/main/pallas_call | solution.py:347
  137.5 1.7 collective-permute-start.16
  139.5 12.0 %main.2 = (bf16[256,512]{1,0:T(8,128)(2,1)S(1)}, bf16[256,512]{1,0:T(8,128)(2,1)}, bf16[256,512]{1,0:T(8,128)(2,1)}, bf16[256,512]{1,0:T(8,128)(2,1)}, f32[4,512...) custom-call(s32[66]{0:T(128)S(1)} %pad_add_fusion.1.meta, bf16[256,1024]{1,0:T(8,128)(2,1)S(1)} %get-tuple-element.56.refs_0_.kv0.refs_4_, ...), custom_call_target="tpu_custom_call" | custom-call | flops 3221225472 | bytes 4194304 | tf_op jit(solution)/shard_map/main/pallas_call | solution.py:347
  157.8 3.4 %late.3 = (bf16[256,512]{1,0:T(8,128)(2,1)S(1)}, bf16[256,512]{1,0:T(8,128)(2,1)S(1)}, bf16[256,512]{1,0:T(8,128)(2,1)S(1)}, bf16[256,512]{1,0:T(8,128)(2,1)S(1)...) custom-call(s32[66]{0:T(128)S(1)} %pad_add_fusion.1.meta, ...), custom_call_target="tpu_custom_call" | custom-call | flops 125829120 | bytes 4194304 | tf_op jit(solution)/shard_map/late/pallas_call | solution.py:407
  163.2 3.4 %late.2 = (bf16[256,512]{1,0:T(8,128)(2,1)S(1)}, bf16[256,512]{1,0:T(8,128)(2,1)S(1)}, bf16[256,512]{1,0:T(8,128)(2,1)S(1)}, bf16[256,512]{1,0:T(8,128)(2,1)S(1)...) custom-call(s32[66]{0:T(128)S(1)} %pad_add_fusion.1.meta, ...), custom_call_target="tpu_custom_call" | custom-call | flops 125829120 | bytes 4194304 | tf_op jit(solution)/shard_map/late/pallas_call | solution.py:407
  175.1 3.5 %finish_oq.1 = (bf16[128,4096]{1,0:T(8,128)(2,1)}, bf16[128,4096]{1,0:T(8,128)(2,1)}) custom-call(s32[66]{0:T(128)S(1)} %pad_add_fusion.1.meta, bf16[256,512]{1,0:T(8,128)(2,1)S(1)} %copy-done.16, bf16[256,512]{1,0:T(8,128)(2,1)} %collective-permute-done.9.refs_1_, bf16[256,512]{1,0:T(8,128)(2,1)} %collective-permute-done.10.refs_2_, ...), custom_call_target="tpu_custom_call" | custom-call | bytes 5242880 | tf_op jit(solution)/shard_map/finish_oq/pallas_call | solution.py:449
  178.6 6.0 %collective-permute-done.41.refs_7_ = bf16[256,512]{1,0:T(8,128)(2,1)S(1)} collective-permute-done((bf16[256,512]{1,0:T(8,128)(2,1)S(1)}, bf16[256,512]{1,0:T(8,128)(2,1)S(1)}, u32[]{:S(2)}, u32[]{:S(2)}) %collective-permute-start.41) | collective-permute-done | bytes 262176 | tf_op jit(solution)/shard_map/ppermute | solution.py:49
  184.6 4.7 %collective-permute-done.37.refs_2_ = bf16[256,512]{1,0:T(8,128)(2,1)S(1)} collective-permute-done((bf16[256,512]{1,0:T(8,128)(2,1)S(1)}, bf16[256,512]{1,0:T(8,128)(2,1)S(1)}, u32[]{:S(2)}, u32[]{:S(2)}) %collective-permute-start.37) | collective-permute-done | bytes 262176 | tf_op jit(solution)/shard_map/ppermute | solution.py:49
  189.3 6.0 %collective-permute-done.38.refs_3_ = bf16[256,512]{1,0:T(8,128)(2,1)S(1)} collective-permute-done((bf16[256,512]{1,0:T(8,128)(2,1)S(1)}, bf16[256,512]{1,0:T(8,128)(2,1)S(1)}, u32[]{:S(2)}, u32[]{:S(2)}) %collective-permute-start.38) | collective-permute-done | bytes 262176 | tf_op jit(solution)/shard_map/ppermute | solution.py:49
  195.2 2.0 %finish_kv.1 = (bf16[128,4096]{1,0:T(8,128)(2,1)}, bf16[128,4096]{1,0:T(8,128)(2,1)}) custom-call(s32[66]{0:T(128)S(1)} %pad_add_fusion.2.meta, bf16[256,512]{1,0:T(8,128)(2,1)S(1)} %get-tuple-element.98.refs_0_, bf16[256,512]{1,0:T(8,128)(2,1)S(1)} %collective-permute-done.36.refs_1_, bf16[256,512]{1,0:T(8,128)(2,1)S(1)} %collective-permute-done.37.refs_2_, ...), custom_call_target="tpu_custom_call" | custom-call | bytes 4194304 | tf_op jit(solution)/shard_map/finish_kv/pallas_call | solution.py:483
  (170 shorter events, 57.2 us)
Async XLA Ops:
  24.3 12.9 %all-to-all-start = ((bf16[8,160,128]{2,1,0:T(8,128)(2,1)}), bf16[8,160,128]{2,1,0:T(8,128)(2,1)}, u32[]{:S(2)}, u32[]{:S(2)}) async-start(bf16[8,160,128]{2,1,0:T(8,128)(2,1)} %bitcast.76), calls=%async_computation | async-start | bytes 655360 | tf_op jit(solution)/shard_map/all_to_all | solution.py:53
  31.2 11.0 %collective-permute-start.3 = (bf16[256,1024]{1,0:T(8,128)(2,1)}, bf16[256,1024]{1,0:T(8,128)(2,1)S(1)}, u32[]{:S(2)}, u32[]{:S(2)}) collective-permute-start(bf16[256,1024]{1,0:T(8,128)(2,1)} %get-tuple-element.57), channel_id=1, source_target_pairs={{0,1},{1,0},{2,3},{3,2},{4,5},{5,4},{6,7},{7,6},{8,9},{9,8},{10,11... | collective-permute-start | bytes 1572872 | tf_op jit(solution)/shard_map/ppermute | solution.py:49
  31.8 13.7 %collective-permute-start.4 = (bf16[256,1024]{1,0:T(8,128)(2,1)}, bf16[256,1024]{1,0:T(8,128)(2,1)S(1)}, u32[]{:S(2)}, u32[]{:S(2)}) collective-permute-start(bf16[256,1024]{1,0:T(8,128)(2,1)} %get-tuple-element.58), channel_id=1, source_target_pairs={{0,2},{1,3},{2,0},{3,1},{4,6},{5,7},{6,4},{7,5},{8,10},{9,11},{10,... | collective-permute-start | bytes 1572872 | tf_op jit(solution)/shard_map/ppermute | solution.py:49
  32.1 24.8 %collective-permute-start.5 = (bf16[256,1024]{1,0:T(8,128)(2,1)S(1)}, bf16[256,1024]{1,0:T(8,128)(2,1)S(1)}, u32[]{:S(2)}, u32[]{:S(2)}) collective-permute-start(bf16[256,1024]{1,0:T(8,128)(2,1)S(1)} %get-tuple-element.59), channel_id=1, source_target_pairs={{0,3},{1,2},{2,1},{3,0},{4,7},{5,6},{6,5},{7,4},{8,11},{9,10},{10,... | collective-permute-start | bytes 1572872 | tf_op jit(solution)/shard_map/ppermute | solution.py:49
  40.5 32.7 %collective-permute-start.21 = (bf16[2,320,128]{2,1,0:T(8,128)(2,1)}, bf16[2,320,128]{2,1,0:T(8,128)(2,1)}, u32[]{:S(2)}, u32[]{:S(2)}) collective-permute-start(bf16[2,320,128]{2,1,0:T(8,128)(2,1)} %pad_maximum_fusion.2), channel_id=1, source_target_pairs={{0,32},{1,33},{2,34},{3,35},{4,36},{5,37},{6,38},{7,39},{8,40},{9,... | collective-permute-start | bytes 491528 | tf_op jit(solution)/shard_map/ppermute | solution.py:49
  61.0 22.5 %all-to-all-start.1 = ((f32[8,40,128]{2,1,0:T(8,128)}), f32[8,40,128]{2,1,0:T(8,128)}, u32[]{:S(2)}, u32[]{:S(2)}) async-start(f32[8,40,128]{2,1,0:T(8,128)} %copy-done.14), calls=%async_computation.1 | async-start | bytes 327680 | tf_op jit(solution)/shard_map/all_to_all | solution.py:53
  72.8 66.4 %collective-permute-start.6 = (bf16[256,512]{1,0:T(8,128)(2,1)}, bf16[256,512]{1,0:T(8,128)(2,1)}, u32[]{:S(2)}, u32[]{:S(2)}) collective-permute-start(bf16[256,512]{1,0:T(8,128)(2,1)} %get-tuple-element.61), channel_id=1, source_target_pairs={{0,1},{1,0},{2,3},{3,2},{4,5},{5,4},{6,7},{7,6},{8,9},{9,8},{10,11... | collective-permute-start | bytes 786440 | tf_op jit(solution)/shard_map/ppermute | solution.py:49
  73.3 66.2 %collective-permute-start.7 = (bf16[256,512]{1,0:T(8,128)(2,1)}, bf16[256,512]{1,0:T(8,128)(2,1)}, u32[]{:S(2)}, u32[]{:S(2)}) collective-permute-start(bf16[256,512]{1,0:T(8,128)(2,1)} %get-tuple-element.62), channel_id=1, source_target_pairs={{0,2},{1,3},{2,0},{3,1},{4,6},{5,7},{6,4},{7,5},{8,10},{9,11},{10,... | collective-permute-start | bytes 786440 | tf_op jit(solution)/shard_map/ppermute | solution.py:49
  74.1 11.0 %collective-permute-start.24 = (bf16[2,128,128]{2,1,0:T(8,128)(2,1)S(1)}, bf16[2,128,128]{2,1,0:T(8,128)(2,1)S(1)}, u32[]{:S(2)}, u32[]{:S(2)}) collective-permute-start(bf16[2,128,128]{2,1,0:T(8,128)(2,1)S(1)} %pad_maximum_fusion.4), channel_id=1, source_target_pairs={{0,192},{1,193},{2,194},{3,195},{4,196},{5,197},{6,198},{7,199},{8... | collective-permute-start | bytes 196616 | tf_op jit(solution)/shard_map/ppermute | solution.py:49
  80.2 7.2 %collective-permute-start.23 = (bf16[2,128,128]{2,1,0:T(8,128)(2,1)S(1)}, bf16[2,128,128]{2,1,0:T(8,128)(2,1)S(1)}, u32[]{:S(2)}, u32[]{:S(2)}) collective-permute-start(bf16[2,128,128]{2,1,0:T(8,128)(2,1)S(1)} %pad_maximum_fusion.4), channel_id=1, source_target_pairs={{0,128},{1,129},{2,130},{3,131},{4,132},{5,133},{6,134},{7,135},{8... | collective-permute-start | bytes 196616 | tf_op jit(solution)/shard_map/ppermute | solution.py:49
  81.2 7.2 %collective-permute-start.22 = (bf16[2,128,128]{2,1,0:T(8,128)(2,1)S(1)}, bf16[2,128,128]{2,1,0:T(8,128)(2,1)S(1)}, u32[]{:S(2)}, u32[]{:S(2)}) collective-permute-start(bf16[2,128,128]{2,1,0:T(8,128)(2,1)S(1)} %pad_maximum_fusion.4), channel_id=1, source_target_pairs={{0,64},{1,65},{2,66},{3,67},{4,68},{5,69},{6,70},{7,71},{8,72},{9,... | collective-permute-start | bytes 196616 | tf_op jit(solution)/shard_map/ppermute | solution.py:49
  91.0 7.4 %collective-permute-start.26 = (bf16[2,128,128]{2,1,0:T(8,128)(2,1)S(1)}, bf16[2,128,128]{2,1,0:T(8,128)(2,1)S(1)}, u32[]{:S(2)}, u32[]{:S(2)}) collective-permute-start(bf16[2,128,128]{2,1,0:T(8,128)(2,1)S(1)} %get-tuple-element.108), channel_id=1, source_target_pairs={{0,192},{1,193},{2,194},{3,195},{4,196},{5,197},{6,198},{7,199},{8... | collective-permute-start | bytes 196616 | tf_op jit(solution)/shard_map/ppermute | solution.py:49
  93.3 7.4 %collective-permute-start.28 = (bf16[2,128,128]{2,1,0:T(8,128)(2,1)S(1)}, bf16[2,128,128]{2,1,0:T(8,128)(2,1)S(1)}, u32[]{:S(2)}, u32[]{:S(2)}) collective-permute-start(bf16[2,128,128]{2,1,0:T(8,128)(2,1)S(1)} %get-tuple-element.109), channel_id=1, source_target_pairs={{0,64},{1,65},{2,66},{3,67},{4,68},{5,69},{6,70},{7,71},{8,72},{9,... | collective-permute-start | bytes 196616 | tf_op jit(solution)/shard_map/ppermute | solution.py:49
  93.5 8.8 %collective-permute-start.27 = (bf16[2,128,128]{2,1,0:T(8,128)(2,1)S(1)}, bf16[2,128,128]{2,1,0:T(8,128)(2,1)S(1)}, u32[]{:S(2)}, u32[]{:S(2)}) collective-permute-start(bf16[2,128,128]{2,1,0:T(8,128)(2,1)S(1)} %get-tuple-element.110), channel_id=1, source_target_pairs={{0,128},{1,129},{2,130},{3,131},{4,132},{5,133},{6,134},{7,135},{8... | collective-permute-start | bytes 196616 | tf_op jit(solution)/shard_map/ppermute | solution.py:49
  98.5 25.8 %collective-permute-start.12 = (bf16[256,512]{1,0:T(8,128)(2,1)}, bf16[256,512]{1,0:T(8,128)(2,1)}, u32[]{:S(2)}, u32[]{:S(2)}) collective-permute-start(bf16[256,512]{1,0:T(8,128)(2,1)} %get-tuple-element.69), channel_id=1, source_target_pairs={{0,1},{1,0},{2,3},{3,2},{4,5},{5,4},{6,7},{7,6},{8,9},{9,8},{10,11... | collective-permute-start | bytes 786440 | tf_op jit(solution)/shard_map/ppermute | solution.py:49
  100.6 23.8 %collective-permute-start.13 = (bf16[256,512]{1,0:T(8,128)(2,1)}, bf16[256,512]{1,0:T(8,128)(2,1)}, u32[]{:S(2)}, u32[]{:S(2)}) collective-permute-start(bf16[256,512]{1,0:T(8,128)(2,1)} %get-tuple-element.70), channel_id=1, source_target_pairs={{0,2},{1,3},{2,0},{3,1},{4,6},{5,7},{6,4},{7,5},{8,10},{9,11},{10,... | collective-permute-start | bytes 786440 | tf_op jit(solution)/shard_map/ppermute | solution.py:49
  109.8 14.6 %collective-permute-start.14 = (bf16[256,512]{1,0:T(8,128)(2,1)S(1)}, bf16[256,512]{1,0:T(8,128)(2,1)}, u32[]{:S(2)}, u32[]{:S(2)}) collective-permute-start(bf16[256,512]{1,0:T(8,128)(2,1)S(1)} %copy-done.23), channel_id=1, source_target_pairs={{0,3},{1,2},{2,1},{3,0},{4,7},{5,6},{6,5},{7,4},{8,11},{9,10},{10,... | collective-permute-start | bytes 786440 | tf_op jit(solution)/shard_map/ppermute | solution.py:49
  117.7 37.6 %all-to-all-start.2 = ((bf16[8,200,128]{2,1,0:T(8,128)(2,1)}), bf16[8,200,128]{2,1,0:T(8,128)(2,1)S(1)}, u32[]{:S(2)}, u32[]{:S(2)}) async-start(bf16[8,200,128]{2,1,0:T(8,128)(2,1)} %bitcast_dynamic-update-slice_fusion.2), calls=%async_computation.2 | async-start | bytes 819200 | tf_op jit(solution)/shard_map/all_to_all | solution.py:53
  124.3 15.3 %collective-permute-start.8 = (bf16[256,512]{1,0:T(8,128)(2,1)}, bf16[256,512]{1,0:T(8,128)(2,1)S(1)}, u32[]{:S(2)}, u32[]{:S(2)}) collective-permute-start(bf16[256,512]{1,0:T(8,128)(2,1)} %get-tuple-element.63), channel_id=1, source_target_pairs={{0,3},{1,2},{2,1},{3,0},{4,7},{5,6},{6,5},{7,4},{8,11},{9,10},{10,... | collective-permute-start | bytes 786440 | tf_op jit(solution)/shard_map/ppermute | solution.py:49
  137.4 17.3 %collective-permute-start.15 = (bf16[256,512]{1,0:T(8,128)(2,1)S(1)}, bf16[256,512]{1,0:T(8,128)(2,1)S(1)}, u32[]{:S(2)}, u32[]{:S(2)}) collective-permute-start(bf16[256,512]{1,0:T(8,128)(2,1)S(1)} %get-tuple-element.73), channel_id=1, source_target_pairs={{0,1},{1,0},{2,3},{3,2},{4,5},{5,4},{6,7},{7,6},{8,9},{9,8},{10,11... | collective-permute-start | bytes 786440 | tf_op jit(solution)/shard_map/ppermute | solution.py:49
  137.5 23.8 %collective-permute-start.16 = (bf16[256,512]{1,0:T(8,128)(2,1)}, bf16[256,512]{1,0:T(8,128)(2,1)}, u32[]{:S(2)}, u32[]{:S(2)}) collective-permute-start(bf16[256,512]{1,0:T(8,128)(2,1)} %get-tuple-element.74), channel_id=1, source_target_pairs={{0,2},{1,3},{2,0},{3,1},{4,6},{5,7},{6,4},{7,5},{8,10},{9,11},{10,... | collective-permute-start | bytes 786440 | tf_op jit(solution)/shard_map/ppermute | solution.py:49
  139.2 22.1 %collective-permute-start.17 = (bf16[256,512]{1,0:T(8,128)(2,1)}, bf16[256,512]{1,0:T(8,128)(2,1)}, u32[]{:S(2)}, u32[]{:S(2)}) collective-permute-start(bf16[256,512]{1,0:T(8,128)(2,1)} %get-tuple-element.75), channel_id=1, source_target_pairs={{0,3},{1,2},{2,1},{3,0},{4,7},{5,6},{6,5},{7,4},{8,11},{9,10},{10,... | collective-permute-start | bytes 786440 | tf_op jit(solution)/shard_map/ppermute | solution.py:49
  153.2 8.7 %collective-permute-start.9 = (bf16[256,512]{1,0:T(8,128)(2,1)}, bf16[256,512]{1,0:T(8,128)(2,1)}, u32[]{:S(2)}, u32[]{:S(2)}) collective-permute-start(bf16[256,512]{1,0:T(8,128)(2,1)} %get-tuple-element.65), channel_id=1, source_target_pairs={{0,1},{1,0},{2,3},{3,2},{4,5},{5,4},{6,7},{7,6},{8,9},{9,8},{10,11... | collective-permute-start | bytes 786440 | tf_op jit(solution)/shard_map/ppermute | solution.py:49
  153.3 13.4 %collective-permute-start.10 = (bf16[256,512]{1,0:T(8,128)(2,1)}, bf16[256,512]{1,0:T(8,128)(2,1)}, u32[]{:S(2)}, u32[]{:S(2)}) collective-permute-start(bf16[256,512]{1,0:T(8,128)(2,1)} %get-tuple-element.66), channel_id=1, source_target_pairs={{0,2},{1,3},{2,0},{3,1},{4,6},{5,7},{6,4},{7,5},{8,10},{9,11},{10,... | collective-permute-start | bytes 786440 | tf_op jit(solution)/shard_map/ppermute | solution.py:49
  154.7 12.9 %collective-permute-start.11 = (bf16[256,512]{1,0:T(8,128)(2,1)}, bf16[256,512]{1,0:T(8,128)(2,1)}, u32[]{:S(2)}, u32[]{:S(2)}) collective-permute-start(bf16[256,512]{1,0:T(8,128)(2,1)} %get-tuple-element.67), channel_id=1, source_target_pairs={{0,3},{1,2},{2,1},{3,0},{4,7},{5,6},{6,5},{7,4},{8,11},{9,10},{10,... | collective-permute-start | bytes 786440 | tf_op jit(solution)/shard_map/ppermute | solution.py:49
  161.3 12.4 %collective-permute-start.39 = (bf16[256,512]{1,0:T(8,128)(2,1)S(1)}, bf16[256,512]{1,0:T(8,128)(2,1)S(1)}, u32[]{:S(2)}, u32[]{:S(2)}) collective-permute-start(bf16[256,512]{1,0:T(8,128)(2,1)S(1)} %get-tuple-element.103), channel_id=1, source_target_pairs={{0,1},{1,0},{2,3},{3,2},{4,5},{5,4},{6,7},{7,6},{8,9},{9,8},{10,11... | collective-permute-start | bytes 786440 | tf_op jit(solution)/shard_map/ppermute | solution.py:49
  161.9 7.2 %collective-permute-start.34 = (bf16[32,512]{1,0:T(8,128)(2,1)S(1)}, bf16[32,512]{1,0:T(8,128)(2,1)S(1)}, u32[]{:S(2)}, u32[]{:S(2)}) collective-permute-start(bf16[32,512]{1,0:T(8,128)(2,1)S(1)} %get-tuple-element.94), channel_id=1, source_target_pairs={{0,2},{1,3},{2,0},{3,1},{4,6},{5,7},{6,4},{7,5},{8,10},{9,11},{10,... | collective-permute-start | bytes 98312 | tf_op jit(solution)/shard_map/ppermute | solution.py:49
  170.2 8.4 %collective-permute-start.40 = (bf16[256,512]{1,0:T(8,128)(2,1)S(1)}, bf16[256,512]{1,0:T(8,128)(2,1)S(1)}, u32[]{:S(2)}, u32[]{:S(2)}) collective-permute-start(bf16[256,512]{1,0:T(8,128)(2,1)S(1)} %get-tuple-element.104), channel_id=1, source_target_pairs={{0,2},{1,3},{2,0},{3,1},{4,6},{5,7},{6,4},{7,5},{8,10},{9,11},{10,... | collective-permute-start | bytes 786440 | tf_op jit(solution)/shard_map/ppermute | solution.py:49
  171.2 13.4 %collective-permute-start.41 = (bf16[256,512]{1,0:T(8,128)(2,1)S(1)}, bf16[256,512]{1,0:T(8,128)(2,1)S(1)}, u32[]{:S(2)}, u32[]{:S(2)}) collective-permute-start(bf16[256,512]{1,0:T(8,128)(2,1)S(1)} %get-tuple-element.105), channel_id=1, source_target_pairs={{0,3},{1,2},{2,1},{3,0},{4,7},{5,6},{6,5},{7,4},{8,11},{9,10},{10,... | collective-permute-start | bytes 786440 | tf_op jit(solution)/shard_map/ppermute | solution.py:49
  172.1 12.5 %collective-permute-start.36 = (bf16[256,512]{1,0:T(8,128)(2,1)S(1)}, bf16[256,512]{1,0:T(8,128)(2,1)S(1)}, u32[]{:S(2)}, u32[]{:S(2)}) collective-permute-start(bf16[256,512]{1,0:T(8,128)(2,1)S(1)} %get-tuple-element.99), channel_id=1, source_target_pairs={{0,1},{1,0},{2,3},{3,2},{4,5},{5,4},{6,7},{7,6},{8,9},{9,8},{10,11... | collective-permute-start | bytes 786440 | tf_op jit(solution)/shard_map/ppermute | solution.py:49
  172.9 16.3 %collective-permute-start.37 = (bf16[256,512]{1,0:T(8,128)(2,1)S(1)}, bf16[256,512]{1,0:T(8,128)(2,1)S(1)}, u32[]{:S(2)}, u32[]{:S(2)}) collective-permute-start(bf16[256,512]{1,0:T(8,128)(2,1)S(1)} %get-tuple-element.100), channel_id=1, source_target_pairs={{0,2},{1,3},{2,0},{3,1},{4,6},{5,7},{6,4},{7,5},{8,10},{9,11},{10,... | collective-permute-start | bytes 786440 | tf_op jit(solution)/shard_map/ppermute | solution.py:49
  173.7 21.5 %collective-permute-start.38 = (bf16[256,512]{1,0:T(8,128)(2,1)S(1)}, bf16[256,512]{1,0:T(8,128)(2,1)S(1)}, u32[]{:S(2)}, u32[]{:S(2)}) collective-permute-start(bf16[256,512]{1,0:T(8,128)(2,1)S(1)} %get-tuple-element.101), channel_id=1, source_target_pairs={{0,3},{1,2},{2,1},{3,0},{4,7},{5,6},{6,5},{7,4},{8,11},{9,10},{10,... | collective-permute-start | bytes 786440 | tf_op jit(solution)/shard_map/ppermute | solution.py:49
  (42 other events, 155.0 us)

commit v2 on v1

v2 whole, which is shorter than its diff:
```python
import functools

import jax
import jax.numpy as jnp
from jax import lax
from jax.experimental import pallas as pl
from jax.experimental.pallas import tpu as pltpu
from jax.sharding import PartitionSpec as P

AXES = ("ctx", "head")
SCALE = 128.0 ** -0.5
LOG2E = 1.4426950408889634
F32 = jnp.float32
BF16 = jnp.bfloat16
VMEM_LIMIT = 60 * 1024 * 1024


def decode(i):
    return i // 64, i // 32 % 2, i // 16 % 2, i // 4 % 4, i // 2 % 2, i % 2


def encode(s, zl, xh, y, xl, c):
    return ((((s * 2 + zl) * 2 + xh) * 4 + y) * 2 + xl) * 2 + c


def route(move):
    return [(i, encode(*move(*decode(i)))) for i in range(256)]


def rel_route(r):
    return route(lambda s, zl, xh, y, xl, c: (s, zl, xh, y, xl ^ (r >> 1), c ^ (r & 1)))


ZL_ROUTE = route(lambda s, zl, xh, y, xl, c: (s, zl ^ 1, xh, y, xl, c))


def unit_groups():
    groups = {}
    for i in range(256):
        s, zl, xh, y, xl, c = decode(i)
        groups.setdefault((s, zl, xl ^ xh, c), []).append(i)
    return list(groups.values())


def send(value, where):
    return lax.ppermute(value, AXES, where)


def z_groups():
    groups = {}
    for i in range(256):
        groups.setdefault(i % 32, []).append(i)
    return list(groups.values())


def unit_exchange(value, groups):
    flat = value.reshape(value.shape[0] * value.shape[1], 128)
    return lax.all_to_all(flat, AXES, 0, 0, tiled=True, axis_index_groups=groups).reshape(value.shape)


def dot_nt(a, b):
    return lax.dot_general(a, b, (((1,), (1,)), ((), ())), preferred_element_type=F32)


def dot_nn(a, b):
    return lax.dot_general(a, b, (((1,), (0,)), ((), ())), preferred_element_type=F32)


def dot_tn(a, b):
    return lax.dot_general(a, b, (((0,), (0,)), ((), ())), preferred_element_type=F32)


def params():
    return pltpu.CompilerParams(vmem_limit_bytes=VMEM_LIMIT)


COST = pl.CostEstimate(flops=0, bytes_accessed=1024, transcendentals=0)
SMEM = pl.BlockSpec(memory_space=pltpu.SMEM)
VMEM = pl.BlockSpec(memory_space=pltpu.VMEM)
ANY = pl.BlockSpec(memory_space=pl.ANY)


def columns(group, index):
    return pl.ds(pl.multiple_of(group * 1024 + index * 128, 128), 128)


def head_offsets(meta, r, h):
    at = (r ^ meta[65]) * 16 + h
    return meta[at], meta[at + 8]


def open_kernel(meta, key, value, query, grad, *refs):
    acts, blocks = refs[:4], refs[4:12]
    held, full, tops, sems, loads = refs[12:]
    group = meta[64]
    ready = []
    for a, ref in enumerate((key, value, query, grad)):
        ready.append(pltpu.make_async_copy(ref, held.at[a], loads.at[a]))
        ready[a].start()
    copies = []
    for a in range(4):
        ready[a].wait()
        for r in range(4):
            at = pl.ds(pl.multiple_of((group ^ r) * 1024, 128), 1024)
            to = blocks[a // 2 * 4 + r].at[pl.ds(a % 2 * 128, 128), :]
            copies.append(pltpu.make_async_copy(held.at[a, :, at], to, sems.at[4 * a + r]))
            copies[-1].start()
    for r in range(4):
        for h in range(8):
            o1, o2 = head_offsets(meta, r, h)
            at = columns(group ^ r, h)
            rows = []
            for a in range(4):
                full[a] = held[a, :, at].astype(F32)
                rows.append(full[a, pl.ds(o1, 8, stride=16), :])
                tops[pl.ds(2 * a, 2), :] = full[a, pl.ds(o2, 2, stride=64), :]
            rows.append(tops[...])
            acts[r][:, h * 128 : h * 128 + 128] = jnp.concatenate(rows, 0).astype(BF16)
    for copy in copies:
        copy.wait()


def open_blocks(meta, key, value, query, grad):
    outs = pl.pallas_call(
        open_kernel,
        out_shape=[jax.ShapeDtypeStruct((40, 1024), BF16)] * 4
        + [jax.ShapeDtypeStruct((256, 1024), BF16)] * 8,
        in_specs=[SMEM] + [ANY] * 4,
        out_specs=[VMEM] * 4 + [ANY] * 8,
        scratch_shapes=[
            pltpu.VMEM((4, 128, 4096), BF16),
            pltpu.VMEM((4, 128, 128), F32),
            pltpu.VMEM((8, 128), F32),
            pltpu.SemaphoreType.DMA((16,)),
            pltpu.SemaphoreType.DMA((4,)),
        ],
        compiler_params=params(),
        cost_estimate=COST,
        name="open",
    )(meta, key, value, query, grad)
    return outs[:4], outs[4:8], outs[8:]


def arrange_kernel(a0, a1, a2, a3, *refs):
    act, out = refs[3:5]
    mid = [[] for _ in range(4)]
    top = [[] for _ in range(4)]
    for ref in (a0, a1, a2, a3):
        x = ref[...].astype(F32)
        for a in range(4):
            mid[a].append(x[8 * a : 8 * a + 8])
            top[a].append(x[32 + 2 * a : 34 + 2 * a])
    rows = []
    for a in range(4):
        rows.append(jnp.concatenate(mid[a] + [jnp.concatenate(top[a], 0)], 0))
        act[a] = rows[a].astype(BF16)
    whole = jnp.concatenate(rows, 0).astype(BF16)
    for h in range(8):
        out[h] = whole[:, 128 * h : 128 * h + 128]


def arrange(acts, blocks):
    outs = pl.pallas_call(
        arrange_kernel,
        out_shape=[
            jax.ShapeDtypeStruct((4, 40, 1024), BF16),
            jax.ShapeDtypeStruct((8, 160, 128), BF16),
        ]
        + [jax.ShapeDtypeStruct((256, 1024), BF16)] * 3,
        in_specs=[VMEM] * 4 + [ANY] * 3,
        out_specs=[VMEM] * 2 + [ANY] * 3,
        input_output_aliases={4: 2, 5: 3, 6: 4},
        compiler_params=params(),
        cost_estimate=COST,
        name="arrange",
    )(*acts, *blocks)
    return outs[0], outs[1], outs[2:]


def fan_kernel(got, mid, top, far):
    blocks = [got[j].astype(F32) for j in range(8)]
    tops = []
    for a in range(4):
        at = 40 * a
        mid[a] = jnp.concatenate([x[at : at + 32] for x in blocks], 0).astype(BF16)
        tops.append(jnp.concatenate([x[at + 32 : at + 40] for x in blocks], 0))
        top[a] = tops[a].astype(BF16)
    both_rows = jnp.concatenate(tops[:2], 0).astype(BF16)
    for z in range(8):
        far[z] = both_rows


def fan(got):
    return pl.pallas_call(
        fan_kernel,
        out_shape=[
            jax.ShapeDtypeStruct((4, 256, 128), BF16),
            jax.ShapeDtypeStruct((4, 64, 128), BF16),
            jax.ShapeDtypeStruct((8, 128, 128), BF16),
        ],
        in_specs=[VMEM],
        out_specs=[VMEM] * 3,
        compiler_params=params(),
        cost_estimate=COST,
        name="fan",
    )(got)


def lane(shape):
    return lax.broadcasted_iota(jnp.int32, shape, 1)


def row(shape):
    return lax.broadcasted_iota(jnp.int32, shape, 0)


def softmax_stats(score, dprob):
    top = jnp.max(score, -1, keepdims=True)
    weight = jnp.exp(score - top)
    total = jnp.sum(weight, -1, keepdims=True)
    delta = jnp.sum(weight * dprob, -1, keepdims=True) / total
    return top + jnp.log(total), delta


def stats_kernel(act, *refs):
    kvs, out = refs[:4], refs[-1]
    for h in range(8):
        at = pl.ds(128 * h, 128)
        key = jnp.concatenate([kv[:128, at] for kv in kvs], 0)
        value = jnp.concatenate([kv[128:, at] for kv in kvs], 0)
        score = dot_nt(key, act[2, :, at]) * SCALE
        top = jnp.max(score, 0, keepdims=True)
        weight = jnp.exp(score - top)
        total = jnp.sum(weight, 0, keepdims=True)
        dprob = dot_nt(value, act[3, :, at])
        out[h, 0:1, 0:40] = top + jnp.log(total)
        out[h, 1:2, 0:40] = jnp.sum(weight * dprob, 0, keepdims=True) / total


def stats(act, kvs, last):
    return pl.pallas_call(
        stats_kernel,
        out_shape=jax.ShapeDtypeStruct((8, 8, 128), F32),
        in_specs=[VMEM] * 5 + [ANY] * len(last),
        out_specs=VMEM,
        compiler_params=params(),
        cost_estimate=COST,
        name="stats",
    )(act, *kvs, *last)


def split_three(x):
    high = x.astype(BF16)
    rest = x - high.astype(F32)
    middle = rest.astype(BF16)
    low = (rest - middle.astype(F32)).astype(BF16)
    return high.astype(F32), middle.astype(F32), low.astype(F32)


def encode_stats(lse, delta, rows):
    at = lane((rows, 128))
    out = jnp.zeros((rows, 128), F32)
    for index, part in enumerate(split_three(lse) + split_three(delta)):
        out = jnp.where(at == index, part, out)
    return out.astype(BF16)


def decode_stats(x):
    at = lane(x.shape)
    lse = jnp.sum(jnp.where(at < 3, x, 0.0), -1, keepdims=True)
    delta = jnp.sum(jnp.where((at >= 3) & (at < 6), x, 0.0), -1, keepdims=True)
    return lse, delta


def merge_stats(entries):
    top = functools.reduce(jnp.maximum, [lse for lse, _ in entries])
    weights = [jnp.exp(lse - top) for lse, _ in entries]
    total = sum(weights)
    delta = sum(w * d for w, (_, d) in zip(weights, entries)) / total
    return top + jnp.log(total), delta


NONE = -1e30


def unit_kernel(meta, mid, top, oth, topz, st, *refs):
    out_mid, out_top, mid_oth, top_far = refs[-4:]
    o1, o2 = head_offsets(meta, 0, meta[66])
    lap = lax.rem(o2, 16) == o1
    shift = lax.div(o2, 16)
    k1, v1 = (jnp.concatenate([mid[a], oth[a]], 0) for a in range(2))
    k2 = jnp.concatenate([topz[z, :64] for z in range(8)], 0)
    v2 = jnp.concatenate([topz[z, 64:] for z in range(8)], 0)
    q1, g1, q2, g2 = mid[2], mid[3], top[2], top[3]
    level0 = []
    for index in range(2):
        rows = jnp.concatenate([st[j, index : index + 1, :] for j in range(8)], 0).T
        level0.append(
            (
                jnp.concatenate([rows[:32, j : j + 1] for j in range(8)], 0),
                jnp.concatenate([rows[32:40, j : j + 1] for j in range(8)], 0),
            )
        )
    s1, s2 = dot_nt(q1, k1) * SCALE, dot_nt(q2, k2) * SCALE
    p1, p2 = dot_nt(g1, v1), dot_nt(g2, v2)
    lse1, d1 = softmax_stats(s1, p1)
    lse2, d2 = softmax_stats(s2, p2)
    up = (lane((64, 256)) == 4 * row((64, 256)) + shift) & lap
    down = (row((256, 64)) == 4 * lane((256, 64)) + shift) & lap
    one = jnp.ones((), F32)
    none = jnp.zeros((), F32)
    at_top = dot_nn(jnp.where(up, one, none).astype(BF16), encode_stats(lse1, d1, 256))
    at_mid = dot_nn(jnp.where(down, one, none).astype(BF16), encode_stats(lse2, d2, 64))
    lse1_top, d1_top = decode_stats(at_top)
    lse2_mid, d2_mid = decode_stats(at_mid)
    lse1_top = jnp.where(lap, lse1_top, NONE)
    has = (lax.rem(row((256, 1)), 4) == shift) & lap
    lse2_mid = jnp.where(has, lse2_mid, NONE)

    lse_m, delta_m = merge_stats([(level0[0][0], level0[1][0]), (lse1, d1), (lse2_mid, d2_mid)])
    lse_t, delta_t = merge_stats([(level0[0][1], level0[1][1]), (lse2, d2), (lse1_top, d1_top)])

    def back(score, dprob, lse, delta, q, k, v, g):
        prob = jnp.exp(score - lse)
        dscore = (prob * (dprob - delta)).astype(BF16)
        prob = prob.astype(BF16)
        return (
            dot_nn(prob, v).astype(BF16),
            (dot_nn(dscore, k) * SCALE).astype(BF16),
            dot_tn(dscore, q) * SCALE,
            dot_tn(prob, g),
        )

    oo, qq, kk, vv = back(s1, p1, lse_m, delta_m, q1, k1, v1, g1)
    out_mid[0] = oo
    out_mid[1] = qq
    out_mid[2] = kk[:256].astype(BF16)
    out_mid[3] = vv[:256].astype(BF16)
    out_mid[4] = encode_stats(lse_m, delta_m, 256)
    mid_oth[0] = kk[256:].astype(BF16)
    mid_oth[1] = vv[256:].astype(BF16)
    oo, qq, kk, vv = back(s2, p2, lse_t, delta_t, q2, k2, v2, g2)
    out_top[0] = oo
    out_top[1] = qq
    out_top[2] = encode_stats(lse_t, delta_t, 64)
    for z in range(8):
        top_far[z, :64] = kk[64 * z : 64 * z + 64].astype(BF16)
        top_far[z, 64:] = vv[64 * z : 64 * z + 64].astype(BF16)


def unit(meta, arrays, last):
    return pl.pallas_call(
        unit_kernel,
        out_shape=[
            jax.ShapeDtypeStruct((5, 256, 128), BF16),
            jax.ShapeDtypeStruct((3, 64, 128), BF16),
            jax.ShapeDtypeStruct((2, 256, 128), BF16),
            jax.ShapeDtypeStruct((8, 128, 128), BF16),
        ],
        in_specs=[SMEM] + [VMEM] * 5 + [ANY] * len(last),
        out_specs=[VMEM] * 4,
        compiler_params=params(),
        cost_estimate=COST,
        name="unit",
    )(meta, *arrays, *last)


def combine_kernel(out_mid, out_top, near, tops, *refs):
    back = refs[-1]
    top_kv = sum(tops[z].astype(F32) for z in range(8))
    mids = [out_mid[a].astype(F32) for a in range(5)]
    mids[2] = mids[2] + near[0].astype(F32)
    mids[3] = mids[3] + near[1].astype(F32)
    outs = [out_top[a].astype(F32) for a in range(3)]
    highs = [outs[0], outs[1], top_kv[:64], top_kv[64:]]
    for j in range(8):
        rows = [x[32 * j : 32 * j + 32] for x in mids[:4]]
        rows += [x[8 * j : 8 * j + 8] for x in highs]
        rows += [mids[4][32 * j : 32 * j + 32], outs[2][8 * j : 8 * j + 8]]
        back[j] = jnp.concatenate(rows, 0).astype(BF16)


def combine(arrays, last):
    return pl.pallas_call(
        combine_kernel,
        out_shape=jax.ShapeDtypeStruct((8, 200, 128), BF16),
        in_specs=[VMEM] * 4 + [ANY] * len(last),
        out_specs=VMEM,
        compiler_params=params(),
        cost_estimate=COST,
        name="combine",
    )(*arrays, *last)


def main_kernel(first, meta, *refs):
    kvs, qgs = refs[:4], refs[4:8]
    oqs, dk, dv = refs[-6:-2], refs[-2], refs[-1]
    o1, o2 = head_offsets(meta, 0, first + pl.program_id(0))
    key = jnp.concatenate([kv[:128] for kv in kvs], 0)
    value = jnp.concatenate([kv[128:] for kv in kvs], 0)
    query = jnp.concatenate([qg[:128] for qg in qgs], 0)
    grad = jnp.concatenate([qg[128:] for qg in qgs], 0)
    score = dot_nt(key, query) * (SCALE * LOG2E)
    weight = jnp.exp2(score - jnp.max(score, 0, keepdims=True))
    inverse = 1.0 / jnp.sum(weight, 0, keepdims=True)
    attended = dot_nn(value.T, weight.astype(BF16)) * inverse
    delta = jnp.sum(attended * grad.astype(F32).T, 0, keepdims=True)
    prob = weight * inverse
    dscore = (prob * (dot_nt(value, grad) - delta)).astype(BF16)
    attended = attended.T.astype(BF16)
    query_grad = (dot_nn(key.T, dscore) * SCALE).T.astype(BF16)
    for r in range(4):
        oqs[r][:128] = attended[128 * r : 128 * r + 128]
        oqs[r][128:] = query_grad[128 * r : 128 * r + 128]
    at = row((512, 128))
    active = (lax.rem(at, 16) == o1) | (lax.rem(at, 64) == o2)
    zero = jnp.zeros((), BF16)
    dk[0] = dot_nn(dscore, jnp.where(active, zero, query)) * SCALE
    dv[0] = dot_nn(prob.astype(BF16), jnp.where(active, zero, grad))


def head_block(rows, first):
    return pl.BlockSpec((rows, 128), lambda h: (0, first + h))


def part_shapes(rows):
    return [jax.ShapeDtypeStruct((rows, 1024), BF16)] * 2 + [
        jax.ShapeDtypeStruct((rows, 512), BF16)
    ] * 2


def part_specs(rows, first):
    return [head_block(rows, first)] * 2 + [head_block(rows, 0)] * 2


def main(meta, kvs, qgs, first, held, last):
    before = [meta, *kvs, *qgs, *last]
    return pl.pallas_call(
        functools.partial(main_kernel, first),
        grid=(4,),
        out_shape=part_shapes(256) + [jax.ShapeDtypeStruct((4, 512, 128), F32)] * 2,
        in_specs=[SMEM]
        + [head_block(256, first)] * 8
        + [ANY] * (len(last) + len(held)),
        out_specs=part_specs(256, first)
        + [pl.BlockSpec((1, 512, 128), lambda h: (h, 0, 0))] * 2,
        input_output_aliases={len(before) + i: i for i in range(len(held))},
        compiler_params=params(),
        cost_estimate=COST,
        name="main",
    )(*before, *held)


def late_kernel(first, meta, *refs):
    act, back, dk0, dv0 = refs[:4]
    kvs = refs[4:8]
    dkvs, oas, full = refs[-9:-5], refs[-5:-1], refs[-1]
    o1, o2 = head_offsets(meta, 0, first + pl.program_id(0))
    lap = lax.rem(o2, 16) == o1
    shift = lax.div(o2, 16)
    key = jnp.concatenate([kv[:128] for kv in kvs], 0)
    value = jnp.concatenate([kv[128:] for kv in kvs], 0)
    query, grad = act[2], act[3]
    ret = back[0].astype(F32)
    lse, delta = decode_stats(ret[160:200])
    prob = jnp.exp(dot_nt(query, key) * SCALE - lse)
    dscore = (prob * (dot_nt(grad, value) - delta)).astype(BF16)
    prob = prob.astype(BF16)
    o_act, q_act = dot_nn(prob, value), dot_nn(dscore, key) * SCALE
    up = (lane((8, 32)) == 4 * row((8, 32)) + shift) & lap
    up = jnp.where(up, 1.0, 0.0).astype(BF16)
    o_mid = o_act[:32] + ret[0:32]
    q_mid = q_act[:32] + ret[32:64]
    o_top = o_act[32:] + ret[128:136] + dot_nn(up, ret[0:32].astype(BF16))
    q_top = q_act[32:] + ret[136:144] + dot_nn(up, ret[32:64].astype(BF16))
    for r in range(4):
        oas[r][...] = jnp.concatenate(
            [o_mid[8 * r : 8 * r + 8], q_mid[8 * r : 8 * r + 8], o_top, q_top], 0
        ).astype(BF16)
    twice = (row((40, 128)) >= 32) & lap
    for half, (start, weights, rows, mid_at, top_at, scale) in enumerate(
        ((dk0, dscore, query, 64, 144, SCALE), (dv0, prob, grad, 96, 152, 1.0))
    ):
        rows = jnp.where(twice, 0.0, rows.astype(F32)).astype(BF16)
        full[...] = start[0] + dot_tn(weights, rows) * scale
        at_mid = pl.ds(o1, 32, stride=16)
        full[at_mid, :] = full[at_mid, :] + ret[mid_at : mid_at + 32]
        at_top = pl.ds(o2, 8, stride=64)
        full[at_top, :] = full[at_top, :] + ret[top_at : top_at + 8]
        for r in range(4):
            dkvs[r][half * 128 : half * 128 + 128] = full[128 * r : 128 * r + 128].astype(BF16)


def late(meta, act, back, dk0, dv0, kvs, first, held, last):
    before = [meta, act, back, dk0, dv0, *kvs, *last]
    places = (0, 1, 4, 5, 6, 7)[: len(held)]
    return pl.pallas_call(
        functools.partial(late_kernel, first),
        grid=(4,),
        out_shape=part_shapes(256) + [jax.ShapeDtypeStruct((32, 1024), BF16)] * 4,
        in_specs=[
            SMEM,
            pl.BlockSpec((4, 40, 128), lambda h: (0, 0, first + h)),
            pl.BlockSpec((1, 200, 128), lambda h: (first + h, 0, 0)),
            pl.BlockSpec((1, 512, 128), lambda h: (h, 0, 0)),
            pl.BlockSpec((1, 512, 128), lambda h: (h, 0, 0)),
        ]
        + [head_block(256, first)] * 4
        + [ANY] * (len(last) + len(held)),
        out_specs=part_specs(256, first) + [head_block(32, first)] * 4,
        scratch_shapes=[pltpu.VMEM((512, 128), F32)],
        input_output_aliases={len(before) + i: at for i, at in enumerate(places)},
        compiler_params=params(),
        cost_estimate=COST,
        name="late",
    )(*before, *held)


def piece(blocks, r, h):
    if r < 2:
        return blocks[r], 128 * h
    return blocks[2 * (h // 4) + r], h % 4 * 128


def finish_oq_kernel(meta, *refs):
    oqs, oas = refs[:6], refs[6:10]
    attended, query_grad, full = refs[-3:]
    group = meta[64]
    for r in range(4):
        for h in range(8):
            o1, o2 = head_offsets(meta, r, h)
            at = columns(group ^ r, h)
            source, near = piece(oqs, r, h)
            rows = oas[r][:, 128 * h : 128 * h + 128].astype(F32)
            for half, out in enumerate((attended, query_grad)):
                block = source[half * 128 : half * 128 + 128, near : near + 128]
                full[half] = block.astype(F32)
                full[half, pl.ds(o1, 8, stride=16), :] = rows[8 * half : 8 * half + 8]
                from_row = 16 + 8 * half + 2 * r
                full[half, pl.ds(o2, 2, stride=64), :] = rows[from_row : from_row + 2]
                out[:, at] = full[half].astype(BF16)


def finish_oq(meta, oqs, oas, last):
    return pl.pallas_call(
        finish_oq_kernel,
        out_shape=[jax.ShapeDtypeStruct((128, 4096), BF16)] * 2,
        in_specs=[SMEM] + [VMEM] * 10 + [ANY] * len(last),
        out_specs=[VMEM] * 2,
        scratch_shapes=[pltpu.VMEM((2, 128, 128), F32)],
        compiler_params=params(),
        cost_estimate=COST,
        name="finish_oq",
    )(meta, *oqs, *oas, *last)


def finish_kv_kernel(meta, *refs):
    dkvs, outs, held, sems = refs[:6], refs[6:8], refs[8], refs[9]
    group = meta[64]
    copies = []
    for half in range(2):
        for index, block in enumerate(dkvs):
            r = index if index < 4 else index - 2
            wide = 1024 if r < 2 else 512
            start = (group ^ r) * 1024 + (512 if index >= 4 else 0)
            at = pl.ds(pl.multiple_of(start, 128), wide)
            from_rows = block.at[pl.ds(half * 128, 128), :]
            copies.append(
                pltpu.make_async_copy(from_rows, held.at[half, :, at], sems.at[len(copies)])
            )
            copies[-1].start()
    stores = []
    for half in range(2):
        for copy in copies[6 * half : 6 * half + 6]:
            copy.wait()
        stores.append(pltpu.make_async_copy(held.at[half], outs[half], sems.at[12 + half]))
        stores[half].start()
    for copy in stores:
        copy.wait()


def finish_kv(meta, dkvs):
    return pl.pallas_call(
        finish_kv_kernel,
        out_shape=[jax.ShapeDtypeStruct((128, 4096), BF16)] * 2,
        in_specs=[SMEM] + [ANY] * 6,
        out_specs=[ANY] * 2,
        scratch_shapes=[pltpu.VMEM((2, 128, 4096), BF16), pltpu.SemaphoreType.DMA((14,))],
        compiler_params=params(),
        cost_estimate=COST,
        name="finish_kv",
    )(meta, *dkvs)


def local(query, key, value, out_grad, offsets):
    place = lax.axis_index("ctx")
    slot = lax.axis_index("head")
    xh, y = place // 4 % 2, place % 4
    group = slot ^ (2 * xh)
    routes = [None] + [rel_route(r) for r in (1, 2, 3)]
    units, levels = unit_groups(), z_groups()

    def go(block, r):
        return block if r == 0 else send(block, routes[r])

    def spread(blocks):
        return [go(block, r) for r, block in enumerate(blocks)]

    table = jnp.concatenate([block.reshape(16) for block in spread([offsets] * 4)])
    meta = jnp.concatenate([table, jnp.stack([group, 2 * xh, xh * 4 + y])])

    acts, kvs, qgs = open_blocks(meta, key, value, query, out_grad)
    acts = spread(acts)
    act, sent, passed = arrange(acts, kvs[1:])
    kvs = spread([kvs[0], *passed])
    qgs = spread(qgs)

    mid, top, far = fan(unit_exchange(sent, units))
    oth = send(mid[:2], ZL_ROUTE)
    topz = unit_exchange(far, levels)
    st = unit_exchange(stats(act, kvs, [oth, topz]), units)
    out_mid, out_top, mid_oth, top_far = unit(meta, (mid, top, oth, topz, st), [qgs[2]])
    near = send(mid_oth, ZL_ROUTE)
    tops = unit_exchange(top_far, levels)
    first = main(meta, kvs, qgs, 0, [], [top_far])
    second = main(meta, kvs, qgs, 4, first[:2], [])
    oqs = [second[0], go(second[1], 1)]
    oqs += [go(first[2], 2), go(first[3], 3), go(second[2], 2), go(second[3], 3)]
    sums = combine((out_mid, out_top, near, tops), [second[4], oqs[2], oqs[3]])
    back = unit_exchange(sums, units)
    early = late(meta, act, back, first[4], first[5], kvs, 0, [], [oqs[4]])
    dkv2, dkv3 = send(early[2], routes[2]), send(early[3], routes[3])
    held = [early[0], early[1], *early[4:]]
    final = late(meta, act, back, second[4], second[5], kvs, 4, held, [oqs[5]])
    oas = spread(final[4:])
    dkvs = [final[0], go(final[1], 1), dkv2, dkv3, go(final[2], 2), go(final[3], 3)]
    attended, query_grad = finish_oq(meta, oqs, oas, [dkv2])
    key_grad, value_grad = finish_kv(meta, dkvs)
    return attended, query_grad, key_grad, value_grad


def solution(mesh):
    rows = P(AXES, None)
    return jax.shard_map(
        local,
        mesh=mesh,
        in_specs=(rows, rows, rows, rows, P(None, "head")),
        out_specs=(rows, rows, rows, rows),
        check_vma=False,
    )
```

time: 198 us -> 168 us (0.85)
  starting transfers between devices: 71.8 us -> 54 us
  local copies, waits for them, and re-layouts: 26 us -> 9.61 us
  waiting for transfers between devices: 49 us -> 51.9 us
    ppermute x42 -> x27, starting transfers between devices: 53.3 us -> 26.7 us  [send(): return lax.ppermute(value, AXES, where)]
    unnamed x63 -> x74, local copies, waits for them, and re-layouts: 18.1 us -> 8.68 us
    all_to_all x3 -> x5, starting transfers between devices: 18.4 us -> 27.4 us  [unit_exchange(): lax.all_to_all(flat, AXES, 0, 0, tiled=True, axis_index_groups=groups)]
    all_to_all x3 -> x5, waiting for transfers between devices: 3.71 us -> 12.2 us  [unit_exchange(): lax.all_to_all(flat, AXES, 0, 0, tiled=True, axis_index_groups=groups)]
    ppermute x42 -> x27, waiting for transfers between devices: 45.3 us -> 39.7 us  [send(): return lax.ppermute(value, AXES, where)]
    transpose x3 -> x0, local copies, waits for them, and re-layouts: 2.6 us -> none  [the longest x1 1.73 us: local(): mid = got[:, :, :32].transpose(1, 0, 2, 3).reshape(4, 256, 128)]
    pallas_call x8 -> x9, Pallas kernels: 39.7 us -> 39 us  [the longest x2 14.2 us: main(): pl.pallas_call(functools.partial(main_kernel, first), grid=(4,), out_shap...]
  transfers between devices with their start and end apart: 45 -> 32, of which waited for: 16 -> 15; matrix products, arithmetic and copies ran while one was open for 5% -> 0% of each run, Pallas kernels for 22% -> 22%
where the time goes in v2:
time: 168 us; the launch traced here: 166 us
  starting transfers between devices  54 us (32%)
  waiting for transfers between devices  51.9 us (31%)
  Pallas kernels  49.6 us (30%)
  local copies, waits for them, and re-layouts  9.61 us (6%)
    ppermute x27, waiting for transfers between devices, send(): return lax.ppermute(value, AXES, where)  39.7 us
    all_to_all x5, starting transfers between devices, unit_exchange(): lax.all_to_all(flat, AXES, 0, 0, tiled=True, axis_index_groups=groups)  27.4 us
    ppermute x27, starting transfers between devices, send(): return lax.ppermute(value, AXES, where)  26.7 us
    pallas_call x2, Pallas kernels, main(): pl.pallas_call(functools.partial(main_kernel, first), grid=(4,), out_shap...  14.2 us
    all_to_all x5, waiting for transfers between devices, unit_exchange(): lax.all_to_all(flat, AXES, 0, 0, tiled=True, axis_index_groups=groups)  12.2 us
    pallas_call x2, Pallas kernels, late(): pl.pallas_call(functools.partial(late_kernel, first), grid=(4,), out_shap...  9.95 us
    unnamed x74, local copies, waits for them, and re-layouts  8.68 us
    pallas_call x1, Pallas kernels, open_blocks(): pl.pallas_call(open_kernel, out_shape=[jax.ShapeDtypeStruct((40, 1024), B...  5.39 us
  transfers between devices with their start and end apart: 32, of which 15 were waited for; matrix products, arithmetic and copies ran while one was open for 0% of the time, Pallas kernels for 22%

profile of v2, /device:TPU:1, one launch (start us, length us, event | category | flops | bytes accessed | tf_op | source)
XLA Modules:
  0.0 166.3 jit_solution(17587983577241892762)
XLA Ops:
  0.6 3.3 %collective-permute-start = (s32[2,8]{1,0:T(2,128)}, s32[2,8]{1,0:T(2,128)S(1)}, u32[]{:S(2)}, u32[]{:S(2)}) collective-permute-start(s32[2,8]{1,0:T(2,128)} %param.9), channel_id=1, source_target_pairs={{0,1},{1,0},{2,3},{3,2},{4,5},{5,4},{6,7},{7,6},{8,9},{9,8},{10,11... | collective-permute-start | bytes 200 | tf_op jit(solution)/shard_map/ppermute | solution.py:46
  7.9 5.4 %open.1 = (bf16[40,1024]{1,0:T(8,128)(2,1)}, bf16[40,1024]{1,0:T(8,128)(2,1)}, bf16[40,1024]{1,0:T(8,128)(2,1)}, bf16[40,1024]{1,0:T(8,128)(2,1)}, bf16[256,1024...) custom-call(s32[67]{0:T(128)} %concatenate.3.meta, ...), custom_call_target="tpu_custom_call" | custom-call | bytes 1024 | tf_op jit(solution)/shard_map/open/pallas_call | solution.py:124
  15.9 2.9 %collective-permute-done.4.a2 = bf16[40,1024]{1,0:T(8,128)(2,1)S(1)} collective-permute-done((bf16[40,1024]{1,0:T(8,128)(2,1)}, bf16[40,1024]{1,0:T(8,128)(2,1)S(1)}, u32[]{:S(2)}, u32[]{:S(2)}) %collective-permute-start.4) | collective-permute-done | bytes 81952 | tf_op jit(solution)/shard_map/ppermute | solution.py:46
  21.1 1.9 %arrange.1 = (bf16[4,40,1024]{2,1,0:T(8,128)(2,1)}, bf16[8,160,128]{2,1,0:T(8,128)(2,1)}, bf16[256,1024]{1,0:T(8,128)(2,1)}, bf16[256,1024]{1,0:T(8,128)(2,1)}, bf16[256,1024]{1,0:T(8,128)(2,1)}) custom-call(bf16[40,1024]{1,0:T(8,128)(2,1)} %get-tuple-element.61.a0, ...), custom_call_target="tpu_custom_call", output_to_operand_aliasing={{2}: (4, {}), {3}: (5, {}), {4}: (6, {})} | custom-call | bytes 1024 | tf_op jit(solution)/shard_map/arrange/pallas_call | solution.py:163
  23.4 5.0 %all-to-all-start = ((bf16[8,160,128]{2,1,0:T(8,128)(2,1)}), bf16[8,160,128]{2,1,0:T(8,128)(2,1)S(1)}, u32[]{:S(2)}, u32[]{:S(2)}) async-start(bf16[8,160,128]{2,1,0:T(8,128)(2,1)} %get-tuple-element.75), calls=%async_computation | async-start | bytes 655360 | tf_op jit(solution)/shard_map/all_to_all | solution.py:58
  28.7 1.9 %collective-permute-start.8 = (bf16[256,1024]{1,0:T(8,128)(2,1)}, bf16[256,1024]{1,0:T(8,128)(2,1)S(1)}, u32[]{:S(2)}, u32[]{:S(2)}) collective-permute-start(bf16[256,1024]{1,0:T(8,128)(2,1)} %get-tuple-element.70), channel_id=1, source_target_pairs={{0,3},{1,2},{2,1},{3,0},{4,7},{5,6},{6,5},{7,4},{8,11},{9,10},{10,... | collective-permute-start | bytes 1572872 | tf_op jit(solution)/shard_map/ppermute | solution.py:46
  30.9 5.0 %all-to-all-done.got = bf16[8,160,128]{2,1,0:T(8,128)(2,1)S(1)} async-done(((bf16[8,160,128]{2,1,0:T(8,128)(2,1)}), bf16[8,160,128]{2,1,0:T(8,128)(2,1)S(1)}, u32[]{:S(2)}, u32[]{:S(2)}) %all-to-all-start) | async-done | bytes 327712 | tf_op jit(solution)/shard_map/all_to_all | solution.py:58
  36.7 1.9 %fan.1 = (bf16[4,256,128]{2,1,0:T(8,128)(2,1)}, bf16[4,64,128]{2,1,0:T(8,128)(2,1)}, bf16[8,128,128]{2,1,0:T(8,128)(2,1)}) custom-call(bf16[8,160,128]{2,1,0:T(8,128)(2,1)} %copy-done.8), custom_call_target="tpu_custom_call" | custom-call | bytes 1024 | tf_op jit(solution)/shard_map/fan/pallas_call | solution.py:194
  38.6 8.3 %all-to-all-start.1 = ((bf16[8,128,128]{2,1,0:T(8,128)(2,1)}), bf16[8,128,128]{2,1,0:T(8,128)(2,1)S(1)}, u32[]{:S(2)}, u32[]{:S(2)}) async-start(bf16[8,128,128]{2,1,0:T(8,128)(2,1)} %get-tuple-element.78), calls=%async_computation.1 | async-start | bytes 524288 | tf_op jit(solution)/shard_map/all_to_all | solution.py:58
  48.5 7.1 %collective-permute-done.12.refs_4_.oth = bf16[2,256,128]{2,1,0:T(8,128)(2,1)S(1)} collective-permute-done((bf16[2,256,128]{2,1,0:T(8,128)(2,1)S(1)}, bf16[2,256,128]{2,1,0:T(8,128)(2,1)S(1)}, u32[]{:S(2)}, u32[]{:S(2)}) %collective-permute-start.12) | collective-permute-done | bytes 131104 | tf_op jit(solution)/shard_map/ppermute | solution.py:46
  55.6 3.1 %collective-permute-start.9 = (bf16[256,1024]{1,0:T(8,128)(2,1)}, bf16[256,1024]{1,0:T(8,128)(2,1)S(1)}, u32[]{:S(2)}, u32[]{:S(2)}) collective-permute-start(bf16[256,1024]{1,0:T(8,128)(2,1)} %get-tuple-element.72), channel_id=1, source_target_pairs={{0,1},{1,0},{2,3},{3,2},{4,5},{5,4},{6,7},{7,6},{8,9},{9,8},{10,11... | collective-permute-start | bytes 1572872 | tf_op jit(solution)/shard_map/ppermute | solution.py:46
  59.9 3.7 %stats.1 = f32[8,8,128]{2,1,0:T(8,128)} custom-call(bf16[4,40,1024]{2,1,0:T(8,128)(2,1)} %get-tuple-element.79.act.refs_0_, bf16[256,1024]{1,0:T(8,128)(2,1)} %get-tuple-element.60.refs_0_.refs_4_, bf16[256,1024]{1,0:T(8,128)(2,1)} %copy-done, bf16[256,1024]{1,0:T(8,128)(2,1)} %copy-done.1, bf16[256,1024]{1,0:T(8,128)(2,1)} %copy-done.2, ...), custom_call_target="tpu_custom_call" | custom-call | bytes 1024 | tf_op jit(solution)/shard_map/stats/pallas_call | solution.py:241
  63.5 4.5 %all-to-all-start.2 = ((f32[8,8,128]{2,1,0:T(8,128)}), f32[8,8,128]{2,1,0:T(8,128)S(1)}, u32[]{:S(2)}, u32[]{:S(2)}) async-start(f32[8,8,128]{2,1,0:T(8,128)} %stats.1), calls=%async_computation.2 | async-start | bytes 65536 | tf_op jit(solution)/shard_map/all_to_all | solution.py:58
  68.0 6.3 %all-to-all-done.2.st = f32[8,8,128]{2,1,0:T(8,128)S(1)} async-done(((f32[8,8,128]{2,1,0:T(8,128)}), f32[8,8,128]{2,1,0:T(8,128)S(1)}, u32[]{:S(2)}, u32[]{:S(2)}) %all-to-all-start.2) | async-done | bytes 32800 | tf_op jit(solution)/shard_map/all_to_all | solution.py:58
  75.0 3.6 %unit.1 = (bf16[5,256,128]{2,1,0:T(8,128)(2,1)}, bf16[3,64,128]{2,1,0:T(8,128)(2,1)}, bf16[2,256,128]{2,1,0:T(8,128)(2,1)}, bf16[8,128,128]{2,1,0:T(8,128)(2,1)}) custom-call(s32[67]{0:T(128)} %concatenate.3.meta, bf16[4,256,128]{2,1,0:T(8,128)(2,1)} %get-tuple-element.76.mid, bf16[4,64,128]{2,1,0:T(8,128)(2,1)} %get-tuple-element.77.top, ...), custom_call_target="tpu_custom_call" | custom-call | bytes 1024 | tf_op jit(solution)/shard_map/unit/pallas_call | solution.py:352
  78.5 5.9 %all-to-all-start.3 = ((bf16[8,128,128]{2,1,0:T(8,128)(2,1)}), bf16[8,128,128]{2,1,0:T(8,128)(2,1)S(1)}, u32[]{:S(2)}, u32[]{:S(2)}) async-start(bf16[8,128,128]{2,1,0:T(8,128)(2,1)} %get-tuple-element.80.refs_8_), calls=%async_computation.3 | async-start | bytes 524288 | tf_op jit(solution)/shard_map/all_to_all | solution.py:58
  85.5 7.1 %main.2 = (bf16[256,1024]{1,0:T(8,128)(2,1)}, bf16[256,1024]{1,0:T(8,128)(2,1)}, bf16[256,512]{1,0:T(8,128)(2,1)}, bf16[256,512]{1,0:T(8,128)(2,1)}, f32[4,512,128]{2,1,0:T(8,128)}, /*index=5*/f32[4,512,128]{2,1,0:T(8,128)}) custom-call(s32[67]{0:T(128)} %concatenate.3.meta, bf16[256,1024]{1,0:T(8,128)(2,1)} %get-tuple-element.60.refs_0_.refs_4_, ...), custom_call_target="tpu_custom_call" | custom-call | bytes 1024 | tf_op jit(solution)/shard_map/main/pallas_call | solution.py:438
  92.7 2.9 %collective-permute-start.15 = (bf16[256,512]{1,0:T(8,128)(2,1)}, bf16[256,512]{1,0:T(8,128)(2,1)S(1)}, u32[]{:S(2)}, u32[]{:S(2)}) collective-permute-start(bf16[256,512]{1,0:T(8,128)(2,1)} %get-tuple-element.86), channel_id=1, source_target_pairs={{0,3},{1,2},{2,1},{3,0},{4,7},{5,6},{6,5},{7,4},{8,11},{9,10},{10,... | collective-permute-start | bytes 786440 | tf_op jit(solution)/shard_map/ppermute | solution.py:46
  97.3 7.1 %main.3 = (bf16[256,1024]{1,0:T(8,128)(2,1)}, bf16[256,1024]{1,0:T(8,128)(2,1)}, bf16[256,512]{1,0:T(8,128)(2,1)}, bf16[256,512]{1,0:T(8,128)(2,1)}, f32[4,512,128]{2,1,0:T(8,128)}, /*index=5*/f32[4,512,128]{2,1,0:T(8,128)}) custom-call(s32[67]{0:T(128)} %concatenate.3.meta, ...), custom_call_target="tpu_custom_call", output_to_operand_aliasing={{0}: (9, {}), {1}: (10, {})} | custom-call | bytes 1024 | tf_op jit(solution)/shard_map/main/pallas_call | solution.py:438
  104.4 2.1 %collective-permute-done.15.refs_2_.refs_3_ = bf16[256,512]{1,0:T(8,128)(2,1)S(1)} collective-permute-done((bf16[256,512]{1,0:T(8,128)(2,1)}, bf16[256,512]{1,0:T(8,128)(2,1)S(1)}, u32[]{:S(2)}, u32[]{:S(2)}) %collective-permute-start.15) | collective-permute-done | bytes 262176 | tf_op jit(solution)/shard_map/ppermute | solution.py:46
  107.3 2.0 %combine.1 = bf16[8,200,128]{2,1,0:T(8,128)(2,1)} custom-call(bf16[5,256,128]{2,1,0:T(8,128)(2,1)} %get-tuple-element.89.out_mid, bf16[3,64,128]{2,1,0:T(8,128)(2,1)} %get-tuple-element.90.out_top, bf16[2,256,128]{2,1,0:T(8,128)(2,1)} %copy-done.24, bf16[8,128,128]{2,1,0:T(8,128)(2,1)} %copy-done.11, f32[4,512,128]{2,1,0:T(8,128)} %get-tuple-element.92.refs_0_.refs_2_, ...), custom_call_target="tpu_custom_call" | custom-call | bytes 1024 | tf_op jit(solution)/shard_map/combine/pallas_call | solution.py:384
  109.4 3.6 %all-to-all-start.4 = ((bf16[8,200,128]{2,1,0:T(8,128)(2,1)}), bf16[8,200,128]{2,1,0:T(8,128)(2,1)S(1)}, u32[]{:S(2)}, u32[]{:S(2)}) async-start(bf16[8,200,128]{2,1,0:T(8,128)(2,1)} %combine.1), calls=%async_computation.4 | async-start | bytes 819200 | tf_op jit(solution)/shard_map/all_to_all | solution.py:58
  114.9 6.2 %collective-permute-done.16.refs_8_.refs_4_ = bf16[256,512]{1,0:T(8,128)(2,1)S(1)} collective-permute-done((bf16[256,512]{1,0:T(8,128)(2,1)S(1)}, bf16[256,512]{1,0:T(8,128)(2,1)S(1)}, u32[]{:S(2)}, u32[]{:S(2)}) %collective-permute-start.16) | collective-permute-done | bytes 262176 | tf_op jit(solution)/shard_map/ppermute | solution.py:46
  122.7 5.0 %late.2 = (bf16[256,1024]{1,0:T(8,128)(2,1)}, bf16[256,1024]{1,0:T(8,128)(2,1)}, bf16[256,512]{1,0:T(8,128)(2,1)}, bf16[256,512]{1,0:T(8,128)(2,1)}, bf16[32,102...) custom-call(s32[67]{0:T(128)} %concatenate.3.meta, ...), custom_call_target="tpu_custom_call" | custom-call | bytes 1024 | tf_op jit(solution)/shard_map/late/pallas_call | solution.py:497
  128.4 5.0 %late.3 = (bf16[256,1024]{1,0:T(8,128)(2,1)}, bf16[256,1024]{1,0:T(8,128)(2,1)}, bf16[256,512]{1,0:T(8,128)(2,1)}, bf16[256,512]{1,0:T(8,128)(2,1)}, bf16[32,102...) custom-call(s32[67]{0:T(128)} %concatenate.3.meta, ...), custom_call_target="tpu_custom_call", output_to_operand_aliasing={{0}: (10, {}), {1}: (11, {}), {4}: (12, {}), {5}: (13, {}),... | custom-call | bytes 1024 | tf_op jit(solution)/shard_map/late/pallas_call | solution.py:497
  137.9 2.1 %collective-permute-done.21.refs_9_ = bf16[32,1024]{1,0:T(8,128)(2,1)S(1)} collective-permute-done((bf16[32,1024]{1,0:T(8,128)(2,1)}, bf16[32,1024]{1,0:T(8,128)(2,1)S(1)}, u32[]{:S(2)}, u32[]{:S(2)}) %collective-permute-start.21) | collective-permute-done | bytes 65568 | tf_op jit(solution)/shard_map/ppermute | solution.py:46
  140.9 4.0 %collective-permute-done.22.refs_10_.refs_2_ = bf16[256,512]{1,0:T(8,128)(2,1)S(1)} collective-permute-done((bf16[256,512]{1,0:T(8,128)(2,1)S(1)}, bf16[256,512]{1,0:T(8,128)(2,1)S(1)}, u32[]{:S(2)}, u32[]{:S(2)}) %collective-permute-start.22) | collective-permute-done | bytes 262176 | tf_op jit(solution)/shard_map/ppermute | solution.py:46
  145.6 3.8 %finish_oq.1 = (bf16[128,4096]{1,0:T(8,128)(2,1)}, bf16[128,4096]{1,0:T(8,128)(2,1)}) custom-call(s32[67]{0:T(128)} %concatenate.3.meta, bf16[256,1024]{1,0:T(8,128)(2,1)} %get-tuple-element.83.refs_0_, bf16[256,1024]{1,0:T(8,128)(2,1)} %copy-done.18, bf16[256,512]{1,0:T(8,128)(2,1)} %copy-done.12, bf16[256,512]{1,0:T(8,128)(2,1)} %copy-done.13, ...), custom_call_target="tpu_custom_call" | custom-call | bytes 1024 | tf_op jit(solution)/shard_map/finish_oq/pallas_call | solution.py:545
  149.4 1.8 %collective-permute-done.24.refs_3_ = bf16[256,512]{1,0:T(8,128)(2,1)S(1)} collective-permute-done((bf16[256,512]{1,0:T(8,128)(2,1)S(1)}, bf16[256,512]{1,0:T(8,128)(2,1)S(1)}, u32[]{:S(2)}, u32[]{:S(2)}) %collective-permute-start.24) | collective-permute-done | bytes 262176 | tf_op jit(solution)/shard_map/ppermute | solution.py:46
  151.2 5.0 %collective-permute-done.25.refs_4_ = bf16[256,512]{1,0:T(8,128)(2,1)S(1)} collective-permute-done((bf16[256,512]{1,0:T(8,128)(2,1)}, bf16[256,512]{1,0:T(8,128)(2,1)S(1)}, u32[]{:S(2)}, u32[]{:S(2)}) %collective-permute-start.25) | collective-permute-done | bytes 262176 | tf_op jit(solution)/shard_map/ppermute | solution.py:46
  156.1 5.8 %collective-permute-done.26.refs_5_ = bf16[256,512]{1,0:T(8,128)(2,1)S(1)} collective-permute-done((bf16[256,512]{1,0:T(8,128)(2,1)}, bf16[256,512]{1,0:T(8,128)(2,1)S(1)}, u32[]{:S(2)}, u32[]{:S(2)}) %collective-permute-start.26) | collective-permute-done | bytes 262176 | tf_op jit(solution)/shard_map/ppermute | solution.py:46
  162.9 3.3 %finish_kv.1 = (bf16[128,4096]{1,0:T(8,128)(2,1)}, bf16[128,4096]{1,0:T(8,128)(2,1)}) custom-call(s32[67]{0:T(128)} %concatenate.3.meta, bf16[256,1024]{1,0:T(8,128)(2,1)} %get-tuple-element.109.refs_0_, bf16[256,1024]{1,0:T(8,128)(2,1)} %copy-done.16, bf16[256,512]{1,0:T(8,128)(2,1)} %copy-done.10, bf16[256,512]{1,0:T(8,128)(2,1)} %copy-done.20, ...), custom_call_target="tpu_custom_call" | custom-call | bytes 1024 | tf_op jit(solution)/shard_map/finish_kv/pallas_call | solution.py:583
  (124 shorter events, 28.8 us)
Async XLA Ops:
  0.6 5.6 %collective-permute-start = (s32[2,8]{1,0:T(2,128)}, s32[2,8]{1,0:T(2,128)S(1)}, u32[]{:S(2)}, u32[]{:S(2)}) collective-permute-start(s32[2,8]{1,0:T(2,128)} %param.9), channel_id=1, source_target_pairs={{0,1},{1,0},{2,3},{3,2},{4,5},{5,4},{6,7},{7,6},{8,9},{9,8},{10,11... | collective-permute-start | bytes 200 | tf_op jit(solution)/shard_map/ppermute | solution.py:46
  4.0 3.2 %collective-permute-start.2 = (s32[2,8]{1,0:T(2,128)}, s32[2,8]{1,0:T(2,128)S(1)}, u32[]{:S(2)}, u32[]{:S(2)}) collective-permute-start(s32[2,8]{1,0:T(2,128)} %param.9), channel_id=1, source_target_pairs={{0,3},{1,2},{2,1},{3,0},{4,7},{5,6},{6,5},{7,4},{8,11},{9,10},{10,... | collective-permute-start | bytes 200 | tf_op jit(solution)/shard_map/ppermute | solution.py:46
  4.0 3.3 %collective-permute-start.1 = (s32[2,8]{1,0:T(2,128)}, s32[2,8]{1,0:T(2,128)S(1)}, u32[]{:S(2)}, u32[]{:S(2)}) collective-permute-start(s32[2,8]{1,0:T(2,128)} %param.9), channel_id=1, source_target_pairs={{0,2},{1,3},{2,0},{3,1},{4,6},{5,7},{6,4},{7,5},{8,10},{9,11},{10,... | collective-permute-start | bytes 200 | tf_op jit(solution)/shard_map/ppermute | solution.py:46
  13.3 2.5 %collective-permute-start.3 = (bf16[40,1024]{1,0:T(8,128)(2,1)}, bf16[40,1024]{1,0:T(8,128)(2,1)S(1)}, u32[]{:S(2)}, u32[]{:S(2)}) collective-permute-start(bf16[40,1024]{1,0:T(8,128)(2,1)} %get-tuple-element.62), channel_id=1, source_target_pairs={{0,1},{1,0},{2,3},{3,2},{4,5},{5,4},{6,7},{7,6},{8,9},{9,8},{10,11... | collective-permute-start | bytes 245768 | tf_op jit(solution)/shard_map/ppermute | solution.py:46
  14.1 4.6 %collective-permute-start.4 = (bf16[40,1024]{1,0:T(8,128)(2,1)}, bf16[40,1024]{1,0:T(8,128)(2,1)S(1)}, u32[]{:S(2)}, u32[]{:S(2)}) collective-permute-start(bf16[40,1024]{1,0:T(8,128)(2,1)} %get-tuple-element.63), channel_id=1, source_target_pairs={{0,2},{1,3},{2,0},{3,1},{4,6},{5,7},{6,4},{7,5},{8,10},{9,11},{10,... | collective-permute-start | bytes 245768 | tf_op jit(solution)/shard_map/ppermute | solution.py:46
  15.8 4.7 %collective-permute-start.5 = (bf16[40,1024]{1,0:T(8,128)(2,1)}, bf16[40,1024]{1,0:T(8,128)(2,1)S(1)}, u32[]{:S(2)}, u32[]{:S(2)}) collective-permute-start(bf16[40,1024]{1,0:T(8,128)(2,1)} %get-tuple-element.64), channel_id=1, source_target_pairs={{0,3},{1,2},{2,1},{3,0},{4,7},{5,6},{6,5},{7,4},{8,11},{9,10},{10,... | collective-permute-start | bytes 245768 | tf_op jit(solution)/shard_map/ppermute | solution.py:46
  23.0 35.7 %collective-permute-start.6 = (bf16[256,1024]{1,0:T(8,128)(2,1)}, bf16[256,1024]{1,0:T(8,128)(2,1)S(1)}, u32[]{:S(2)}, u32[]{:S(2)}) collective-permute-start(bf16[256,1024]{1,0:T(8,128)(2,1)} %get-tuple-element.68), channel_id=1, source_target_pairs={{0,1},{1,0},{2,3},{3,2},{4,5},{5,4},{6,7},{7,6},{8,9},{9,8},{10,11... | collective-permute-start | bytes 1572872 | tf_op jit(solution)/shard_map/ppermute | solution.py:46
  23.4 12.6 %all-to-all-start = ((bf16[8,160,128]{2,1,0:T(8,128)(2,1)}), bf16[8,160,128]{2,1,0:T(8,128)(2,1)S(1)}, u32[]{:S(2)}, u32[]{:S(2)}) async-start(bf16[8,160,128]{2,1,0:T(8,128)(2,1)} %get-tuple-element.75), calls=%async_computation | async-start | bytes 655360 | tf_op jit(solution)/shard_map/all_to_all | solution.py:58
  28.4 30.2 %collective-permute-start.7 = (bf16[256,1024]{1,0:T(8,128)(2,1)}, bf16[256,1024]{1,0:T(8,128)(2,1)S(1)}, u32[]{:S(2)}, u32[]{:S(2)}) collective-permute-start(bf16[256,1024]{1,0:T(8,128)(2,1)} %get-tuple-element.69), channel_id=1, source_target_pairs={{0,2},{1,3},{2,0},{3,1},{4,6},{5,7},{6,4},{7,5},{8,10},{9,11},{10,... | collective-permute-start | bytes 1572872 | tf_op jit(solution)/shard_map/ppermute | solution.py:46
  28.7 30.0 %collective-permute-start.8 = (bf16[256,1024]{1,0:T(8,128)(2,1)}, bf16[256,1024]{1,0:T(8,128)(2,1)S(1)}, u32[]{:S(2)}, u32[]{:S(2)}) collective-permute-start(bf16[256,1024]{1,0:T(8,128)(2,1)} %get-tuple-element.70), channel_id=1, source_target_pairs={{0,3},{1,2},{2,1},{3,0},{4,7},{5,6},{6,5},{7,4},{8,11},{9,10},{10,... | collective-permute-start | bytes 1572872 | tf_op jit(solution)/shard_map/ppermute | solution.py:46
  30.6 37.4 %collective-permute-start.10 = (bf16[256,1024]{1,0:T(8,128)(2,1)}, bf16[256,1024]{1,0:T(8,128)(2,1)S(1)}, u32[]{:S(2)}, u32[]{:S(2)}) collective-permute-start(bf16[256,1024]{1,0:T(8,128)(2,1)} %get-tuple-element.73), channel_id=1, source_target_pairs={{0,2},{1,3},{2,0},{3,1},{4,6},{5,7},{6,4},{7,5},{8,10},{9,11},{10,... | collective-permute-start | bytes 1572872 | tf_op jit(solution)/shard_map/ppermute | solution.py:46
  38.6 20.1 %all-to-all-start.1 = ((bf16[8,128,128]{2,1,0:T(8,128)(2,1)}), bf16[8,128,128]{2,1,0:T(8,128)(2,1)S(1)}, u32[]{:S(2)}, u32[]{:S(2)}) async-start(bf16[8,128,128]{2,1,0:T(8,128)(2,1)} %get-tuple-element.78), calls=%async_computation.1 | async-start | bytes 524288 | tf_op jit(solution)/shard_map/all_to_all | solution.py:58
  46.9 8.6 %collective-permute-start.12 = (bf16[2,256,128]{2,1,0:T(8,128)(2,1)S(1)}, bf16[2,256,128]{2,1,0:T(8,128)(2,1)S(1)}, u32[]{:S(2)}, u32[]{:S(2)}) collective-permute-start(bf16[2,256,128]{2,1,0:T(8,128)(2,1)S(1)} %slice.3), channel_id=1, source_target_pairs={{0,32},{1,33},{2,34},{3,35},{4,36},{5,37},{6,38},{7,39},{8,40},{9,... | collective-permute-start | bytes 393224 | tf_op jit(solution)/shard_map/ppermute | solution.py:46
  55.6 28.9 %collective-permute-start.9 = (bf16[256,1024]{1,0:T(8,128)(2,1)}, bf16[256,1024]{1,0:T(8,128)(2,1)S(1)}, u32[]{:S(2)}, u32[]{:S(2)}) collective-permute-start(bf16[256,1024]{1,0:T(8,128)(2,1)} %get-tuple-element.72), channel_id=1, source_target_pairs={{0,1},{1,0},{2,3},{3,2},{4,5},{5,4},{6,7},{7,6},{8,9},{9,8},{10,11... | collective-permute-start | bytes 1572872 | tf_op jit(solution)/shard_map/ppermute | solution.py:46
  58.6 25.8 %collective-permute-start.11 = (bf16[256,1024]{1,0:T(8,128)(2,1)}, bf16[256,1024]{1,0:T(8,128)(2,1)S(1)}, u32[]{:S(2)}, u32[]{:S(2)}) collective-permute-start(bf16[256,1024]{1,0:T(8,128)(2,1)} %get-tuple-element.74), channel_id=1, source_target_pairs={{0,3},{1,2},{2,1},{3,0},{4,7},{5,6},{6,5},{7,4},{8,11},{9,10},{10,... | collective-permute-start | bytes 1572872 | tf_op jit(solution)/shard_map/ppermute | solution.py:46
  63.5 10.8 %all-to-all-start.2 = ((f32[8,8,128]{2,1,0:T(8,128)}), f32[8,8,128]{2,1,0:T(8,128)S(1)}, u32[]{:S(2)}, u32[]{:S(2)}) async-start(f32[8,8,128]{2,1,0:T(8,128)} %stats.1), calls=%async_computation.2 | async-start | bytes 65536 | tf_op jit(solution)/shard_map/all_to_all | solution.py:58
  78.5 28.0 %all-to-all-start.3 = ((bf16[8,128,128]{2,1,0:T(8,128)(2,1)}), bf16[8,128,128]{2,1,0:T(8,128)(2,1)S(1)}, u32[]{:S(2)}, u32[]{:S(2)}) async-start(bf16[8,128,128]{2,1,0:T(8,128)(2,1)} %get-tuple-element.80.refs_8_), calls=%async_computation.3 | async-start | bytes 524288 | tf_op jit(solution)/shard_map/all_to_all | solution.py:58
  92.6 11.9 %collective-permute-start.14 = (bf16[256,512]{1,0:T(8,128)(2,1)}, bf16[256,512]{1,0:T(8,128)(2,1)S(1)}, u32[]{:S(2)}, u32[]{:S(2)}) collective-permute-start(bf16[256,512]{1,0:T(8,128)(2,1)} %get-tuple-element.85), channel_id=1, source_target_pairs={{0,2},{1,3},{2,0},{3,1},{4,6},{5,7},{6,4},{7,5},{8,10},{9,11},{10,... | collective-permute-start | bytes 786440 | tf_op jit(solution)/shard_map/ppermute | solution.py:46
  92.7 13.8 %collective-permute-start.15 = (bf16[256,512]{1,0:T(8,128)(2,1)}, bf16[256,512]{1,0:T(8,128)(2,1)S(1)}, u32[]{:S(2)}, u32[]{:S(2)}) collective-permute-start(bf16[256,512]{1,0:T(8,128)(2,1)} %get-tuple-element.86), channel_id=1, source_target_pairs={{0,3},{1,2},{2,1},{3,0},{4,7},{5,6},{6,5},{7,4},{8,11},{9,10},{10,... | collective-permute-start | bytes 786440 | tf_op jit(solution)/shard_map/ppermute | solution.py:46
  95.6 8.8 %collective-permute-start.18 = (bf16[2,256,128]{2,1,0:T(8,128)(2,1)S(1)}, bf16[2,256,128]{2,1,0:T(8,128)(2,1)S(1)}, u32[]{:S(2)}, u32[]{:S(2)}) collective-permute-start(bf16[2,256,128]{2,1,0:T(8,128)(2,1)S(1)} %copy-done.35), channel_id=1, source_target_pairs={{0,32},{1,33},{2,34},{3,35},{4,36},{5,37},{6,38},{7,39},{8,40},{9,... | collective-permute-start | bytes 393224 | tf_op jit(solution)/shard_map/ppermute | solution.py:46
  109.4 12.6 %all-to-all-start.4 = ((bf16[8,200,128]{2,1,0:T(8,128)(2,1)}), bf16[8,200,128]{2,1,0:T(8,128)(2,1)S(1)}, u32[]{:S(2)}, u32[]{:S(2)}) async-start(bf16[8,200,128]{2,1,0:T(8,128)(2,1)} %combine.1), calls=%async_computation.4 | async-start | bytes 819200 | tf_op jit(solution)/shard_map/all_to_all | solution.py:58
  113.0 8.1 %collective-permute-start.16 = (bf16[256,512]{1,0:T(8,128)(2,1)S(1)}, bf16[256,512]{1,0:T(8,128)(2,1)S(1)}, u32[]{:S(2)}, u32[]{:S(2)}) collective-permute-start(bf16[256,512]{1,0:T(8,128)(2,1)S(1)} %copy-done.34), channel_id=1, source_target_pairs={{0,2},{1,3},{2,0},{3,1},{4,6},{5,7},{6,4},{7,5},{8,10},{9,11},{10,... | collective-permute-start | bytes 786440 | tf_op jit(solution)/shard_map/ppermute | solution.py:46
  113.1 22.7 %collective-permute-start.13 = (bf16[256,1024]{1,0:T(8,128)(2,1)S(1)}, bf16[256,1024]{1,0:T(8,128)(2,1)S(1)}, u32[]{:S(2)}, u32[]{:S(2)}) collective-permute-start(bf16[256,1024]{1,0:T(8,128)(2,1)S(1)} %copy-done.19), channel_id=1, source_target_pairs={{0,1},{1,0},{2,3},{3,2},{4,5},{5,4},{6,7},{7,6},{8,9},{9,8},{10,11... | collective-permute-start | bytes 1572872 | tf_op jit(solution)/shard_map/ppermute | solution.py:46
  113.4 14.3 %collective-permute-start.17 = (bf16[256,512]{1,0:T(8,128)(2,1)S(1)}, bf16[256,512]{1,0:T(8,128)(2,1)S(1)}, u32[]{:S(2)}, u32[]{:S(2)}) collective-permute-start(bf16[256,512]{1,0:T(8,128)(2,1)S(1)} %copy-done.33), channel_id=1, source_target_pairs={{0,3},{1,2},{2,1},{3,0},{4,7},{5,6},{6,5},{7,4},{8,11},{9,10},{10,... | collective-permute-start | bytes 786440 | tf_op jit(solution)/shard_map/ppermute | solution.py:46
  133.4 28.5 %collective-permute-start.23 = (bf16[256,1024]{1,0:T(8,128)(2,1)}, bf16[256,1024]{1,0:T(8,128)(2,1)S(1)}, u32[]{:S(2)}, u32[]{:S(2)}) collective-permute-start(bf16[256,1024]{1,0:T(8,128)(2,1)} %get-tuple-element.110), channel_id=1, source_target_pairs={{0,1},{1,0},{2,3},{3,2},{4,5},{5,4},{6,7},{7,6},{8,9},{9,8},{10,11... | collective-permute-start | bytes 1572872 | tf_op jit(solution)/shard_map/ppermute | solution.py:46
  133.5 2.6 %collective-permute-start.19 = (bf16[32,1024]{1,0:T(8,128)(2,1)}, bf16[32,1024]{1,0:T(8,128)(2,1)S(1)}, u32[]{:S(2)}, u32[]{:S(2)}) collective-permute-start(bf16[32,1024]{1,0:T(8,128)(2,1)} %get-tuple-element.103), channel_id=1, source_target_pairs={{0,1},{1,0},{2,3},{3,2},{4,5},{5,4},{6,7},{7,6},{8,9},{9,8},{10,11... | collective-permute-start | bytes 196616 | tf_op jit(solution)/shard_map/ppermute | solution.py:46
  134.0 3.9 %collective-permute-start.20 = (bf16[32,1024]{1,0:T(8,128)(2,1)}, bf16[32,1024]{1,0:T(8,128)(2,1)S(1)}, u32[]{:S(2)}, u32[]{:S(2)}) collective-permute-start(bf16[32,1024]{1,0:T(8,128)(2,1)} %get-tuple-element.104), channel_id=1, source_target_pairs={{0,2},{1,3},{2,0},{3,1},{4,6},{5,7},{6,4},{7,5},{8,10},{9,11},{10,... | collective-permute-start | bytes 196616 | tf_op jit(solution)/shard_map/ppermute | solution.py:46
  134.0 5.9 %collective-permute-start.21 = (bf16[32,1024]{1,0:T(8,128)(2,1)}, bf16[32,1024]{1,0:T(8,128)(2,1)S(1)}, u32[]{:S(2)}, u32[]{:S(2)}) collective-permute-start(bf16[32,1024]{1,0:T(8,128)(2,1)} %get-tuple-element.105), channel_id=1, source_target_pairs={{0,3},{1,2},{2,1},{3,0},{4,7},{5,6},{6,5},{7,4},{8,11},{9,10},{10,... | collective-permute-start | bytes 196616 | tf_op jit(solution)/shard_map/ppermute | solution.py:46
  135.8 9.1 %collective-permute-start.22 = (bf16[256,512]{1,0:T(8,128)(2,1)S(1)}, bf16[256,512]{1,0:T(8,128)(2,1)S(1)}, u32[]{:S(2)}, u32[]{:S(2)}) collective-permute-start(bf16[256,512]{1,0:T(8,128)(2,1)S(1)} %copy-done.32), channel_id=1, source_target_pairs={{0,2},{1,3},{2,0},{3,1},{4,6},{5,7},{6,4},{7,5},{8,10},{9,11},{10,... | collective-permute-start | bytes 786440 | tf_op jit(solution)/shard_map/ppermute | solution.py:46
  136.1 15.1 %collective-permute-start.24 = (bf16[256,512]{1,0:T(8,128)(2,1)S(1)}, bf16[256,512]{1,0:T(8,128)(2,1)S(1)}, u32[]{:S(2)}, u32[]{:S(2)}) collective-permute-start(bf16[256,512]{1,0:T(8,128)(2,1)S(1)} %copy-done.31), channel_id=1, source_target_pairs={{0,3},{1,2},{2,1},{3,0},{4,7},{5,6},{6,5},{7,4},{8,11},{9,10},{10,... | collective-permute-start | bytes 786440 | tf_op jit(solution)/shard_map/ppermute | solution.py:46
  137.9 18.3 %collective-permute-start.25 = (bf16[256,512]{1,0:T(8,128)(2,1)}, bf16[256,512]{1,0:T(8,128)(2,1)S(1)}, u32[]{:S(2)}, u32[]{:S(2)}) collective-permute-start(bf16[256,512]{1,0:T(8,128)(2,1)} %get-tuple-element.112), channel_id=1, source_target_pairs={{0,2},{1,3},{2,0},{3,1},{4,6},{5,7},{6,4},{7,5},{8,10},{9,11},{10,... | collective-permute-start | bytes 786440 | tf_op jit(solution)/shard_map/ppermute | solution.py:46
  140.0 22.0 %collective-permute-start.26 = (bf16[256,512]{1,0:T(8,128)(2,1)}, bf16[256,512]{1,0:T(8,128)(2,1)S(1)}, u32[]{:S(2)}, u32[]{:S(2)}) collective-permute-start(bf16[256,512]{1,0:T(8,128)(2,1)} %get-tuple-element.113), channel_id=1, source_target_pairs={{0,3},{1,2},{2,1},{3,0},{4,7},{5,6},{6,5},{7,4},{8,11},{9,10},{10,... | collective-permute-start | bytes 786440 | tf_op jit(solution)/shard_map/ppermute | solution.py:46
  (37 other events, 128.0 us)

commit v3 on v2

--- a/solution.py
+++ b/solution.py
@@ -395,11 +395,17 @@
 def main_kernel(first, meta, *refs):
     kvs, qgs = refs[:4], refs[4:8]
     oqs, dk, dv = refs[-6:-2], refs[-2], refs[-1]
-    o1, o2 = head_offsets(meta, 0, first + pl.program_id(0))
-    key = jnp.concatenate([kv[:128] for kv in kvs], 0)
-    value = jnp.concatenate([kv[128:] for kv in kvs], 0)
-    query = jnp.concatenate([qg[:128] for qg in qgs], 0)
-    grad = jnp.concatenate([qg[128:] for qg in qgs], 0)
+    for sub in range(2):
+        main_head(first + 2 * pl.program_id(0) + sub, sub, meta, kvs, qgs, oqs, dk, dv)
+
+
+def main_head(head, sub, meta, kvs, qgs, oqs, dk, dv):
+    o1, o2 = head_offsets(meta, 0, head)
+    cols = pl.ds(128 * sub, 128)
+    key = jnp.concatenate([kv[:128, cols] for kv in kvs], 0)
+    value = jnp.concatenate([kv[128:, cols] for kv in kvs], 0)
+    query = jnp.concatenate([qg[:128, cols] for qg in qgs], 0)
+    grad = jnp.concatenate([qg[128:, cols] for qg in qgs], 0)
     score = dot_nt(key, query) * (SCALE * LOG2E)
     weight = jnp.exp2(score - jnp.max(score, 0, keepdims=True))
     inverse = 1.0 / jnp.sum(weight, 0, keepdims=True)
@@ -410,13 +416,17 @@
     attended = attended.T.astype(BF16)
     query_grad = (dot_nn(key.T, dscore) * SCALE).T.astype(BF16)
     for r in range(4):
-        oqs[r][:128] = attended[128 * r : 128 * r + 128]
-        oqs[r][128:] = query_grad[128 * r : 128 * r + 128]
+        oqs[r][:128, cols] = attended[128 * r : 128 * r + 128]
+        oqs[r][128:, cols] = query_grad[128 * r : 128 * r + 128]
     at = row((512, 128))
     active = (lax.rem(at, 16) == o1) | (lax.rem(at, 64) == o2)
     zero = jnp.zeros((), BF16)
-    dk[0] = dot_nn(dscore, jnp.where(active, zero, query)) * SCALE
-    dv[0] = dot_nn(prob.astype(BF16), jnp.where(active, zero, grad))
+    dk[sub] = dot_nn(dscore, jnp.where(active, zero, query)) * SCALE
+    dv[sub] = dot_nn(prob.astype(BF16), jnp.where(active, zero, grad))
+
+
+def pair_block(rows, first):
+    return pl.BlockSpec((rows, 256), lambda h: (0, first // 2 + h))
 
 
 def head_block(rows, first):
@@ -437,13 +447,13 @@
     before = [meta, *kvs, *qgs, *last]
     return pl.pallas_call(
         functools.partial(main_kernel, first),
-        grid=(4,),
+        grid=(2,),
         out_shape=part_shapes(256) + [jax.ShapeDtypeStruct((4, 512, 128), F32)] * 2,
         in_specs=[SMEM]
-        + [head_block(256, first)] * 8
+        + [pair_block(256, first)] * 8
         + [ANY] * (len(last) + len(held)),
-        out_specs=part_specs(256, first)
-        + [pl.BlockSpec((1, 512, 128), lambda h: (h, 0, 0))] * 2,
+        out_specs=[pair_block(256, first)] * 2 + [pair_block(256, 0)] * 2
+        + [pl.BlockSpec((2, 512, 128), lambda h: (h, 0, 0))] * 2,
         input_output_aliases={len(before) + i: i for i in range(len(held))},
         compiler_params=params(),
         cost_estimate=COST,
@@ -455,13 +465,19 @@
     act, back, dk0, dv0 = refs[:4]
     kvs = refs[4:8]
     dkvs, oas, full = refs[-9:-5], refs[-5:-1], refs[-1]
-    o1, o2 = head_offsets(meta, 0, first + pl.program_id(0))
+    for sub in range(2):
+        late_head(first + 2 * pl.program_id(0) + sub, sub, meta, act, back, dk0, dv0, kvs, dkvs, oas, full.at[sub])
+
+
+def late_head(head, sub, meta, act, back, dk0, dv0, kvs, dkvs, oas, full):
+    o1, o2 = head_offsets(meta, 0, head)
+    at = pl.ds(128 * sub, 128)
     lap = lax.rem(o2, 16) == o1
     shift = lax.div(o2, 16)
-    key = jnp.concatenate([kv[:128] for kv in kvs], 0)
-    value = jnp.concatenate([kv[128:] for kv in kvs], 0)
-    query, grad = act[2], act[3]
-    ret = back[0].astype(F32)
+    key = jnp.concatenate([kv[:128, at] for kv in kvs], 0)
+    value = jnp.concatenate([kv[128:, at] for kv in kvs], 0)
+    query, grad = act[2, :, at], act[3, :, at]
+    ret = back[sub].astype(F32)
     lse, delta = decode_stats(ret[160:200])
     prob = jnp.exp(dot_nt(query, key) * SCALE - lse)
     dscore = (prob * (dot_nt(grad, value) - delta)).astype(BF16)
@@ -474,7 +490,7 @@
     o_top = o_act[32:] + ret[128:136] + dot_nn(up, ret[0:32].astype(BF16))
     q_top = q_act[32:] + ret[136:144] + dot_nn(up, ret[32:64].astype(BF16))
     for r in range(4):
-        oas[r][...] = jnp.concatenate(
+        oas[r][:, at] = jnp.concatenate(
             [o_mid[8 * r : 8 * r + 8], q_mid[8 * r : 8 * r + 8], o_top, q_top], 0
         ).astype(BF16)
     twice = (row((40, 128)) >= 32) & lap
@@ -482,13 +498,13 @@
         ((dk0, dscore, query, 64, 144, SCALE), (dv0, prob, grad, 96, 152, 1.0))
     ):
         rows = jnp.where(twice, 0.0, rows.astype(F32)).astype(BF16)
-        full[...] = start[0] + dot_tn(weights, rows) * scale
+        full[...] = start[sub] + dot_tn(weights, rows) * scale
         at_mid = pl.ds(o1, 32, stride=16)
         full[at_mid, :] = full[at_mid, :] + ret[mid_at : mid_at + 32]
         at_top = pl.ds(o2, 8, stride=64)
         full[at_top, :] = full[at_top, :] + ret[top_at : top_at + 8]
         for r in range(4):
-            dkvs[r][half * 128 : half * 128 + 128] = full[128 * r : 128 * r + 128].astype(BF16)
+            dkvs[r][half * 128 : half * 128 + 128, at] = full[128 * r : 128 * r + 128].astype(BF16)
 
 
 def late(meta, act, back, dk0, dv0, kvs, first, held, last):
@@ -496,19 +512,19 @@
     places = (0, 1, 4, 5, 6, 7)[: len(held)]
     return pl.pallas_call(
         functools.partial(late_kernel, first),
-        grid=(4,),
+        grid=(2,),
         out_shape=part_shapes(256) + [jax.ShapeDtypeStruct((32, 1024), BF16)] * 4,
         in_specs=[
             SMEM,
-            pl.BlockSpec((4, 40, 128), lambda h: (0, 0, first + h)),
-            pl.BlockSpec((1, 200, 128), lambda h: (first + h, 0, 0)),
-            pl.BlockSpec((1, 512, 128), lambda h: (h, 0, 0)),
-            pl.BlockSpec((1, 512, 128), lambda h: (h, 0, 0)),
+            pl.BlockSpec((4, 40, 256), lambda h: (0, 0, first // 2 + h)),
+            pl.BlockSpec((2, 200, 128), lambda h: (first // 2 + h, 0, 0)),
+            pl.BlockSpec((2, 512, 128), lambda h: (h, 0, 0)),
+            pl.BlockSpec((2, 512, 128), lambda h: (h, 0, 0)),
         ]
-        + [head_block(256, first)] * 4
+        + [pair_block(256, first)] * 4
         + [ANY] * (len(last) + len(held)),
-        out_specs=part_specs(256, first) + [head_block(32, first)] * 4,
-        scratch_shapes=[pltpu.VMEM((512, 128), F32)],
+        out_specs=[pair_block(256, first)] * 2 + [pair_block(256, 0)] * 2 + [pair_block(32, first)] * 4,
+        scratch_shapes=[pltpu.VMEM((2, 512, 128), F32)],
         input_output_aliases={len(before) + i: at for i, at in enumerate(places)},
         compiler_params=params(),
         cost_estimate=COST,
@@ -618,20 +634,20 @@
     mid, top, far = fan(unit_exchange(sent, units))
     oth = send(mid[:2], ZL_ROUTE)
     topz = unit_exchange(far, levels)
-    st = unit_exchange(stats(act, kvs, [oth, topz]), units)
+    st = unit_exchange(stats(act, kvs, [topz]), units)
     out_mid, out_top, mid_oth, top_far = unit(meta, (mid, top, oth, topz, st), [qgs[2]])
     near = send(mid_oth, ZL_ROUTE)
     tops = unit_exchange(top_far, levels)
     first = main(meta, kvs, qgs, 0, [], [top_far])
-    second = main(meta, kvs, qgs, 4, first[:2], [])
+    sums = combine((out_mid, out_top, near, tops), [first[4]])
+    back = unit_exchange(sums, units)
+    second = main(meta, kvs, qgs, 4, first[:2], [sums])
     oqs = [second[0], go(second[1], 1)]
     oqs += [go(first[2], 2), go(first[3], 3), go(second[2], 2), go(second[3], 3)]
-    sums = combine((out_mid, out_top, near, tops), [second[4], oqs[2], oqs[3]])
-    back = unit_exchange(sums, units)
-    early = late(meta, act, back, first[4], first[5], kvs, 0, [], [oqs[4]])
+    early = late(meta, act, back, first[4], first[5], kvs, 0, [], [second[4], oqs[2], oqs[3]])
     dkv2, dkv3 = send(early[2], routes[2]), send(early[3], routes[3])
     held = [early[0], early[1], *early[4:]]
-    final = late(meta, act, back, second[4], second[5], kvs, 4, held, [oqs[5]])
+    final = late(meta, act, back, second[4], second[5], kvs, 4, held, [oqs[4]])
     oas = spread(final[4:])
     dkvs = [final[0], go(final[1], 1), dkv2, dkv3, go(final[2], 2), go(final[3], 3)]
     attended, query_grad = finish_oq(meta, oqs, oas, [dkv2])

time: 168 us -> 160 us (0.952)
  waiting for transfers between devices: 51.9 us -> 40.5 us
  starting transfers between devices: 54 us -> 59.5 us
    ppermute x27, waiting for transfers between devices: 39.7 us -> 26.4 us  [send(): return lax.ppermute(value, AXES, where)]
    ppermute x27, starting transfers between devices: 26.7 us -> 29.6 us  [send(): return lax.ppermute(value, AXES, where)]
    all_to_all x5, starting transfers between devices: 27.4 us -> 29.9 us  [unit_exchange(): lax.all_to_all(flat, AXES, 0, 0, tiled=True, axis_index_groups=groups)]
    all_to_all x5, waiting for transfers between devices: 12.2 us -> 14.1 us  [unit_exchange(): lax.all_to_all(flat, AXES, 0, 0, tiled=True, axis_index_groups=groups)]
  transfers between devices with their start and end apart: 32 -> 32, of which waited for: 15 -> 15; matrix products, arithmetic and copies ran while one was open for 0% -> 1% of each run, Pallas kernels for 22% -> 22%
where the time goes in v3:
time: 160 us; the launch traced here: 159 us
  starting transfers between devices  59.5 us (37%)
  Pallas kernels  48.1 us (30%)
  waiting for transfers between devices  40.5 us (25%)
  local copies, waits for them, and re-layouts  9.85 us (6%)
    all_to_all x5, starting transfers between devices, unit_exchange(): lax.all_to_all(flat, AXES, 0, 0, tiled=True, axis_index_groups=groups)  29.9 us
    ppermute x27, starting transfers between devices, send(): return lax.ppermute(value, AXES, where)  29.6 us
    ppermute x27, waiting for transfers between devices, send(): return lax.ppermute(value, AXES, where)  26.4 us
    pallas_call x2, Pallas kernels, main(): pl.pallas_call(functools.partial(main_kernel, first), grid=(2,), out_shap...  14.2 us
    all_to_all x5, waiting for transfers between devices, unit_exchange(): lax.all_to_all(flat, AXES, 0, 0, tiled=True, axis_index_groups=groups)  14.1 us
    pallas_call x2, Pallas kernels, late(): pl.pallas_call(functools.partial(late_kernel, first), grid=(2,), out_shap...  8.44 us
    unnamed x74, local copies, waits for them, and re-layouts  8.24 us
    pallas_call x1, Pallas kernels, open_blocks(): pl.pallas_call(open_kernel, out_shape=[jax.ShapeDtypeStruct((40, 1024), B...  5.38 us
  transfers between devices with their start and end apart: 32, of which 15 were waited for; matrix products, arithmetic and copies ran while one was open for 1% of the time, Pallas kernels for 22%

profile of v3, /device:TPU:1, one launch (start us, length us, event | category | flops | bytes accessed | tf_op | source)
XLA Modules:
  0.0 158.9 jit_solution(16243725215857832354)
XLA Ops:
  0.6 3.3 %collective-permute-start = (s32[2,8]{1,0:T(2,128)}, s32[2,8]{1,0:T(2,128)S(1)}, u32[]{:S(2)}, u32[]{:S(2)}) collective-permute-start(s32[2,8]{1,0:T(2,128)} %param.9), channel_id=1, source_target_pairs={{0,1},{1,0},{2,3},{3,2},{4,5},{5,4},{6,7},{7,6},{8,9},{9,8},{10,11... | collective-permute-start | bytes 200 | tf_op jit(solution)/shard_map/ppermute | solution.py:46
  4.0 1.7 %collective-permute-start.2 = (s32[2,8]{1,0:T(2,128)}, s32[2,8]{1,0:T(2,128)S(1)}, u32[]{:S(2)}, u32[]{:S(2)}) collective-permute-start(s32[2,8]{1,0:T(2,128)} %param.9), channel_id=1, source_target_pairs={{0,3},{1,2},{2,1},{3,0},{4,7},{5,6},{6,5},{7,4},{8,11},{9,10},{10,... | collective-permute-start | bytes 200 | tf_op jit(solution)/shard_map/ppermute | solution.py:46
  8.2 5.4 %open.1 = (bf16[40,1024]{1,0:T(8,128)(2,1)}, bf16[40,1024]{1,0:T(8,128)(2,1)}, bf16[40,1024]{1,0:T(8,128)(2,1)}, bf16[40,1024]{1,0:T(8,128)(2,1)}, bf16[256,1024...) custom-call(s32[67]{0:T(128)} %concatenate.3.meta, ...), custom_call_target="tpu_custom_call" | custom-call | bytes 1024 | tf_op jit(solution)/shard_map/open/pallas_call | solution.py:124
  15.8 2.5 %collective-permute-done.4.a2 = bf16[40,1024]{1,0:T(8,128)(2,1)S(1)} collective-permute-done((bf16[40,1024]{1,0:T(8,128)(2,1)}, bf16[40,1024]{1,0:T(8,128)(2,1)S(1)}, u32[]{:S(2)}, u32[]{:S(2)}) %collective-permute-start.4) | collective-permute-done | bytes 81952 | tf_op jit(solution)/shard_map/ppermute | solution.py:46
  18.3 1.9 %collective-permute-done.5.a3 = bf16[40,1024]{1,0:T(8,128)(2,1)S(1)} collective-permute-done((bf16[40,1024]{1,0:T(8,128)(2,1)}, bf16[40,1024]{1,0:T(8,128)(2,1)S(1)}, u32[]{:S(2)}, u32[]{:S(2)}) %collective-permute-start.5) | collective-permute-done | bytes 81952 | tf_op jit(solution)/shard_map/ppermute | solution.py:46
  20.9 1.9 %arrange.1 = (bf16[4,40,1024]{2,1,0:T(8,128)(2,1)}, bf16[8,160,128]{2,1,0:T(8,128)(2,1)}, bf16[256,1024]{1,0:T(8,128)(2,1)}, bf16[256,1024]{1,0:T(8,128)(2,1)}, bf16[256,1024]{1,0:T(8,128)(2,1)}) custom-call(bf16[40,1024]{1,0:T(8,128)(2,1)} %get-tuple-element.61.a0, ...), custom_call_target="tpu_custom_call", output_to_operand_aliasing={{2}: (4, {}), {3}: (5, {}), {4}: (6, {})} | custom-call | bytes 1024 | tf_op jit(solution)/shard_map/arrange/pallas_call | solution.py:163
  22.8 4.9 %all-to-all-start = ((bf16[8,160,128]{2,1,0:T(8,128)(2,1)}), bf16[8,160,128]{2,1,0:T(8,128)(2,1)S(1)}, u32[]{:S(2)}, u32[]{:S(2)}) async-start(bf16[8,160,128]{2,1,0:T(8,128)(2,1)} %get-tuple-element.75), calls=%async_computation | async-start | bytes 655360 | tf_op jit(solution)/shard_map/all_to_all | solution.py:58
  30.3 5.1 %all-to-all-done.got = bf16[8,160,128]{2,1,0:T(8,128)(2,1)S(1)} async-done(((bf16[8,160,128]{2,1,0:T(8,128)(2,1)}), bf16[8,160,128]{2,1,0:T(8,128)(2,1)S(1)}, u32[]{:S(2)}, u32[]{:S(2)}) %all-to-all-start) | async-done | bytes 327712 | tf_op jit(solution)/shard_map/all_to_all | solution.py:58
  36.2 1.9 %fan.1 = (bf16[4,256,128]{2,1,0:T(8,128)(2,1)}, bf16[4,64,128]{2,1,0:T(8,128)(2,1)}, bf16[8,128,128]{2,1,0:T(8,128)(2,1)}) custom-call(bf16[8,160,128]{2,1,0:T(8,128)(2,1)} %copy-done.8), custom_call_target="tpu_custom_call" | custom-call | bytes 1024 | tf_op jit(solution)/shard_map/fan/pallas_call | solution.py:194
  38.1 8.3 %all-to-all-start.1 = ((bf16[8,128,128]{2,1,0:T(8,128)(2,1)}), bf16[8,128,128]{2,1,0:T(8,128)(2,1)S(1)}, u32[]{:S(2)}, u32[]{:S(2)}) async-start(bf16[8,128,128]{2,1,0:T(8,128)(2,1)} %get-tuple-element.78), calls=%async_computation.1 | async-start | bytes 524288 | tf_op jit(solution)/shard_map/all_to_all | solution.py:58
  48.5 2.0 %collective-permute-start.11 = (bf16[256,1024]{1,0:T(8,128)(2,1)}, bf16[256,1024]{1,0:T(8,128)(2,1)S(1)}, u32[]{:S(2)}, u32[]{:S(2)}) collective-permute-start(bf16[256,1024]{1,0:T(8,128)(2,1)} %get-tuple-element.74), channel_id=1, source_target_pairs={{0,3},{1,2},{2,1},{3,0},{4,7},{5,6},{6,5},{7,4},{8,11},{9,10},{10,... | collective-permute-start | bytes 1572872 | tf_op jit(solution)/shard_map/ppermute | solution.py:46
  51.6 2.2 %collective-permute-done.8.refs_3_.refs_7_ = bf16[256,1024]{1,0:T(8,128)(2,1)S(1)} collective-permute-done((bf16[256,1024]{1,0:T(8,128)(2,1)}, bf16[256,1024]{1,0:T(8,128)(2,1)S(1)}, u32[]{:S(2)}, u32[]{:S(2)}) %collective-permute-start.8) | collective-permute-done | bytes 524320 | tf_op jit(solution)/shard_map/ppermute | solution.py:46
  53.8 2.0 %all-to-all-done.1.refs_4_.topz = bf16[8,128,128]{2,1,0:T(8,128)(2,1)S(1)} async-done(((bf16[8,128,128]{2,1,0:T(8,128)(2,1)}), bf16[8,128,128]{2,1,0:T(8,128)(2,1)S(1)}, u32[]{:S(2)}, u32[]{:S(2)}) %all-to-all-start.1) | async-done | bytes 262176 | tf_op jit(solution)/shard_map/all_to_all | solution.py:58
  56.5 3.7 %stats.1 = f32[8,8,128]{2,1,0:T(8,128)} custom-call(bf16[4,40,1024]{2,1,0:T(8,128)(2,1)} %get-tuple-element.79.act.refs_0_, bf16[256,1024]{1,0:T(8,128)(2,1)} %get-tuple-element.60.refs_0_.refs_4_, bf16[256,1024]{1,0:T(8,128)(2,1)} %copy-done, bf16[256,1024]{1,0:T(8,128)(2,1)} %copy-done.1, bf16[256,1024]{1,0:T(8,128)(2,1)} %copy-done.2, ...), custom_call_target="tpu_custom_call" | custom-call | bytes 1024 | tf_op jit(solution)/shard_map/stats/pallas_call | solution.py:241
  60.2 5.7 %all-to-all-start.2 = ((f32[8,8,128]{2,1,0:T(8,128)}), f32[8,8,128]{2,1,0:T(8,128)S(1)}, u32[]{:S(2)}, u32[]{:S(2)}) async-start(f32[8,8,128]{2,1,0:T(8,128)} %stats.1), calls=%async_computation.2 | async-start | bytes 65536 | tf_op jit(solution)/shard_map/all_to_all | solution.py:58
  66.0 6.3 %all-to-all-done.2.st = f32[8,8,128]{2,1,0:T(8,128)S(1)} async-done(((f32[8,8,128]{2,1,0:T(8,128)}), f32[8,8,128]{2,1,0:T(8,128)S(1)}, u32[]{:S(2)}, u32[]{:S(2)}) %all-to-all-start.2) | async-done | bytes 32800 | tf_op jit(solution)/shard_map/all_to_all | solution.py:58
  72.9 3.6 %unit.1 = (bf16[5,256,128]{2,1,0:T(8,128)(2,1)}, bf16[3,64,128]{2,1,0:T(8,128)(2,1)}, bf16[2,256,128]{2,1,0:T(8,128)(2,1)}, bf16[8,128,128]{2,1,0:T(8,128)(2,1)}) custom-call(s32[67]{0:T(128)} %concatenate.3.meta, bf16[4,256,128]{2,1,0:T(8,128)(2,1)} %get-tuple-element.76.mid, bf16[4,64,128]{2,1,0:T(8,128)(2,1)} %get-tuple-element.77.top, ...), custom_call_target="tpu_custom_call" | custom-call | bytes 1024 | tf_op jit(solution)/shard_map/unit/pallas_call | solution.py:352
  76.5 7.3 %all-to-all-start.3 = ((bf16[8,128,128]{2,1,0:T(8,128)(2,1)}), bf16[8,128,128]{2,1,0:T(8,128)(2,1)S(1)}, u32[]{:S(2)}, u32[]{:S(2)}) async-start(bf16[8,128,128]{2,1,0:T(8,128)(2,1)} %get-tuple-element.83.refs_8_), calls=%async_computation.3 | async-start | bytes 524288 | tf_op jit(solution)/shard_map/all_to_all | solution.py:58
  83.8 1.5 collective-permute-start.13
  86.2 7.1 %main.2 = (bf16[256,1024]{1,0:T(8,128)(2,1)}, bf16[256,1024]{1,0:T(8,128)(2,1)}, bf16[256,512]{1,0:T(8,128)(2,1)}, bf16[256,512]{1,0:T(8,128)(2,1)}, f32[4,512,128]{2,1,0:T(8,128)}, /*index=5*/f32[4,512,128]{2,1,0:T(8,128)}) custom-call(s32[67]{0:T(128)} %concatenate.3.meta, bf16[256,1024]{1,0:T(8,128)(2,1)} %get-tuple-element.60.refs_0_.refs_4_, ...), custom_call_target="tpu_custom_call" | custom-call | bytes 1024 | tf_op jit(solution)/shard_map/main/pallas_call | solution.py:448
  94.7 1.9 %combine.1.refs_8_ = bf16[8,200,128]{2,1,0:T(8,128)(2,1)} custom-call(bf16[5,256,128]{2,1,0:T(8,128)(2,1)} %get-tuple-element.80.out_mid, bf16[3,64,128]{2,1,0:T(8,128)(2,1)} %get-tuple-element.81.out_top, bf16[2,256,128]{2,1,0:T(8,128)(2,1)} %copy-done.23, bf16[8,128,128]{2,1,0:T(8,128)(2,1)} %copy-done.9, f32[4,512,128]{2,1,0:T(8,128)} %get-tuple-element.84.refs_0_.refs_2_), custom_call_target="tpu_custom_call" | custom-call | bytes 1024 | tf_op jit(solution)/shard_map/combine/pallas_call | solution.py:384
  96.7 3.6 %all-to-all-start.4 = ((bf16[8,200,128]{2,1,0:T(8,128)(2,1)}), bf16[8,200,128]{2,1,0:T(8,128)(2,1)S(1)}, u32[]{:S(2)}, u32[]{:S(2)}) async-start(bf16[8,200,128]{2,1,0:T(8,128)(2,1)} %combine.1.refs_8_), calls=%async_computation.4 | async-start | bytes 819200 | tf_op jit(solution)/shard_map/all_to_all | solution.py:58
  100.4 5.1 %collective-permute-start.16 = (bf16[256,512]{1,0:T(8,128)(2,1)S(1)}, bf16[256,512]{1,0:T(8,128)(2,1)S(1)}, u32[]{:S(2)}, u32[]{:S(2)}) collective-permute-start(bf16[256,512]{1,0:T(8,128)(2,1)S(1)} %copy-done.33), channel_id=1, source_target_pairs={{0,3},{1,2},{2,1},{3,0},{4,7},{5,6},{6,5},{7,4},{8,11},{9,10},{10,... | collective-permute-start | bytes 786440 | tf_op jit(solution)/shard_map/ppermute | solution.py:46
  105.5 7.1 %main.3 = (bf16[256,1024]{1,0:T(8,128)(2,1)}, bf16[256,1024]{1,0:T(8,128)(2,1)}, bf16[256,512]{1,0:T(8,128)(2,1)}, bf16[256,512]{1,0:T(8,128)(2,1)}, f32[4,512,128]{2,1,0:T(8,128)}, /*index=5*/f32[4,512,128]{2,1,0:T(8,128)}) custom-call(s32[67]{0:T(128)} %concatenate.3.meta, ...), custom_call_target="tpu_custom_call", output_to_operand_aliasing={{0}: (10, {}), {1}: (11, {})} | custom-call | bytes 1024 | tf_op jit(solution)/shard_map/main/pallas_call | solution.py:448
  113.1 1.5 collective-permute-start.18
  115.6 4.2 %late.2 = (bf16[256,1024]{1,0:T(8,128)(2,1)}, bf16[256,1024]{1,0:T(8,128)(2,1)}, bf16[256,512]{1,0:T(8,128)(2,1)}, bf16[256,512]{1,0:T(8,128)(2,1)}, bf16[32,102...) custom-call(s32[67]{0:T(128)} %concatenate.3.meta, ...), custom_call_target="tpu_custom_call" | custom-call | bytes 1024 | tf_op jit(solution)/shard_map/late/pallas_call | solution.py:513
  121.7 4.2 %late.3 = (bf16[256,1024]{1,0:T(8,128)(2,1)}, bf16[256,1024]{1,0:T(8,128)(2,1)}, bf16[256,512]{1,0:T(8,128)(2,1)}, bf16[256,512]{1,0:T(8,128)(2,1)}, bf16[32,102...) custom-call(s32[67]{0:T(128)} %concatenate.3.meta, ...), custom_call_target="tpu_custom_call", output_to_operand_aliasing={{0}: (10, {}), {1}: (11, {}), {4}: (12, {}), {5}: (13, {}),... | custom-call | bytes 1024 | tf_op jit(solution)/shard_map/late/pallas_call | solution.py:513
  134.1 9.2 %collective-permute-done.22.refs_10_.refs_2_ = bf16[256,512]{1,0:T(8,128)(2,1)S(1)} collective-permute-done((bf16[256,512]{1,0:T(8,128)(2,1)S(1)}, bf16[256,512]{1,0:T(8,128)(2,1)S(1)}, u32[]{:S(2)}, u32[]{:S(2)}) %collective-permute-start.22) | collective-permute-done | bytes 262176 | tf_op jit(solution)/shard_map/ppermute | solution.py:46
  144.0 3.7 %finish_oq.1 = (bf16[128,4096]{1,0:T(8,128)(2,1)}, bf16[128,4096]{1,0:T(8,128)(2,1)}) custom-call(s32[67]{0:T(128)} %concatenate.3.meta, bf16[256,1024]{1,0:T(8,128)(2,1)} %get-tuple-element.87.refs_0_, bf16[256,1024]{1,0:T(8,128)(2,1)} %copy-done.16, bf16[256,512]{1,0:T(8,128)(2,1)} %copy-done.10, bf16[256,512]{1,0:T(8,128)(2,1)} %copy-done.11, ...), custom_call_target="tpu_custom_call" | custom-call | bytes 1024 | tf_op jit(solution)/shard_map/finish_oq/pallas_call | solution.py:561
  147.8 1.6 %collective-permute-done.26.refs_5_ = bf16[256,512]{1,0:T(8,128)(2,1)S(1)} collective-permute-done((bf16[256,512]{1,0:T(8,128)(2,1)}, bf16[256,512]{1,0:T(8,128)(2,1)S(1)}, u32[]{:S(2)}, u32[]{:S(2)}) %collective-permute-start.26) | collective-permute-done | bytes 262176 | tf_op jit(solution)/shard_map/ppermute | solution.py:46
  149.4 5.1 %collective-permute-done.24.refs_3_ = bf16[256,512]{1,0:T(8,128)(2,1)S(1)} collective-permute-done((bf16[256,512]{1,0:T(8,128)(2,1)S(1)}, bf16[256,512]{1,0:T(8,128)(2,1)S(1)}, u32[]{:S(2)}, u32[]{:S(2)}) %collective-permute-start.24) | collective-permute-done | bytes 262176 | tf_op jit(solution)/shard_map/ppermute | solution.py:46
  155.5 3.3 %finish_kv.1 = (bf16[128,4096]{1,0:T(8,128)(2,1)}, bf16[128,4096]{1,0:T(8,128)(2,1)}) custom-call(s32[67]{0:T(128)} %concatenate.3.meta, bf16[256,1024]{1,0:T(8,128)(2,1)} %get-tuple-element.109.refs_0_, bf16[256,1024]{1,0:T(8,128)(2,1)} %copy-done.15, bf16[256,512]{1,0:T(8,128)(2,1)} %copy-done.13, bf16[256,512]{1,0:T(8,128)(2,1)} %copy-done.20, ...), custom_call_target="tpu_custom_call" | custom-call | bytes 1024 | tf_op jit(solution)/shard_map/finish_kv/pallas_call | solution.py:599
  (124 shorter events, 28.9 us)
Async XLA Ops:
  0.6 5.9 %collective-permute-start = (s32[2,8]{1,0:T(2,128)}, s32[2,8]{1,0:T(2,128)S(1)}, u32[]{:S(2)}, u32[]{:S(2)}) collective-permute-start(s32[2,8]{1,0:T(2,128)} %param.9), channel_id=1, source_target_pairs={{0,1},{1,0},{2,3},{3,2},{4,5},{5,4},{6,7},{7,6},{8,9},{9,8},{10,11... | collective-permute-start | bytes 200 | tf_op jit(solution)/shard_map/ppermute | solution.py:46
  4.0 2.6 %collective-permute-start.1 = (s32[2,8]{1,0:T(2,128)}, s32[2,8]{1,0:T(2,128)S(1)}, u32[]{:S(2)}, u32[]{:S(2)}) collective-permute-start(s32[2,8]{1,0:T(2,128)} %param.9), channel_id=1, source_target_pairs={{0,2},{1,3},{2,0},{3,1},{4,6},{5,7},{6,4},{7,5},{8,10},{9,11},{10,... | collective-permute-start | bytes 200 | tf_op jit(solution)/shard_map/ppermute | solution.py:46
  4.0 3.5 %collective-permute-start.2 = (s32[2,8]{1,0:T(2,128)}, s32[2,8]{1,0:T(2,128)S(1)}, u32[]{:S(2)}, u32[]{:S(2)}) collective-permute-start(s32[2,8]{1,0:T(2,128)} %param.9), channel_id=1, source_target_pairs={{0,3},{1,2},{2,1},{3,0},{4,7},{5,6},{6,5},{7,4},{8,11},{9,10},{10,... | collective-permute-start | bytes 200 | tf_op jit(solution)/shard_map/ppermute | solution.py:46
  13.5 2.3 %collective-permute-start.3 = (bf16[40,1024]{1,0:T(8,128)(2,1)}, bf16[40,1024]{1,0:T(8,128)(2,1)S(1)}, u32[]{:S(2)}, u32[]{:S(2)}) collective-permute-start(bf16[40,1024]{1,0:T(8,128)(2,1)} %get-tuple-element.62), channel_id=1, source_target_pairs={{0,1},{1,0},{2,3},{3,2},{4,5},{5,4},{6,7},{7,6},{8,9},{9,8},{10,11... | collective-permute-start | bytes 245768 | tf_op jit(solution)/shard_map/ppermute | solution.py:46
  14.1 4.2 %collective-permute-start.4 = (bf16[40,1024]{1,0:T(8,128)(2,1)}, bf16[40,1024]{1,0:T(8,128)(2,1)S(1)}, u32[]{:S(2)}, u32[]{:S(2)}) collective-permute-start(bf16[40,1024]{1,0:T(8,128)(2,1)} %get-tuple-element.63), channel_id=1, source_target_pairs={{0,2},{1,3},{2,0},{3,1},{4,6},{5,7},{6,4},{7,5},{8,10},{9,11},{10,... | collective-permute-start | bytes 245768 | tf_op jit(solution)/shard_map/ppermute | solution.py:46
  15.2 5.1 %collective-permute-start.5 = (bf16[40,1024]{1,0:T(8,128)(2,1)}, bf16[40,1024]{1,0:T(8,128)(2,1)S(1)}, u32[]{:S(2)}, u32[]{:S(2)}) collective-permute-start(bf16[40,1024]{1,0:T(8,128)(2,1)} %get-tuple-element.64), channel_id=1, source_target_pairs={{0,3},{1,2},{2,1},{3,0},{4,7},{5,6},{6,5},{7,4},{8,11},{9,10},{10,... | collective-permute-start | bytes 245768 | tf_op jit(solution)/shard_map/ppermute | solution.py:46
  22.8 12.6 %all-to-all-start = ((bf16[8,160,128]{2,1,0:T(8,128)(2,1)}), bf16[8,160,128]{2,1,0:T(8,128)(2,1)S(1)}, u32[]{:S(2)}, u32[]{:S(2)}) async-start(bf16[8,160,128]{2,1,0:T(8,128)(2,1)} %get-tuple-element.75), calls=%async_computation | async-start | bytes 655360 | tf_op jit(solution)/shard_map/all_to_all | solution.py:58
  27.7 20.8 %collective-permute-start.6 = (bf16[256,1024]{1,0:T(8,128)(2,1)S(1)}, bf16[256,1024]{1,0:T(8,128)(2,1)S(1)}, u32[]{:S(2)}, u32[]{:S(2)}) collective-permute-start(bf16[256,1024]{1,0:T(8,128)(2,1)S(1)} %copy-done.17), channel_id=1, source_target_pairs={{0,1},{1,0},{2,3},{3,2},{4,5},{5,4},{6,7},{7,6},{8,9},{9,8},{10,11... | collective-permute-start | bytes 1572872 | tf_op jit(solution)/shard_map/ppermute | solution.py:46
  28.3 22.2 %collective-permute-start.7 = (bf16[256,1024]{1,0:T(8,128)(2,1)}, bf16[256,1024]{1,0:T(8,128)(2,1)S(1)}, u32[]{:S(2)}, u32[]{:S(2)}) collective-permute-start(bf16[256,1024]{1,0:T(8,128)(2,1)} %get-tuple-element.69), channel_id=1, source_target_pairs={{0,2},{1,3},{2,0},{3,1},{4,6},{5,7},{6,4},{7,5},{8,10},{9,11},{10,... | collective-permute-start | bytes 1572872 | tf_op jit(solution)/shard_map/ppermute | solution.py:46
  28.6 25.3 %collective-permute-start.8 = (bf16[256,1024]{1,0:T(8,128)(2,1)}, bf16[256,1024]{1,0:T(8,128)(2,1)S(1)}, u32[]{:S(2)}, u32[]{:S(2)}) collective-permute-start(bf16[256,1024]{1,0:T(8,128)(2,1)} %get-tuple-element.70), channel_id=1, source_target_pairs={{0,3},{1,2},{2,1},{3,0},{4,7},{5,6},{6,5},{7,4},{8,11},{9,10},{10,... | collective-permute-start | bytes 1572872 | tf_op jit(solution)/shard_map/ppermute | solution.py:46
  30.0 36.0 %collective-permute-start.10 = (bf16[256,1024]{1,0:T(8,128)(2,1)}, bf16[256,1024]{1,0:T(8,128)(2,1)S(1)}, u32[]{:S(2)}, u32[]{:S(2)}) collective-permute-start(bf16[256,1024]{1,0:T(8,128)(2,1)} %get-tuple-element.73), channel_id=1, source_target_pairs={{0,2},{1,3},{2,0},{3,1},{4,6},{5,7},{6,4},{7,5},{8,10},{9,11},{10,... | collective-permute-start | bytes 1572872 | tf_op jit(solution)/shard_map/ppermute | solution.py:46
  38.1 17.8 %all-to-all-start.1 = ((bf16[8,128,128]{2,1,0:T(8,128)(2,1)}), bf16[8,128,128]{2,1,0:T(8,128)(2,1)S(1)}, u32[]{:S(2)}, u32[]{:S(2)}) async-start(bf16[8,128,128]{2,1,0:T(8,128)(2,1)} %get-tuple-element.78), calls=%async_computation.1 | async-start | bytes 524288 | tf_op jit(solution)/shard_map/all_to_all | solution.py:58
  47.1 18.9 %collective-permute-start.12 = (bf16[2,256,128]{2,1,0:T(8,128)(2,1)}, bf16[2,256,128]{2,1,0:T(8,128)(2,1)S(1)}, u32[]{:S(2)}, u32[]{:S(2)}) collective-permute-start(bf16[2,256,128]{2,1,0:T(8,128)(2,1)} %slice.3), channel_id=1, source_target_pairs={{0,32},{1,33},{2,34},{3,35},{4,36},{5,37},{6,38},{7,39},{8,40},{9,... | collective-permute-start | bytes 393224 | tf_op jit(solution)/shard_map/ppermute | solution.py:46
  48.5 36.7 %collective-permute-start.11 = (bf16[256,1024]{1,0:T(8,128)(2,1)}, bf16[256,1024]{1,0:T(8,128)(2,1)S(1)}, u32[]{:S(2)}, u32[]{:S(2)}) collective-permute-start(bf16[256,1024]{1,0:T(8,128)(2,1)} %get-tuple-element.74), channel_id=1, source_target_pairs={{0,3},{1,2},{2,1},{3,0},{4,7},{5,6},{6,5},{7,4},{8,11},{9,10},{10,... | collective-permute-start | bytes 1572872 | tf_op jit(solution)/shard_map/ppermute | solution.py:46
  50.5 34.7 %collective-permute-start.9 = (bf16[256,1024]{1,0:T(8,128)(2,1)}, bf16[256,1024]{1,0:T(8,128)(2,1)S(1)}, u32[]{:S(2)}, u32[]{:S(2)}) collective-permute-start(bf16[256,1024]{1,0:T(8,128)(2,1)} %get-tuple-element.72), channel_id=1, source_target_pairs={{0,1},{1,0},{2,3},{3,2},{4,5},{5,4},{6,7},{7,6},{8,9},{9,8},{10,11... | collective-permute-start | bytes 1572872 | tf_op jit(solution)/shard_map/ppermute | solution.py:46
  60.2 12.1 %all-to-all-start.2 = ((f32[8,8,128]{2,1,0:T(8,128)}), f32[8,8,128]{2,1,0:T(8,128)S(1)}, u32[]{:S(2)}, u32[]{:S(2)}) async-start(f32[8,8,128]{2,1,0:T(8,128)} %stats.1), calls=%async_computation.2 | async-start | bytes 65536 | tf_op jit(solution)/shard_map/all_to_all | solution.py:58
  76.5 17.6 %all-to-all-start.3 = ((bf16[8,128,128]{2,1,0:T(8,128)(2,1)}), bf16[8,128,128]{2,1,0:T(8,128)(2,1)S(1)}, u32[]{:S(2)}, u32[]{:S(2)}) async-start(bf16[8,128,128]{2,1,0:T(8,128)(2,1)} %get-tuple-element.83.refs_8_), calls=%async_computation.3 | async-start | bytes 524288 | tf_op jit(solution)/shard_map/all_to_all | solution.py:58
  83.8 9.6 %collective-permute-start.13 = (bf16[2,256,128]{2,1,0:T(8,128)(2,1)S(1)}, bf16[2,256,128]{2,1,0:T(8,128)(2,1)S(1)}, u32[]{:S(2)}, u32[]{:S(2)}) collective-permute-start(bf16[2,256,128]{2,1,0:T(8,128)(2,1)S(1)} %copy-done.35), channel_id=1, source_target_pairs={{0,32},{1,33},{2,34},{3,35},{4,36},{5,37},{6,38},{7,39},{8,40},{9,... | collective-permute-start | bytes 393224 | tf_op jit(solution)/shard_map/ppermute | solution.py:46
  96.7 18.0 %all-to-all-start.4 = ((bf16[8,200,128]{2,1,0:T(8,128)(2,1)}), bf16[8,200,128]{2,1,0:T(8,128)(2,1)S(1)}, u32[]{:S(2)}, u32[]{:S(2)}) async-start(bf16[8,200,128]{2,1,0:T(8,128)(2,1)} %combine.1.refs_8_), calls=%async_computation.4 | async-start | bytes 819200 | tf_op jit(solution)/shard_map/all_to_all | solution.py:58
  100.3 14.3 %collective-permute-start.15 = (bf16[256,512]{1,0:T(8,128)(2,1)S(1)}, bf16[256,512]{1,0:T(8,128)(2,1)S(1)}, u32[]{:S(2)}, u32[]{:S(2)}) collective-permute-start(bf16[256,512]{1,0:T(8,128)(2,1)S(1)} %copy-done.34), channel_id=1, source_target_pairs={{0,2},{1,3},{2,0},{3,1},{4,6},{5,7},{6,4},{7,5},{8,10},{9,11},{10,... | collective-permute-start | bytes 786440 | tf_op jit(solution)/shard_map/ppermute | solution.py:46
  100.4 14.3 %collective-permute-start.16 = (bf16[256,512]{1,0:T(8,128)(2,1)S(1)}, bf16[256,512]{1,0:T(8,128)(2,1)S(1)}, u32[]{:S(2)}, u32[]{:S(2)}) collective-permute-start(bf16[256,512]{1,0:T(8,128)(2,1)S(1)} %copy-done.33), channel_id=1, source_target_pairs={{0,3},{1,2},{2,1},{3,0},{4,7},{5,6},{6,5},{7,4},{8,11},{9,10},{10,... | collective-permute-start | bytes 786440 | tf_op jit(solution)/shard_map/ppermute | solution.py:46
  112.6 8.4 %collective-permute-start.17 = (bf16[256,512]{1,0:T(8,128)(2,1)}, bf16[256,512]{1,0:T(8,128)(2,1)S(1)}, u32[]{:S(2)}, u32[]{:S(2)}) collective-permute-start(bf16[256,512]{1,0:T(8,128)(2,1)} %get-tuple-element.91), channel_id=1, source_target_pairs={{0,2},{1,3},{2,0},{3,1},{4,6},{5,7},{6,4},{7,5},{8,10},{9,11},{10,... | collective-permute-start | bytes 786440 | tf_op jit(solution)/shard_map/ppermute | solution.py:46
  112.7 20.5 %collective-permute-start.14 = (bf16[256,1024]{1,0:T(8,128)(2,1)}, bf16[256,1024]{1,0:T(8,128)(2,1)S(1)}, u32[]{:S(2)}, u32[]{:S(2)}) collective-permute-start(bf16[256,1024]{1,0:T(8,128)(2,1)} %get-tuple-element.88), channel_id=1, source_target_pairs={{0,1},{1,0},{2,3},{3,2},{4,5},{5,4},{6,7},{7,6},{8,9},{9,8},{10,11... | collective-permute-start | bytes 1572872 | tf_op jit(solution)/shard_map/ppermute | solution.py:46
  113.1 14.4 %collective-permute-start.18 = (bf16[256,512]{1,0:T(8,128)(2,1)}, bf16[256,512]{1,0:T(8,128)(2,1)S(1)}, u32[]{:S(2)}, u32[]{:S(2)}) collective-permute-start(bf16[256,512]{1,0:T(8,128)(2,1)} %get-tuple-element.92), channel_id=1, source_target_pairs={{0,3},{1,2},{2,1},{3,0},{4,7},{5,6},{6,5},{7,4},{8,11},{9,10},{10,... | collective-permute-start | bytes 786440 | tf_op jit(solution)/shard_map/ppermute | solution.py:46
  125.9 28.6 %collective-permute-start.23 = (bf16[256,1024]{1,0:T(8,128)(2,1)}, bf16[256,1024]{1,0:T(8,128)(2,1)S(1)}, u32[]{:S(2)}, u32[]{:S(2)}) collective-permute-start(bf16[256,1024]{1,0:T(8,128)(2,1)} %get-tuple-element.110), channel_id=1, source_target_pairs={{0,1},{1,0},{2,3},{3,2},{4,5},{5,4},{6,7},{7,6},{8,9},{9,8},{10,11... | collective-permute-start | bytes 1572872 | tf_op jit(solution)/shard_map/ppermute | solution.py:46
  126.0 2.5 %collective-permute-start.19 = (bf16[32,1024]{1,0:T(8,128)(2,1)}, bf16[32,1024]{1,0:T(8,128)(2,1)S(1)}, u32[]{:S(2)}, u32[]{:S(2)}) collective-permute-start(bf16[32,1024]{1,0:T(8,128)(2,1)} %get-tuple-element.103), channel_id=1, source_target_pairs={{0,1},{1,0},{2,3},{3,2},{4,5},{5,4},{6,7},{7,6},{8,9},{9,8},{10,11... | collective-permute-start | bytes 196616 | tf_op jit(solution)/shard_map/ppermute | solution.py:46
  126.5 3.3 %collective-permute-start.20 = (bf16[32,1024]{1,0:T(8,128)(2,1)}, bf16[32,1024]{1,0:T(8,128)(2,1)S(1)}, u32[]{:S(2)}, u32[]{:S(2)}) collective-permute-start(bf16[32,1024]{1,0:T(8,128)(2,1)} %get-tuple-element.104), channel_id=1, source_target_pairs={{0,2},{1,3},{2,0},{3,1},{4,6},{5,7},{6,4},{7,5},{8,10},{9,11},{10,... | collective-permute-start | bytes 196616 | tf_op jit(solution)/shard_map/ppermute | solution.py:46
  127.5 4.8 %collective-permute-start.21 = (bf16[32,1024]{1,0:T(8,128)(2,1)}, bf16[32,1024]{1,0:T(8,128)(2,1)S(1)}, u32[]{:S(2)}, u32[]{:S(2)}) collective-permute-start(bf16[32,1024]{1,0:T(8,128)(2,1)} %get-tuple-element.105), channel_id=1, source_target_pairs={{0,3},{1,2},{2,1},{3,0},{4,7},{5,6},{6,5},{7,4},{8,11},{9,10},{10,... | collective-permute-start | bytes 196616 | tf_op jit(solution)/shard_map/ppermute | solution.py:46
  128.5 19.3 %collective-permute-start.25 = (bf16[256,512]{1,0:T(8,128)(2,1)}, bf16[256,512]{1,0:T(8,128)(2,1)S(1)}, u32[]{:S(2)}, u32[]{:S(2)}) collective-permute-start(bf16[256,512]{1,0:T(8,128)(2,1)} %get-tuple-element.112), channel_id=1, source_target_pairs={{0,2},{1,3},{2,0},{3,1},{4,6},{5,7},{6,4},{7,5},{8,10},{9,11},{10,... | collective-permute-start | bytes 786440 | tf_op jit(solution)/shard_map/ppermute | solution.py:46
  129.9 13.5 %collective-permute-start.22 = (bf16[256,512]{1,0:T(8,128)(2,1)S(1)}, bf16[256,512]{1,0:T(8,128)(2,1)S(1)}, u32[]{:S(2)}, u32[]{:S(2)}) collective-permute-start(bf16[256,512]{1,0:T(8,128)(2,1)S(1)} %copy-done.32), channel_id=1, source_target_pairs={{0,2},{1,3},{2,0},{3,1},{4,6},{5,7},{6,4},{7,5},{8,10},{9,11},{10,... | collective-permute-start | bytes 786440 | tf_op jit(solution)/shard_map/ppermute | solution.py:46
  132.3 17.1 %collective-permute-start.26 = (bf16[256,512]{1,0:T(8,128)(2,1)}, bf16[256,512]{1,0:T(8,128)(2,1)S(1)}, u32[]{:S(2)}, u32[]{:S(2)}) collective-permute-start(bf16[256,512]{1,0:T(8,128)(2,1)} %get-tuple-element.113), channel_id=1, source_target_pairs={{0,3},{1,2},{2,1},{3,0},{4,7},{5,6},{6,5},{7,4},{8,11},{9,10},{10,... | collective-permute-start | bytes 786440 | tf_op jit(solution)/shard_map/ppermute | solution.py:46
  133.2 21.4 %collective-permute-start.24 = (bf16[256,512]{1,0:T(8,128)(2,1)S(1)}, bf16[256,512]{1,0:T(8,128)(2,1)S(1)}, u32[]{:S(2)}, u32[]{:S(2)}) collective-permute-start(bf16[256,512]{1,0:T(8,128)(2,1)S(1)} %copy-done.31), channel_id=1, source_target_pairs={{0,3},{1,2},{2,1},{3,0},{4,7},{5,6},{6,5},{7,4},{8,11},{9,10},{10,... | collective-permute-start | bytes 786440 | tf_op jit(solution)/shard_map/ppermute | solution.py:46
  (37 other events, 170.4 us)

commit v4 on v3

--- a/solution.py
+++ b/solution.py
@@ -111,7 +111,7 @@
             at = columns(group ^ r, h)
             rows = []
             for a in range(4):
-                full[a] = held[a, :, at].astype(F32)
+                full[a, :128] = held[a, :, at].astype(F32)
                 rows.append(full[a, pl.ds(o1, 8, stride=16), :])
                 tops[pl.ds(2 * a, 2), :] = full[a, pl.ds(o2, 2, stride=64), :]
             rows.append(tops[...])
@@ -129,7 +129,7 @@
         out_specs=[VMEM] * 4 + [ANY] * 8,
         scratch_shapes=[
             pltpu.VMEM((4, 128, 4096), BF16),
-            pltpu.VMEM((4, 128, 128), F32),
+            pltpu.VMEM((4, 192, 128), F32),
             pltpu.VMEM((8, 128), F32),
             pltpu.SemaphoreType.DMA((16,)),
             pltpu.SemaphoreType.DMA((4,)),
@@ -498,7 +498,7 @@
         ((dk0, dscore, query, 64, 144, SCALE), (dv0, prob, grad, 96, 152, 1.0))
     ):
         rows = jnp.where(twice, 0.0, rows.astype(F32)).astype(BF16)
-        full[...] = start[sub] + dot_tn(weights, rows) * scale
+        full[:512] = start[sub] + dot_tn(weights, rows) * scale
         at_mid = pl.ds(o1, 32, stride=16)
         full[at_mid, :] = full[at_mid, :] + ret[mid_at : mid_at + 32]
         at_top = pl.ds(o2, 8, stride=64)
@@ -524,7 +524,7 @@
         + [pair_block(256, first)] * 4
         + [ANY] * (len(last) + len(held)),
         out_specs=[pair_block(256, first)] * 2 + [pair_block(256, 0)] * 2 + [pair_block(32, first)] * 4,
-        scratch_shapes=[pltpu.VMEM((2, 512, 128), F32)],
+        scratch_shapes=[pltpu.VMEM((2, 576, 128), F32)],
         input_output_aliases={len(before) + i: at for i, at in enumerate(places)},
         compiler_params=params(),
         cost_estimate=COST,
@@ -550,11 +550,11 @@
             rows = oas[r][:, 128 * h : 128 * h + 128].astype(F32)
             for half, out in enumerate((attended, query_grad)):
                 block = source[half * 128 : half * 128 + 128, near : near + 128]
-                full[half] = block.astype(F32)
+                full[half, :128] = block.astype(F32)
                 full[half, pl.ds(o1, 8, stride=16), :] = rows[8 * half : 8 * half + 8]
                 from_row = 16 + 8 * half + 2 * r
                 full[half, pl.ds(o2, 2, stride=64), :] = rows[from_row : from_row + 2]
-                out[:, at] = full[half].astype(BF16)
+                out[:, at] = full[half, :128].astype(BF16)
 
 
 def finish_oq(meta, oqs, oas, last):
@@ -563,7 +563,7 @@
         out_shape=[jax.ShapeDtypeStruct((128, 4096), BF16)] * 2,
         in_specs=[SMEM] + [VMEM] * 10 + [ANY] * len(last),
         out_specs=[VMEM] * 2,
-        scratch_shapes=[pltpu.VMEM((2, 128, 128), F32)],
+        scratch_shapes=[pltpu.VMEM((2, 192, 128), F32)],
         compiler_params=params(),
         cost_estimate=COST,
         name="finish_oq",

time: 160 us -> 160 us (level)
  no operation moved by 1% of the time
where the time goes in v4:
time: 160 us; the launch traced here: 159 us
  starting transfers between devices  59.5 us (37%)
  Pallas kernels  48.1 us (30%)
  waiting for transfers between devices  40.5 us (25%)
  local copies, waits for them, and re-layouts  9.85 us (6%)
    all_to_all x5, starting transfers between devices, unit_exchange(): lax.all_to_all(flat, AXES, 0, 0, tiled=True, axis_index_groups=groups)  29.9 us
    ppermute x27, starting transfers between devices, send(): return lax.ppermute(value, AXES, where)  29.6 us
    ppermute x27, waiting for transfers between devices, send(): return lax.ppermute(value, AXES, where)  26.4 us
    pallas_call x2, Pallas kernels, main(): pl.pallas_call(functools.partial(main_kernel, first), grid=(2,), out_shap...  14.2 us
    all_to_all x5, waiting for transfers between devices, unit_exchange(): lax.all_to_all(flat, AXES, 0, 0, tiled=True, axis_index_groups=groups)  14.1 us
    pallas_call x2, Pallas kernels, late(): pl.pallas_call(functools.partial(late_kernel, first), grid=(2,), out_shap...  8.43 us
    unnamed x74, local copies, waits for them, and re-layouts  8.24 us
    pallas_call x1, Pallas kernels, open_blocks(): pl.pallas_call(open_kernel, out_shape=[jax.ShapeDtypeStruct((40, 1024), B...  5.38 us
  transfers between devices with their start and end apart: 32, of which 15 were waited for; matrix products, arithmetic and copies ran while one was open for 1% of the time, Pallas kernels for 22%

profile of v4, /device:TPU:1, one launch (start us, length us, event | category | flops | bytes accessed | tf_op | source)
XLA Modules:
  0.0 158.9 jit_solution(5552530274093605067)
XLA Ops:
  0.6 3.3 %collective-permute-start = (s32[2,8]{1,0:T(2,128)}, s32[2,8]{1,0:T(2,128)S(1)}, u32[]{:S(2)}, u32[]{:S(2)}) collective-permute-start(s32[2,8]{1,0:T(2,128)} %param.9), channel_id=1, source_target_pairs={{0,1},{1,0},{2,3},{3,2},{4,5},{5,4},{6,7},{7,6},{8,9},{9,8},{10,11... | collective-permute-start | bytes 200 | tf_op jit(solution)/shard_map/ppermute | solution.py:46
  4.0 1.7 %collective-permute-start.2 = (s32[2,8]{1,0:T(2,128)}, s32[2,8]{1,0:T(2,128)S(1)}, u32[]{:S(2)}, u32[]{:S(2)}) collective-permute-start(s32[2,8]{1,0:T(2,128)} %param.9), channel_id=1, source_target_pairs={{0,3},{1,2},{2,1},{3,0},{4,7},{5,6},{6,5},{7,4},{8,11},{9,10},{10,... | collective-permute-start | bytes 200 | tf_op jit(solution)/shard_map/ppermute | solution.py:46
  8.2 5.4 %open.1 = (bf16[40,1024]{1,0:T(8,128)(2,1)}, bf16[40,1024]{1,0:T(8,128)(2,1)}, bf16[40,1024]{1,0:T(8,128)(2,1)}, bf16[40,1024]{1,0:T(8,128)(2,1)}, bf16[256,1024...) custom-call(s32[67]{0:T(128)} %concatenate.3.meta, ...), custom_call_target="tpu_custom_call" | custom-call | bytes 1024 | tf_op jit(solution)/shard_map/open/pallas_call | solution.py:124
  15.9 2.5 %collective-permute-done.4.a2 = bf16[40,1024]{1,0:T(8,128)(2,1)S(1)} collective-permute-done((bf16[40,1024]{1,0:T(8,128)(2,1)}, bf16[40,1024]{1,0:T(8,128)(2,1)S(1)}, u32[]{:S(2)}, u32[]{:S(2)}) %collective-permute-start.4) | collective-permute-done | bytes 81952 | tf_op jit(solution)/shard_map/ppermute | solution.py:46
  18.3 1.9 %collective-permute-done.5.a3 = bf16[40,1024]{1,0:T(8,128)(2,1)S(1)} collective-permute-done((bf16[40,1024]{1,0:T(8,128)(2,1)}, bf16[40,1024]{1,0:T(8,128)(2,1)S(1)}, u32[]{:S(2)}, u32[]{:S(2)}) %collective-permute-start.5) | collective-permute-done | bytes 81952 | tf_op jit(solution)/shard_map/ppermute | solution.py:46
  20.9 1.9 %arrange.1 = (bf16[4,40,1024]{2,1,0:T(8,128)(2,1)}, bf16[8,160,128]{2,1,0:T(8,128)(2,1)}, bf16[256,1024]{1,0:T(8,128)(2,1)}, bf16[256,1024]{1,0:T(8,128)(2,1)}, bf16[256,1024]{1,0:T(8,128)(2,1)}) custom-call(bf16[40,1024]{1,0:T(8,128)(2,1)} %get-tuple-element.61.a0, ...), custom_call_target="tpu_custom_call", output_to_operand_aliasing={{2}: (4, {}), {3}: (5, {}), {4}: (6, {})} | custom-call | bytes 1024 | tf_op jit(solution)/shard_map/arrange/pallas_call | solution.py:163
  22.8 4.9 %all-to-all-start = ((bf16[8,160,128]{2,1,0:T(8,128)(2,1)}), bf16[8,160,128]{2,1,0:T(8,128)(2,1)S(1)}, u32[]{:S(2)}, u32[]{:S(2)}) async-start(bf16[8,160,128]{2,1,0:T(8,128)(2,1)} %get-tuple-element.75), calls=%async_computation | async-start | bytes 655360 | tf_op jit(solution)/shard_map/all_to_all | solution.py:58
  30.3 5.1 %all-to-all-done.got = bf16[8,160,128]{2,1,0:T(8,128)(2,1)S(1)} async-done(((bf16[8,160,128]{2,1,0:T(8,128)(2,1)}), bf16[8,160,128]{2,1,0:T(8,128)(2,1)S(1)}, u32[]{:S(2)}, u32[]{:S(2)}) %all-to-all-start) | async-done | bytes 327712 | tf_op jit(solution)/shard_map/all_to_all | solution.py:58
  36.2 1.9 %fan.1 = (bf16[4,256,128]{2,1,0:T(8,128)(2,1)}, bf16[4,64,128]{2,1,0:T(8,128)(2,1)}, bf16[8,128,128]{2,1,0:T(8,128)(2,1)}) custom-call(bf16[8,160,128]{2,1,0:T(8,128)(2,1)} %copy-done.8), custom_call_target="tpu_custom_call" | custom-call | bytes 1024 | tf_op jit(solution)/shard_map/fan/pallas_call | solution.py:194
  38.1 8.3 %all-to-all-start.1 = ((bf16[8,128,128]{2,1,0:T(8,128)(2,1)}), bf16[8,128,128]{2,1,0:T(8,128)(2,1)S(1)}, u32[]{:S(2)}, u32[]{:S(2)}) async-start(bf16[8,128,128]{2,1,0:T(8,128)(2,1)} %get-tuple-element.78), calls=%async_computation.1 | async-start | bytes 524288 | tf_op jit(solution)/shard_map/all_to_all | solution.py:58
  48.5 1.9 %collective-permute-start.11 = (bf16[256,1024]{1,0:T(8,128)(2,1)}, bf16[256,1024]{1,0:T(8,128)(2,1)S(1)}, u32[]{:S(2)}, u32[]{:S(2)}) collective-permute-start(bf16[256,1024]{1,0:T(8,128)(2,1)} %get-tuple-element.74), channel_id=1, source_target_pairs={{0,3},{1,2},{2,1},{3,0},{4,7},{5,6},{6,5},{7,4},{8,11},{9,10},{10,... | collective-permute-start | bytes 1572872 | tf_op jit(solution)/shard_map/ppermute | solution.py:46
  51.6 2.2 %collective-permute-done.8.refs_3_.refs_7_ = bf16[256,1024]{1,0:T(8,128)(2,1)S(1)} collective-permute-done((bf16[256,1024]{1,0:T(8,128)(2,1)}, bf16[256,1024]{1,0:T(8,128)(2,1)S(1)}, u32[]{:S(2)}, u32[]{:S(2)}) %collective-permute-start.8) | collective-permute-done | bytes 524320 | tf_op jit(solution)/shard_map/ppermute | solution.py:46
  53.8 2.0 %all-to-all-done.1.refs_4_.topz = bf16[8,128,128]{2,1,0:T(8,128)(2,1)S(1)} async-done(((bf16[8,128,128]{2,1,0:T(8,128)(2,1)}), bf16[8,128,128]{2,1,0:T(8,128)(2,1)S(1)}, u32[]{:S(2)}, u32[]{:S(2)}) %all-to-all-start.1) | async-done | bytes 262176 | tf_op jit(solution)/shard_map/all_to_all | solution.py:58
  56.5 3.7 %stats.1 = f32[8,8,128]{2,1,0:T(8,128)} custom-call(bf16[4,40,1024]{2,1,0:T(8,128)(2,1)} %get-tuple-element.79.act.refs_0_, bf16[256,1024]{1,0:T(8,128)(2,1)} %get-tuple-element.60.refs_0_.refs_4_, bf16[256,1024]{1,0:T(8,128)(2,1)} %copy-done, bf16[256,1024]{1,0:T(8,128)(2,1)} %copy-done.1, bf16[256,1024]{1,0:T(8,128)(2,1)} %copy-done.2, ...), custom_call_target="tpu_custom_call" | custom-call | bytes 1024 | tf_op jit(solution)/shard_map/stats/pallas_call | solution.py:241
  60.2 5.7 %all-to-all-start.2 = ((f32[8,8,128]{2,1,0:T(8,128)}), f32[8,8,128]{2,1,0:T(8,128)S(1)}, u32[]{:S(2)}, u32[]{:S(2)}) async-start(f32[8,8,128]{2,1,0:T(8,128)} %stats.1), calls=%async_computation.2 | async-start | bytes 65536 | tf_op jit(solution)/shard_map/all_to_all | solution.py:58
  66.0 6.3 %all-to-all-done.2.st = f32[8,8,128]{2,1,0:T(8,128)S(1)} async-done(((f32[8,8,128]{2,1,0:T(8,128)}), f32[8,8,128]{2,1,0:T(8,128)S(1)}, u32[]{:S(2)}, u32[]{:S(2)}) %all-to-all-start.2) | async-done | bytes 32800 | tf_op jit(solution)/shard_map/all_to_all | solution.py:58
  72.9 3.6 %unit.1 = (bf16[5,256,128]{2,1,0:T(8,128)(2,1)}, bf16[3,64,128]{2,1,0:T(8,128)(2,1)}, bf16[2,256,128]{2,1,0:T(8,128)(2,1)}, bf16[8,128,128]{2,1,0:T(8,128)(2,1)}) custom-call(s32[67]{0:T(128)} %concatenate.3.meta, bf16[4,256,128]{2,1,0:T(8,128)(2,1)} %get-tuple-element.76.mid, bf16[4,64,128]{2,1,0:T(8,128)(2,1)} %get-tuple-element.77.top, ...), custom_call_target="tpu_custom_call" | custom-call | bytes 1024 | tf_op jit(solution)/shard_map/unit/pallas_call | solution.py:352
  76.5 7.3 %all-to-all-start.3 = ((bf16[8,128,128]{2,1,0:T(8,128)(2,1)}), bf16[8,128,128]{2,1,0:T(8,128)(2,1)S(1)}, u32[]{:S(2)}, u32[]{:S(2)}) async-start(bf16[8,128,128]{2,1,0:T(8,128)(2,1)} %get-tuple-element.83.refs_8_), calls=%async_computation.3 | async-start | bytes 524288 | tf_op jit(solution)/shard_map/all_to_all | solution.py:58
  83.8 1.5 collective-permute-start.13
  86.2 7.1 %main.2 = (bf16[256,1024]{1,0:T(8,128)(2,1)}, bf16[256,1024]{1,0:T(8,128)(2,1)}, bf16[256,512]{1,0:T(8,128)(2,1)}, bf16[256,512]{1,0:T(8,128)(2,1)}, f32[4,512,128]{2,1,0:T(8,128)}, /*index=5*/f32[4,512,128]{2,1,0:T(8,128)}) custom-call(s32[67]{0:T(128)} %concatenate.3.meta, bf16[256,1024]{1,0:T(8,128)(2,1)} %get-tuple-element.60.refs_0_.refs_4_, ...), custom_call_target="tpu_custom_call" | custom-call | bytes 1024 | tf_op jit(solution)/shard_map/main/pallas_call | solution.py:448
  94.7 1.9 %combine.1.refs_8_ = bf16[8,200,128]{2,1,0:T(8,128)(2,1)} custom-call(bf16[5,256,128]{2,1,0:T(8,128)(2,1)} %get-tuple-element.80.out_mid, bf16[3,64,128]{2,1,0:T(8,128)(2,1)} %get-tuple-element.81.out_top, bf16[2,256,128]{2,1,0:T(8,128)(2,1)} %copy-done.23, bf16[8,128,128]{2,1,0:T(8,128)(2,1)} %copy-done.9, f32[4,512,128]{2,1,0:T(8,128)} %get-tuple-element.84.refs_0_.refs_2_), custom_call_target="tpu_custom_call" | custom-call | bytes 1024 | tf_op jit(solution)/shard_map/combine/pallas_call | solution.py:384
  96.7 3.6 %all-to-all-start.4 = ((bf16[8,200,128]{2,1,0:T(8,128)(2,1)}), bf16[8,200,128]{2,1,0:T(8,128)(2,1)S(1)}, u32[]{:S(2)}, u32[]{:S(2)}) async-start(bf16[8,200,128]{2,1,0:T(8,128)(2,1)} %combine.1.refs_8_), calls=%async_computation.4 | async-start | bytes 819200 | tf_op jit(solution)/shard_map/all_to_all | solution.py:58
  100.4 5.1 %collective-permute-start.16 = (bf16[256,512]{1,0:T(8,128)(2,1)S(1)}, bf16[256,512]{1,0:T(8,128)(2,1)S(1)}, u32[]{:S(2)}, u32[]{:S(2)}) collective-permute-start(bf16[256,512]{1,0:T(8,128)(2,1)S(1)} %copy-done.33), channel_id=1, source_target_pairs={{0,3},{1,2},{2,1},{3,0},{4,7},{5,6},{6,5},{7,4},{8,11},{9,10},{10,... | collective-permute-start | bytes 786440 | tf_op jit(solution)/shard_map/ppermute | solution.py:46
  105.5 7.1 %main.3 = (bf16[256,1024]{1,0:T(8,128)(2,1)}, bf16[256,1024]{1,0:T(8,128)(2,1)}, bf16[256,512]{1,0:T(8,128)(2,1)}, bf16[256,512]{1,0:T(8,128)(2,1)}, f32[4,512,128]{2,1,0:T(8,128)}, /*index=5*/f32[4,512,128]{2,1,0:T(8,128)}) custom-call(s32[67]{0:T(128)} %concatenate.3.meta, ...), custom_call_target="tpu_custom_call", output_to_operand_aliasing={{0}: (10, {}), {1}: (11, {})} | custom-call | bytes 1024 | tf_op jit(solution)/shard_map/main/pallas_call | solution.py:448
  113.1 1.5 collective-permute-start.18
  115.6 4.2 %late.2 = (bf16[256,1024]{1,0:T(8,128)(2,1)}, bf16[256,1024]{1,0:T(8,128)(2,1)}, bf16[256,512]{1,0:T(8,128)(2,1)}, bf16[256,512]{1,0:T(8,128)(2,1)}, bf16[32,102...) custom-call(s32[67]{0:T(128)} %concatenate.3.meta, ...), custom_call_target="tpu_custom_call" | custom-call | bytes 1024 | tf_op jit(solution)/shard_map/late/pallas_call | solution.py:513
  121.7 4.2 %late.3 = (bf16[256,1024]{1,0:T(8,128)(2,1)}, bf16[256,1024]{1,0:T(8,128)(2,1)}, bf16[256,512]{1,0:T(8,128)(2,1)}, bf16[256,512]{1,0:T(8,128)(2,1)}, bf16[32,102...) custom-call(s32[67]{0:T(128)} %concatenate.3.meta, ...), custom_call_target="tpu_custom_call", output_to_operand_aliasing={{0}: (10, {}), {1}: (11, {}), {4}: (12, {}), {5}: (13, {}),... | custom-call | bytes 1024 | tf_op jit(solution)/shard_map/late/pallas_call | solution.py:513
  134.1 9.2 %collective-permute-done.22.refs_10_.refs_2_ = bf16[256,512]{1,0:T(8,128)(2,1)S(1)} collective-permute-done((bf16[256,512]{1,0:T(8,128)(2,1)S(1)}, bf16[256,512]{1,0:T(8,128)(2,1)S(1)}, u32[]{:S(2)}, u32[]{:S(2)}) %collective-permute-start.22) | collective-permute-done | bytes 262176 | tf_op jit(solution)/shard_map/ppermute | solution.py:46
  144.0 3.8 %finish_oq.1 = (bf16[128,4096]{1,0:T(8,128)(2,1)}, bf16[128,4096]{1,0:T(8,128)(2,1)}) custom-call(s32[67]{0:T(128)} %concatenate.3.meta, bf16[256,1024]{1,0:T(8,128)(2,1)} %get-tuple-element.87.refs_0_, bf16[256,1024]{1,0:T(8,128)(2,1)} %copy-done.16, bf16[256,512]{1,0:T(8,128)(2,1)} %copy-done.10, bf16[256,512]{1,0:T(8,128)(2,1)} %copy-done.11, ...), custom_call_target="tpu_custom_call" | custom-call | bytes 1024 | tf_op jit(solution)/shard_map/finish_oq/pallas_call | solution.py:561
  147.8 1.6 %collective-permute-done.26.refs_5_ = bf16[256,512]{1,0:T(8,128)(2,1)S(1)} collective-permute-done((bf16[256,512]{1,0:T(8,128)(2,1)}, bf16[256,512]{1,0:T(8,128)(2,1)S(1)}, u32[]{:S(2)}, u32[]{:S(2)}) %collective-permute-start.26) | collective-permute-done | bytes 262176 | tf_op jit(solution)/shard_map/ppermute | solution.py:46
  149.4 5.1 %collective-permute-done.24.refs_3_ = bf16[256,512]{1,0:T(8,128)(2,1)S(1)} collective-permute-done((bf16[256,512]{1,0:T(8,128)(2,1)S(1)}, bf16[256,512]{1,0:T(8,128)(2,1)S(1)}, u32[]{:S(2)}, u32[]{:S(2)}) %collective-permute-start.24) | collective-permute-done | bytes 262176 | tf_op jit(solution)/shard_map/ppermute | solution.py:46
  155.5 3.3 %finish_kv.1 = (bf16[128,4096]{1,0:T(8,128)(2,1)}, bf16[128,4096]{1,0:T(8,128)(2,1)}) custom-call(s32[67]{0:T(128)} %concatenate.3.meta, bf16[256,1024]{1,0:T(8,128)(2,1)} %get-tuple-element.109.refs_0_, bf16[256,1024]{1,0:T(8,128)(2,1)} %copy-done.15, bf16[256,512]{1,0:T(8,128)(2,1)} %copy-done.13, bf16[256,512]{1,0:T(8,128)(2,1)} %copy-done.20, ...), custom_call_target="tpu_custom_call" | custom-call | bytes 1024 | tf_op jit(solution)/shard_map/finish_kv/pallas_call | solution.py:599
  (124 shorter events, 28.9 us)
Async XLA Ops:
  0.6 5.9 %collective-permute-start = (s32[2,8]{1,0:T(2,128)}, s32[2,8]{1,0:T(2,128)S(1)}, u32[]{:S(2)}, u32[]{:S(2)}) collective-permute-start(s32[2,8]{1,0:T(2,128)} %param.9), channel_id=1, source_target_pairs={{0,1},{1,0},{2,3},{3,2},{4,5},{5,4},{6,7},{7,6},{8,9},{9,8},{10,11... | collective-permute-start | bytes 200 | tf_op jit(solution)/shard_map/ppermute | solution.py:46
  4.0 2.6 %collective-permute-start.1 = (s32[2,8]{1,0:T(2,128)}, s32[2,8]{1,0:T(2,128)S(1)}, u32[]{:S(2)}, u32[]{:S(2)}) collective-permute-start(s32[2,8]{1,0:T(2,128)} %param.9), channel_id=1, source_target_pairs={{0,2},{1,3},{2,0},{3,1},{4,6},{5,7},{6,4},{7,5},{8,10},{9,11},{10,... | collective-permute-start | bytes 200 | tf_op jit(solution)/shard_map/ppermute | solution.py:46
  4.0 3.5 %collective-permute-start.2 = (s32[2,8]{1,0:T(2,128)}, s32[2,8]{1,0:T(2,128)S(1)}, u32[]{:S(2)}, u32[]{:S(2)}) collective-permute-start(s32[2,8]{1,0:T(2,128)} %param.9), channel_id=1, source_target_pairs={{0,3},{1,2},{2,1},{3,0},{4,7},{5,6},{6,5},{7,4},{8,11},{9,10},{10,... | collective-permute-start | bytes 200 | tf_op jit(solution)/shard_map/ppermute | solution.py:46
  13.5 2.3 %collective-permute-start.3 = (bf16[40,1024]{1,0:T(8,128)(2,1)}, bf16[40,1024]{1,0:T(8,128)(2,1)S(1)}, u32[]{:S(2)}, u32[]{:S(2)}) collective-permute-start(bf16[40,1024]{1,0:T(8,128)(2,1)} %get-tuple-element.62), channel_id=1, source_target_pairs={{0,1},{1,0},{2,3},{3,2},{4,5},{5,4},{6,7},{7,6},{8,9},{9,8},{10,11... | collective-permute-start | bytes 245768 | tf_op jit(solution)/shard_map/ppermute | solution.py:46
  14.1 4.2 %collective-permute-start.4 = (bf16[40,1024]{1,0:T(8,128)(2,1)}, bf16[40,1024]{1,0:T(8,128)(2,1)S(1)}, u32[]{:S(2)}, u32[]{:S(2)}) collective-permute-start(bf16[40,1024]{1,0:T(8,128)(2,1)} %get-tuple-element.63), channel_id=1, source_target_pairs={{0,2},{1,3},{2,0},{3,1},{4,6},{5,7},{6,4},{7,5},{8,10},{9,11},{10,... | collective-permute-start | bytes 245768 | tf_op jit(solution)/shard_map/ppermute | solution.py:46
  15.2 5.1 %collective-permute-start.5 = (bf16[40,1024]{1,0:T(8,128)(2,1)}, bf16[40,1024]{1,0:T(8,128)(2,1)S(1)}, u32[]{:S(2)}, u32[]{:S(2)}) collective-permute-start(bf16[40,1024]{1,0:T(8,128)(2,1)} %get-tuple-element.64), channel_id=1, source_target_pairs={{0,3},{1,2},{2,1},{3,0},{4,7},{5,6},{6,5},{7,4},{8,11},{9,10},{10,... | collective-permute-start | bytes 245768 | tf_op jit(solution)/shard_map/ppermute | solution.py:46
  22.8 12.6 %all-to-all-start = ((bf16[8,160,128]{2,1,0:T(8,128)(2,1)}), bf16[8,160,128]{2,1,0:T(8,128)(2,1)S(1)}, u32[]{:S(2)}, u32[]{:S(2)}) async-start(bf16[8,160,128]{2,1,0:T(8,128)(2,1)} %get-tuple-element.75), calls=%async_computation | async-start | bytes 655360 | tf_op jit(solution)/shard_map/all_to_all | solution.py:58
  27.7 20.8 %collective-permute-start.6 = (bf16[256,1024]{1,0:T(8,128)(2,1)S(1)}, bf16[256,1024]{1,0:T(8,128)(2,1)S(1)}, u32[]{:S(2)}, u32[]{:S(2)}) collective-permute-start(bf16[256,1024]{1,0:T(8,128)(2,1)S(1)} %copy-done.17), channel_id=1, source_target_pairs={{0,1},{1,0},{2,3},{3,2},{4,5},{5,4},{6,7},{7,6},{8,9},{9,8},{10,11... | collective-permute-start | bytes 1572872 | tf_op jit(solution)/shard_map/ppermute | solution.py:46
  28.3 22.2 %collective-permute-start.7 = (bf16[256,1024]{1,0:T(8,128)(2,1)}, bf16[256,1024]{1,0:T(8,128)(2,1)S(1)}, u32[]{:S(2)}, u32[]{:S(2)}) collective-permute-start(bf16[256,1024]{1,0:T(8,128)(2,1)} %get-tuple-element.69), channel_id=1, source_target_pairs={{0,2},{1,3},{2,0},{3,1},{4,6},{5,7},{6,4},{7,5},{8,10},{9,11},{10,... | collective-permute-start | bytes 1572872 | tf_op jit(solution)/shard_map/ppermute | solution.py:46
  28.5 25.3 %collective-permute-start.8 = (bf16[256,1024]{1,0:T(8,128)(2,1)}, bf16[256,1024]{1,0:T(8,128)(2,1)S(1)}, u32[]{:S(2)}, u32[]{:S(2)}) collective-permute-start(bf16[256,1024]{1,0:T(8,128)(2,1)} %get-tuple-element.70), channel_id=1, source_target_pairs={{0,3},{1,2},{2,1},{3,0},{4,7},{5,6},{6,5},{7,4},{8,11},{9,10},{10,... | collective-permute-start | bytes 1572872 | tf_op jit(solution)/shard_map/ppermute | solution.py:46
  30.0 36.0 %collective-permute-start.10 = (bf16[256,1024]{1,0:T(8,128)(2,1)}, bf16[256,1024]{1,0:T(8,128)(2,1)S(1)}, u32[]{:S(2)}, u32[]{:S(2)}) collective-permute-start(bf16[256,1024]{1,0:T(8,128)(2,1)} %get-tuple-element.73), channel_id=1, source_target_pairs={{0,2},{1,3},{2,0},{3,1},{4,6},{5,7},{6,4},{7,5},{8,10},{9,11},{10,... | collective-permute-start | bytes 1572872 | tf_op jit(solution)/shard_map/ppermute | solution.py:46
  38.1 17.8 %all-to-all-start.1 = ((bf16[8,128,128]{2,1,0:T(8,128)(2,1)}), bf16[8,128,128]{2,1,0:T(8,128)(2,1)S(1)}, u32[]{:S(2)}, u32[]{:S(2)}) async-start(bf16[8,128,128]{2,1,0:T(8,128)(2,1)} %get-tuple-element.78), calls=%async_computation.1 | async-start | bytes 524288 | tf_op jit(solution)/shard_map/all_to_all | solution.py:58
  47.1 18.9 %collective-permute-start.12 = (bf16[2,256,128]{2,1,0:T(8,128)(2,1)}, bf16[2,256,128]{2,1,0:T(8,128)(2,1)S(1)}, u32[]{:S(2)}, u32[]{:S(2)}) collective-permute-start(bf16[2,256,128]{2,1,0:T(8,128)(2,1)} %slice.3), channel_id=1, source_target_pairs={{0,32},{1,33},{2,34},{3,35},{4,36},{5,37},{6,38},{7,39},{8,40},{9,... | collective-permute-start | bytes 393224 | tf_op jit(solution)/shard_map/ppermute | solution.py:46
  48.5 36.7 %collective-permute-start.11 = (bf16[256,1024]{1,0:T(8,128)(2,1)}, bf16[256,1024]{1,0:T(8,128)(2,1)S(1)}, u32[]{:S(2)}, u32[]{:S(2)}) collective-permute-start(bf16[256,1024]{1,0:T(8,128)(2,1)} %get-tuple-element.74), channel_id=1, source_target_pairs={{0,3},{1,2},{2,1},{3,0},{4,7},{5,6},{6,5},{7,4},{8,11},{9,10},{10,... | collective-permute-start | bytes 1572872 | tf_op jit(solution)/shard_map/ppermute | solution.py:46
  50.5 34.8 %collective-permute-start.9 = (bf16[256,1024]{1,0:T(8,128)(2,1)}, bf16[256,1024]{1,0:T(8,128)(2,1)S(1)}, u32[]{:S(2)}, u32[]{:S(2)}) collective-permute-start(bf16[256,1024]{1,0:T(8,128)(2,1)} %get-tuple-element.72), channel_id=1, source_target_pairs={{0,1},{1,0},{2,3},{3,2},{4,5},{5,4},{6,7},{7,6},{8,9},{9,8},{10,11... | collective-permute-start | bytes 1572872 | tf_op jit(solution)/shard_map/ppermute | solution.py:46
  60.2 12.1 %all-to-all-start.2 = ((f32[8,8,128]{2,1,0:T(8,128)}), f32[8,8,128]{2,1,0:T(8,128)S(1)}, u32[]{:S(2)}, u32[]{:S(2)}) async-start(f32[8,8,128]{2,1,0:T(8,128)} %stats.1), calls=%async_computation.2 | async-start | bytes 65536 | tf_op jit(solution)/shard_map/all_to_all | solution.py:58
  76.5 17.5 %all-to-all-start.3 = ((bf16[8,128,128]{2,1,0:T(8,128)(2,1)}), bf16[8,128,128]{2,1,0:T(8,128)(2,1)S(1)}, u32[]{:S(2)}, u32[]{:S(2)}) async-start(bf16[8,128,128]{2,1,0:T(8,128)(2,1)} %get-tuple-element.83.refs_8_), calls=%async_computation.3 | async-start | bytes 524288 | tf_op jit(solution)/shard_map/all_to_all | solution.py:58
  83.8 9.5 %collective-permute-start.13 = (bf16[2,256,128]{2,1,0:T(8,128)(2,1)S(1)}, bf16[2,256,128]{2,1,0:T(8,128)(2,1)S(1)}, u32[]{:S(2)}, u32[]{:S(2)}) collective-permute-start(bf16[2,256,128]{2,1,0:T(8,128)(2,1)S(1)} %copy-done.35), channel_id=1, source_target_pairs={{0,32},{1,33},{2,34},{3,35},{4,36},{5,37},{6,38},{7,39},{8,40},{9,... | collective-permute-start | bytes 393224 | tf_op jit(solution)/shard_map/ppermute | solution.py:46
  96.7 18.0 %all-to-all-start.4 = ((bf16[8,200,128]{2,1,0:T(8,128)(2,1)}), bf16[8,200,128]{2,1,0:T(8,128)(2,1)S(1)}, u32[]{:S(2)}, u32[]{:S(2)}) async-start(bf16[8,200,128]{2,1,0:T(8,128)(2,1)} %combine.1.refs_8_), calls=%async_computation.4 | async-start | bytes 819200 | tf_op jit(solution)/shard_map/all_to_all | solution.py:58
  100.3 14.3 %collective-permute-start.15 = (bf16[256,512]{1,0:T(8,128)(2,1)S(1)}, bf16[256,512]{1,0:T(8,128)(2,1)S(1)}, u32[]{:S(2)}, u32[]{:S(2)}) collective-permute-start(bf16[256,512]{1,0:T(8,128)(2,1)S(1)} %copy-done.34), channel_id=1, source_target_pairs={{0,2},{1,3},{2,0},{3,1},{4,6},{5,7},{6,4},{7,5},{8,10},{9,11},{10,... | collective-permute-start | bytes 786440 | tf_op jit(solution)/shard_map/ppermute | solution.py:46
  100.4 14.3 %collective-permute-start.16 = (bf16[256,512]{1,0:T(8,128)(2,1)S(1)}, bf16[256,512]{1,0:T(8,128)(2,1)S(1)}, u32[]{:S(2)}, u32[]{:S(2)}) collective-permute-start(bf16[256,512]{1,0:T(8,128)(2,1)S(1)} %copy-done.33), channel_id=1, source_target_pairs={{0,3},{1,2},{2,1},{3,0},{4,7},{5,6},{6,5},{7,4},{8,11},{9,10},{10,... | collective-permute-start | bytes 786440 | tf_op jit(solution)/shard_map/ppermute | solution.py:46
  112.6 8.4 %collective-permute-start.17 = (bf16[256,512]{1,0:T(8,128)(2,1)}, bf16[256,512]{1,0:T(8,128)(2,1)S(1)}, u32[]{:S(2)}, u32[]{:S(2)}) collective-permute-start(bf16[256,512]{1,0:T(8,128)(2,1)} %get-tuple-element.91), channel_id=1, source_target_pairs={{0,2},{1,3},{2,0},{3,1},{4,6},{5,7},{6,4},{7,5},{8,10},{9,11},{10,... | collective-permute-start | bytes 786440 | tf_op jit(solution)/shard_map/ppermute | solution.py:46
  112.7 20.5 %collective-permute-start.14 = (bf16[256,1024]{1,0:T(8,128)(2,1)}, bf16[256,1024]{1,0:T(8,128)(2,1)S(1)}, u32[]{:S(2)}, u32[]{:S(2)}) collective-permute-start(bf16[256,1024]{1,0:T(8,128)(2,1)} %get-tuple-element.88), channel_id=1, source_target_pairs={{0,1},{1,0},{2,3},{3,2},{4,5},{5,4},{6,7},{7,6},{8,9},{9,8},{10,11... | collective-permute-start | bytes 1572872 | tf_op jit(solution)/shard_map/ppermute | solution.py:46
  113.1 14.4 %collective-permute-start.18 = (bf16[256,512]{1,0:T(8,128)(2,1)}, bf16[256,512]{1,0:T(8,128)(2,1)S(1)}, u32[]{:S(2)}, u32[]{:S(2)}) collective-permute-start(bf16[256,512]{1,0:T(8,128)(2,1)} %get-tuple-element.92), channel_id=1, source_target_pairs={{0,3},{1,2},{2,1},{3,0},{4,7},{5,6},{6,5},{7,4},{8,11},{9,10},{10,... | collective-permute-start | bytes 786440 | tf_op jit(solution)/shard_map/ppermute | solution.py:46
  125.9 28.6 %collective-permute-start.23 = (bf16[256,1024]{1,0:T(8,128)(2,1)}, bf16[256,1024]{1,0:T(8,128)(2,1)S(1)}, u32[]{:S(2)}, u32[]{:S(2)}) collective-permute-start(bf16[256,1024]{1,0:T(8,128)(2,1)} %get-tuple-element.110), channel_id=1, source_target_pairs={{0,1},{1,0},{2,3},{3,2},{4,5},{5,4},{6,7},{7,6},{8,9},{9,8},{10,11... | collective-permute-start | bytes 1572872 | tf_op jit(solution)/shard_map/ppermute | solution.py:46
  126.0 2.5 %collective-permute-start.19 = (bf16[32,1024]{1,0:T(8,128)(2,1)}, bf16[32,1024]{1,0:T(8,128)(2,1)S(1)}, u32[]{:S(2)}, u32[]{:S(2)}) collective-permute-start(bf16[32,1024]{1,0:T(8,128)(2,1)} %get-tuple-element.103), channel_id=1, source_target_pairs={{0,1},{1,0},{2,3},{3,2},{4,5},{5,4},{6,7},{7,6},{8,9},{9,8},{10,11... | collective-permute-start | bytes 196616 | tf_op jit(solution)/shard_map/ppermute | solution.py:46
  126.5 3.3 %collective-permute-start.20 = (bf16[32,1024]{1,0:T(8,128)(2,1)}, bf16[32,1024]{1,0:T(8,128)(2,1)S(1)}, u32[]{:S(2)}, u32[]{:S(2)}) collective-permute-start(bf16[32,1024]{1,0:T(8,128)(2,1)} %get-tuple-element.104), channel_id=1, source_target_pairs={{0,2},{1,3},{2,0},{3,1},{4,6},{5,7},{6,4},{7,5},{8,10},{9,11},{10,... | collective-permute-start | bytes 196616 | tf_op jit(solution)/shard_map/ppermute | solution.py:46
  127.5 4.8 %collective-permute-start.21 = (bf16[32,1024]{1,0:T(8,128)(2,1)}, bf16[32,1024]{1,0:T(8,128)(2,1)S(1)}, u32[]{:S(2)}, u32[]{:S(2)}) collective-permute-start(bf16[32,1024]{1,0:T(8,128)(2,1)} %get-tuple-element.105), channel_id=1, source_target_pairs={{0,3},{1,2},{2,1},{3,0},{4,7},{5,6},{6,5},{7,4},{8,11},{9,10},{10,... | collective-permute-start | bytes 196616 | tf_op jit(solution)/shard_map/ppermute | solution.py:46
  128.5 19.3 %collective-permute-start.25 = (bf16[256,512]{1,0:T(8,128)(2,1)}, bf16[256,512]{1,0:T(8,128)(2,1)S(1)}, u32[]{:S(2)}, u32[]{:S(2)}) collective-permute-start(bf16[256,512]{1,0:T(8,128)(2,1)} %get-tuple-element.112), channel_id=1, source_target_pairs={{0,2},{1,3},{2,0},{3,1},{4,6},{5,7},{6,4},{7,5},{8,10},{9,11},{10,... | collective-permute-start | bytes 786440 | tf_op jit(solution)/shard_map/ppermute | solution.py:46
  129.9 13.5 %collective-permute-start.22 = (bf16[256,512]{1,0:T(8,128)(2,1)S(1)}, bf16[256,512]{1,0:T(8,128)(2,1)S(1)}, u32[]{:S(2)}, u32[]{:S(2)}) collective-permute-start(bf16[256,512]{1,0:T(8,128)(2,1)S(1)} %copy-done.32), channel_id=1, source_target_pairs={{0,2},{1,3},{2,0},{3,1},{4,6},{5,7},{6,4},{7,5},{8,10},{9,11},{10,... | collective-permute-start | bytes 786440 | tf_op jit(solution)/shard_map/ppermute | solution.py:46
  132.3 17.1 %collective-permute-start.26 = (bf16[256,512]{1,0:T(8,128)(2,1)}, bf16[256,512]{1,0:T(8,128)(2,1)S(1)}, u32[]{:S(2)}, u32[]{:S(2)}) collective-permute-start(bf16[256,512]{1,0:T(8,128)(2,1)} %get-tuple-element.113), channel_id=1, source_target_pairs={{0,3},{1,2},{2,1},{3,0},{4,7},{5,6},{6,5},{7,4},{8,11},{9,10},{10,... | collective-permute-start | bytes 786440 | tf_op jit(solution)/shard_map/ppermute | solution.py:46
  133.2 21.4 %collective-permute-start.24 = (bf16[256,512]{1,0:T(8,128)(2,1)S(1)}, bf16[256,512]{1,0:T(8,128)(2,1)S(1)}, u32[]{:S(2)}, u32[]{:S(2)}) collective-permute-start(bf16[256,512]{1,0:T(8,128)(2,1)S(1)} %copy-done.31), channel_id=1, source_target_pairs={{0,3},{1,2},{2,1},{3,0},{4,7},{5,6},{6,5},{7,4},{8,11},{9,10},{10,... | collective-permute-start | bytes 786440 | tf_op jit(solution)/shard_map/ppermute | solution.py:46
  (37 other events, 170.4 us)
